TPU v7x, 32 devices: a whole 2x2x4 slice. The times are simulated.
32 devices in a mesh: dp: 4 (over z), expert: 8 (over y, x, core).
Axes of the slice: x: 2, y: 2, z: 4, core: 2. Of those that a mesh axis runs over, the one named last changes fastest.
Arguments:
- tokens: bfloat16 [8192, 1280], P(('dp', 'expert')), may hold values from -6 to 6
- expert_ids: int32 [8192, 2], P(('dp', 'expert')), may hold values from 0 to 15, all different within a row; in each aligned block of 256 rows (0 to 255, 256 to 511, ...) at most 48 rows name the same one
- gate_weights: float32 [8192, 2], P(('dp', 'expert')), may hold values from 0.1 to 1
- target: int32 [8192], P(('dp', 'expert')), may hold values from 0 to 8191, as said below
- expert_gate: bfloat16 [16, 1280, 1024], P('expert'), may hold values from -0.15625 to 0.15625
- expert_up: bfloat16 [16, 1280, 1024], P('expert'), may hold values from -0.15625 to 0.15625
- expert_down: bfloat16 [16, 1024, 1280], P('expert'), may hold values from -0.1875 to 0.1875
- dec_embed: bfloat16 [1280, 512], replicated, may hold values from -0.15625 to 0.15625
- mask_token: bfloat16 [512], replicated, may hold values from -5 to 5
- norm_gain: float32 [512], replicated, may hold values from 0.1 to 1.9
- w_qkv: bfloat16 [512, 1536], replicated, may hold values from -0.25 to 0.25
- w_out: bfloat16 [512, 512], replicated, may hold values from -0.25 to 0.25
- w_head: bfloat16 [512, 768], replicated, may hold values from -0.25 to 0.25
- pixels: bfloat16 [32, 1024, 768], P('dp', 'expert'), may hold values from -60 to 60
Outputs:
- decoded: bfloat16 [32, 1024, 512], P('dp', 'expert')
- d_attn: bfloat16 [32, 1024, 512], P('dp', 'expert')
- tile_loss: float32 [4, 8], P('dp', 'expert')
Inputs may be any that keep to these rules, and one draw needn't show every extreme that they name: `expert_ids`: each row names 2 different experts. Among the 256 rows of one device no expert is named more than 48 times, a bound that some block reaches; every expert is named somewhere. target = j * 1024 + q names tile j of the token's dp group and patch q of that tile. No two tokens of one dp group share a value. The 256 tokens of one device name any one tile at most 128 times, and some tile exactly 128 times.
All inputs are finite; a program needn't handle non-finite values.
Results may differ from a plain program's by a relative error of at most 0.012.
Values may be sent and summed in bfloat16 or wider, within the bound.
No kernel may reach another device: no remote copies, remote signals or barrier semaphores. Data moves between devices by JAX's collectives and lax.ppermute only.
A program may use at most 384 MiB of HBM per device.

v0:
```python
import functools
import math

import jax
import jax.numpy as jnp
from jax import lax
from jax.experimental import pallas as pl
from jax.experimental.pallas import tpu as pltpu
from jax.sharding import PartitionSpec as P

TOPK = 2
HD = 32
PD = 768
RAD = 3


EPSILON = 1e-06


def positional(row_ids, col_ids, total_width):
    quarter = total_width // 4
    frequency = jnp.exp(jnp.arange(quarter, dtype=jnp.float32) * (-math.log(10000.0) / quarter))
    row_angle = row_ids.astype(jnp.float32)[:, None] * frequency[None, :]
    col_angle = col_ids.astype(jnp.float32)[:, None] * frequency[None, :]
    return (
        jnp.concatenate([jnp.sin(row_angle), jnp.cos(row_angle)], 1),
        jnp.concatenate([jnp.sin(col_angle), jnp.cos(col_angle)], 1),
    )


def dot(a, b, dims=((1,), (0,))):
    return lax.dot_general(a, b, (dims, ((), ())), preferred_element_type=jnp.float32)


def iota(shape, axis):
    return lax.broadcasted_iota(jnp.int32, shape, axis)


def ones_where(mask):
    return jnp.where(mask, 1.0, 0.0).astype(jnp.bfloat16)


def route_of(width, local_experts, total, axis, shape):
    slot = iota(shape, axis)
    block = slot // (local_experts * width)
    return (block ^ lax.axis_index("expert")) * local_experts + slot // width % local_experts


def slot_matrix(member, width, route):
    buckets, items = member.shape
    total = route.shape[0]
    earlier = ones_where(iota((items, items), 0) < iota((items, items), 1))
    rank = dot(ones_where(member), earlier)
    code = jnp.where(member, rank, -1.0).astype(jnp.bfloat16)
    expand = ones_where(route == iota((total, buckets), 1))
    place = (iota((total, items), 0) % width).astype(jnp.float32)
    return ones_where(dot(expand, code) == place)


def pack_kernel(width, experts, local_experts, ids_ref, tokens_ref, *out_refs):
    items = tokens_ref.shape[0]
    total = experts * width
    member = iota((experts, items), 0) == ids_ref[0:1, :]
    for k in range(1, ids_ref.shape[0]):
        member = member | (iota((experts, items), 0) == ids_ref[k : k + 1, :])
    route = route_of(width, local_experts, total, 0, (total, experts))
    rows = dot(slot_matrix(member, width, route), tokens_ref[...]).astype(jnp.bfloat16)
    share = local_experts * width
    for k, out_ref in enumerate(out_refs):
        out_ref[...] = rows[k * share : (k + 1) * share].reshape(out_ref.shape)


def prep_kernel(
    width, experts, local_experts, relay_cap, tile_size, ids_ref, gates_ref, target_ref, tokens_ref, embed_ref,
    high_ref, low_ref, base_ref, relay_ref, spot_ref,
):
    items = tokens_ref.shape[0]
    slots = high_ref.shape[1]
    lines = iota((experts, items), 0)
    member = jnp.zeros((experts, items), jnp.float32)
    gates = jnp.zeros((experts, items), jnp.float32)
    for k in range(ids_ref.shape[0]):
        hit = ids_ref[k : k + 1, :] == lines
        member = jnp.where(hit, 1.0, member)
        gates = jnp.where(hit, gates_ref[k : k + 1, :], gates)
    earlier = ones_where(iota((items, items), 0) < iota((items, items), 1))
    rank = dot(member.astype(jnp.bfloat16), earlier)
    code = jnp.where(member > 0.5, rank, -1.0).astype(jnp.bfloat16)
    route = route_of(width, local_experts, slots, 1, (experts, slots))
    expand = ones_where(route == iota((experts, slots), 0))
    place = (iota((items, slots), 1) % width).astype(jnp.float32)
    across = ((0,), (0,))
    taken = dot(code, expand, across) == place
    high = gates.astype(jnp.bfloat16)
    low = (gates - high.astype(jnp.float32)).astype(jnp.bfloat16)
    high_ref[...] = jnp.where(taken, dot(high, expand, across), 0.0).astype(jnp.bfloat16)
    low_ref[...] = jnp.where(taken, dot(low, expand, across), 0.0).astype(jnp.bfloat16)
    base_ref[...] = dot(tokens_ref[...], embed_ref[...])
    target = target_ref[...]
    relay_slots = relay_ref.shape[0]
    groups = relay_slots // relay_cap
    me = lax.axis_index("expert")
    route = iota((relay_slots, groups), 0) // relay_cap ^ me
    relay = slot_matrix(iota((groups, items), 0) == target // tile_size, relay_cap, route)
    relay_ref[...] = relay
    spot = target % tile_size
    line = iota((8, items), 0)
    digits = jnp.where(line == 0, spot // 256, jnp.where(line == 1, spot % 256, 1)).astype(jnp.float32)
    found = dot(digits.astype(jnp.bfloat16), relay, ((1,), (1,)))
    spots = jnp.where(found[2:3] > 0.5, found[0:1] * 256.0 + found[1:2], -1.0).astype(jnp.int32)
    for k in range(groups):
        spot_ref[pl.ds(me ^ k, 1), :] = spots[:, k * relay_cap : (k + 1) * relay_cap]


def fold_kernel(down_ref, embed_ref, folded_ref):
    folded_ref[0] = dot(down_ref[0], embed_ref[...]).astype(jnp.bfloat16)


def fold(down, embed):
    local_experts, hidden, model_width = down.shape
    out_width = embed.shape[1]
    chunk = hidden // 2
    return pl.pallas_call(
        fold_kernel,
        grid=(local_experts, hidden // chunk),
        out_shape=shaped((local_experts, hidden, out_width), jnp.bfloat16),
        in_specs=[
            pl.BlockSpec((1, chunk, model_width), lambda e, f: (e, f, 0)),
            pl.BlockSpec((model_width, out_width), lambda e, f: (0, 0)),
        ],
        out_specs=pl.BlockSpec((1, chunk, out_width), lambda e, f: (e, f, 0)),
        compiler_params=pltpu.CompilerParams(vmem_limit_bytes=WIDE_ROOM),
        cost_estimate=pl.CostEstimate(
            flops=2 * local_experts * hidden * model_width * out_width,
            bytes_accessed=2 * math.prod(down.shape),
            transcendentals=0,
        ),
        name="fold",
    )(down, embed)


def ffn_kernel(sources, *refs):
    row_refs, (gate_ref, up_ref, down_ref) = refs[:sources], refs[sources : sources + 3]
    out_refs = refs[sources + 3 :]
    width = row_refs[0].shape[1]
    rows = jnp.concatenate([ref[0] for ref in row_refs], 0)
    gate = dot(rows, gate_ref[0])
    up = dot(rows, up_ref[0])
    hidden = (gate / (1.0 + jnp.exp(-gate)) * up).astype(jnp.bfloat16)
    done = dot(hidden, down_ref[0]).astype(jnp.bfloat16)
    for k, ref in enumerate(out_refs):
        ref[0] = done[k * width : (k + 1) * width]


def combine_kernel(groups, relay_cap, high_ref, low_ref, base_ref, relay_ref, *refs):
    back = jnp.concatenate([ref[...].reshape(-1, ref.shape[-1]) for ref in refs[:groups]], 0)
    embedded = base_ref[...] + dot(high_ref[...], back) + dot(low_ref[...], back)
    packed = dot(relay_ref[...], embedded.astype(jnp.bfloat16)).astype(jnp.bfloat16)
    for k, ref in enumerate(refs[groups:]):
        ref[...] = packed[k * relay_cap : (k + 1) * relay_cap]


def place_kernel(groups, spot_ref, mask_ref, row_ref, col_ref, gain_ref, *refs):
    landed_refs = refs[:groups]
    normed_ref, dec_ref, keep_ref, low_ref, high_ref, first_ref, last_ref = refs[groups:]
    height, breadth, width = normed_ref.shape
    half = width // 2
    me = lax.axis_index("expert")
    spot = jnp.concatenate([spot_ref[pl.ds(me ^ k, 1), :] for k in range(groups)], 1)
    landed = jnp.concatenate([ref[...] for ref in landed_refs], 0)
    slots = landed.shape[0]
    rim = low_ref.shape[0]
    edge = first_ref.shape[1]
    for r in range(height):
        hit = spot == iota((breadth, slots), 0) + r * breadth
        ones = jnp.where(hit, 1.0, 0.0)
        keep = jnp.sum(ones, axis=1, keepdims=True)
        seen = dot(ones.astype(jnp.bfloat16), landed)
        seen = jnp.where(keep > 0.5, seen, mask_ref[...].astype(jnp.float32))
        left = seen[:, :half] + row_ref[r : r + 1, :]
        right = seen[:, half:] + col_ref[...]
        state = jnp.concatenate([left, right], 1)
        square = jnp.sum(state * state, axis=1, keepdims=True) * (1.0 / width)
        normed = (state * lax.rsqrt(square + EPSILON) * gain_ref[...]).astype(jnp.bfloat16)
        normed_ref[r] = normed
        dec_ref[r] = state
        keep_ref[r] = keep
        first_ref[r] = normed[:edge]
        last_ref[r] = normed[breadth - edge :]
        if r < rim:
            low_ref[r] = normed
        if r >= height - rim:
            high_ref[r - height + rim] = normed


VM = pl.BlockSpec(memory_space=pltpu.VMEM)
ROOM = 16 * 2**20
WIDE_ROOM = 56 * 2**20


def whole_call(kernel, outs, ins, name, flops, scratch=(), room=ROOM):
    size = sum(math.prod(a.shape) * a.dtype.itemsize for a in tuple(outs) + tuple(ins))
    return pl.pallas_call(
        kernel,
        out_shape=tuple(outs),
        in_specs=[VM] * len(ins),
        out_specs=tuple([VM] * len(outs)),
        scratch_shapes=list(scratch),
        compiler_params=pltpu.CompilerParams(vmem_limit_bytes=room),
        cost_estimate=pl.CostEstimate(flops=flops, bytes_accessed=size, transcendentals=0),
        name=name,
    )(*ins)


def shaped(shape, dtype):
    return jax.ShapeDtypeStruct(shape, dtype)


def experts_apply(blocks, gate, up, down, name):
    sources = len(blocks)
    local_experts, width, model_width = blocks[0].shape
    hidden = gate.shape[2]
    out_width = down.shape[2]
    each = lambda *shape: pl.BlockSpec((1,) + shape, lambda e: (e, 0, 0))
    return pl.pallas_call(
        functools.partial(ffn_kernel, sources),
        grid=(local_experts,),
        out_shape=[shaped((local_experts, width, out_width), jnp.bfloat16)] * sources,
        in_specs=[each(width, model_width)] * sources
        + [each(model_width, hidden), each(model_width, hidden), each(hidden, out_width)],
        out_specs=[each(width, out_width)] * sources,
        compiler_params=pltpu.CompilerParams(vmem_limit_bytes=WIDE_ROOM),
        cost_estimate=pl.CostEstimate(
            flops=2 * sources * local_experts * width * hidden * (2 * model_width + out_width),
            bytes_accessed=2 * local_experts * hidden * (2 * model_width + out_width),
            transcendentals=0,
        ),
        name=name,
    )(*blocks, gate, up, down)


INNER_ROOM = 32 * 2**20
OUTER_ROOM = 32 * 2**20
SPAN = 32
STRIP = 16


def shift_matrix(cols, total, groups):
    p, q = iota((cols, total), 0), iota((cols, total), 1)
    hit = jnp.zeros((cols, total), jnp.bool_)
    for start, count, origin in groups:
        hit = hit | ((p >= start) & (p < start + count) & (q - origin == p - start))
    return ones_where(hit)


def attention(q_ref, kv_ref, att_ref, starts, first_row, grid_h, grid_w, tile_h, tile_w):
    width = q_ref.shape[2]
    lanes = 256
    heads = lanes // HD
    lane_head = iota((1, lanes), 1) // HD
    masks = [lane_head == h for h in range(heads)]
    picks = [ones_where(m) for m in masks]
    key_rows = 2 + 2 * RAD
    keys = key_rows * SPAN
    scale = math.log2(math.e) / math.sqrt(HD)
    band_row = lax.axis_index("dp")
    owner = lax.axis_index("expert")

    def column(j, carry):
        c0 = pl.multiple_of(j * STRIP, STRIP)
        for count, q_row, k_row in starts:
            items = count * STRIP
            qi, ki = iota((items, keys), 0), iota((items, keys), 1)
            key_row = first_row + k_row + ki // SPAN
            down = key_row - q_row - qi // STRIP
            across = ki % SPAN - qi % STRIP
            grid_row = band_row * tile_h + key_row
            grid_col = owner * tile_w + j * STRIP - RAD + ki % SPAN
            ok = (down >= -RAD) & (down <= RAD) & (across >= 0) & (across <= 2 * RAD)
            ok = ok & (grid_row >= 0) & (grid_row < grid_h) & (grid_col >= 0) & (grid_col < grid_w)
            bias = jnp.where(ok, 0.0, -1e30)
            for g in range(width // lanes):
                part = slice(g * lanes, (g + 1) * lanes)
                queries = q_ref[q_row : q_row + count, pl.ds(c0, STRIP), part].reshape(items, lanes)
                key = kv_ref[k_row : k_row + key_rows, pl.ds(c0, SPAN), part].reshape(keys, lanes)
                value = kv_ref[
                    k_row : k_row + key_rows, pl.ds(c0, SPAN), width + g * lanes : width + (g + 1) * lanes
                ].reshape(keys, lanes)
                stacked = jnp.concatenate([queries * pick for pick in picks], 0)
                score = dot(stacked, key, ((1,), (1,))).reshape(heads, items, keys)
                weight = jnp.exp2(score * scale + bias[None]).reshape(heads * items, keys)
                total = jnp.sum(weight, axis=1, keepdims=True)
                mixed = dot(weight.astype(jnp.bfloat16), value) * (1.0 / total)
                mixed = mixed.reshape(heads, items, lanes)
                out = mixed[0]
                for h in range(1, heads):
                    out = jnp.where(masks[h], mixed[h], out)
                att_ref[q_row : q_row + count, pl.ds(c0, STRIP), part] = out.astype(jnp.bfloat16).reshape(
                    count, STRIP, lanes
                )
        return carry

    lax.fori_loop(0, tile_w // STRIP, column, 0)


def row_groups(rows):
    return [(min(2, rows.stop - r), r) for r in range(rows.start, rows.stop, 2)]


def inner_kernel(grid_h, grid_w, normed_ref, before_ref, after_ref, wqkv_ref, q_ref, kv_ref, att_ref):
    height, breadth, width = normed_ref.shape
    cols = kv_ref.shape[1]
    edge = before_ref.shape[1]
    shift = shift_matrix(
        cols, breadth + 2 * edge, ((RAD, breadth, 0), (0, RAD, breadth + edge - RAD), (RAD + breadth, RAD, breadth + edge))
    )
    rows = []
    for r in range(height):
        joined = jnp.concatenate([normed_ref[r], before_ref[r], after_ref[r]], 0)
        rows.append(dot(shift, joined).astype(jnp.bfloat16))
    wide = jnp.concatenate(rows, 0)
    kv_ref[...] = dot(wide, wqkv_ref[:, width:]).astype(jnp.bfloat16).reshape(kv_ref.shape)
    flat = normed_ref[...].reshape(height * breadth, width)
    q_ref[...] = dot(flat, wqkv_ref[:, :width]).astype(jnp.bfloat16).reshape(q_ref.shape)
    starts = [(n, r, r - RAD) for n, r in row_groups(slice(RAD, height - RAD))]
    attention(q_ref, kv_ref, att_ref, starts, 0, grid_h, grid_w, height, breadth)


def outer_kernel(
    grid_h, grid_w, up_ref, up_edge_ref, down_ref, down_edge_ref, q_ref, kv_in_ref, att_in_ref, dec_in_ref, keep_ref,
    pixels_ref, wqkv_ref, wout_ref, whead_ref, decoded_ref, dattn_ref, loss_ref, kv_ref, att_ref,
):
    height, breadth, pd = pixels_ref.shape
    width = q_ref.shape[2]
    cols = kv_ref.shape[1]
    edge = up_edge_ref.shape[1]
    middle = edge // 2
    bf16 = jnp.bfloat16
    shift = shift_matrix(
        cols, breadth + edge, ((RAD, breadth, 0), (0, RAD, breadth + middle - RAD), (RAD + breadth, RAD, breadth + middle))
    )
    kv_ref[RAD : RAD + height] = kv_in_ref[...]
    for main, side, start in ((up_ref, up_edge_ref, 0), (down_ref, down_edge_ref, RAD + height)):
        wide = [dot(shift, jnp.concatenate([main[r], side[r]], 0)).astype(bf16) for r in range(RAD)]
        kv = dot(jnp.concatenate(wide, 0), wqkv_ref[:, width:]).astype(bf16)
        kv_ref[start : start + RAD] = kv.reshape(RAD, cols, 2 * width)
    inner = slice(RAD, height - RAD)
    att_ref[inner] = att_in_ref[inner]
    starts = [(n, r, r) for n, r in row_groups(slice(0, RAD))]
    starts += [(n, r, min(r, height + 2 * RAD - 2 - 2 * RAD)) for n, r in row_groups(slice(height - RAD, height))]
    attention(q_ref, kv_ref, att_ref, starts, -RAD, grid_h, grid_w, height, breadth)
    loss = jnp.zeros((1, 1), jnp.float32)
    step = height // 2
    for r in range(0, height, step):
        rows = slice(r, r + step)
        count = step * breadth
        att = att_ref[rows].reshape(count, width)
        decoded = (dec_in_ref[rows].reshape(count, width) + dot(att, wout_ref[...])).astype(bf16)
        decoded_ref[rows] = decoded.reshape(step, breadth, width)
        pred = dot(decoded, whead_ref[...])
        pix = pixels_ref[rows].reshape(count, pd).astype(jnp.float32)
        centred = pix - jnp.sum(pix, axis=1, keepdims=True) * (1.0 / pd)
        spread = jnp.sum(centred * centred, axis=1, keepdims=True) * (1.0 / pd)
        error = (pred - centred * lax.rsqrt(spread + EPSILON)) * (1.0 - keep_ref[rows].reshape(count, 1))
        loss = loss + jnp.sum(jnp.sum(error * error, axis=1, keepdims=True), axis=0, keepdims=True)
        back = dot(error.astype(bf16), whead_ref[...], ((1,), (1,))).astype(bf16)
        dattn_ref[rows] = dot(back, wout_ref[...], ((1,), (1,))).astype(bf16).reshape(step, breadth, width)
    loss_ref[...] = loss * (0.5 / (height * breadth * pd))


def local(
    tokens,
    expert_ids,
    gate_weights,
    target,
    expert_gate,
    expert_up,
    expert_down,
    dec_embed,
    mask_token,
    norm_gain,
    w_qkv,
    w_out,
    w_head,
    pixels,
):
    groups = lax.axis_size("expert")
    tok_rows = tokens.shape[0]
    model_width = tokens.shape[1]
    local_experts = expert_gate.shape[0]
    experts_all = local_experts * groups
    capacity = 3 * tok_rows * TOPK // (2 * experts_all)
    tile_height = pixels.shape[0]
    tile_width = pixels.shape[1]
    tile_size = tile_height * tile_width
    relay_cap = tile_size // groups
    dec_width = dec_embed.shape[1]
    bf16 = jnp.bfloat16
    width = -(-capacity // 16) * 16
    slots = experts_all * width
    block = shaped((local_experts, width, model_width), bf16)

    def swap(value, k):
        return value if k == 0 else lax.ppermute(value, "expert", [(i, i ^ k) for i in range(groups)])

    def swap_all(values):
        moved = {k: swap(values[k], k) for k in list(range(cut, groups)) + list(range(cut))[::-1]}
        return [moved[k] for k in range(groups)]

    cut = groups * 3 // 4
    outgoing = whole_call(
        functools.partial(pack_kernel, width, experts_all, local_experts),
        [block] * groups,
        [expert_ids.T, tokens],
        "pack",
        2 * slots * tok_rows * model_width,
        room=WIDE_ROOM,
    )
    outgoing, ids_later, tokens_later, down_later = lax.optimization_barrier(
        (outgoing, expert_ids, tokens, expert_down)
    )
    arrived = swap_all(outgoing)
    relay_slots = groups * relay_cap
    high, low, base, relay, spots = whole_call(
        functools.partial(prep_kernel, width, experts_all, local_experts, relay_cap, tile_size),
        [
            shaped((tok_rows, slots), bf16),
            shaped((tok_rows, slots), bf16),
            shaped((tok_rows, dec_width), jnp.float32),
            shaped((relay_slots, tok_rows), bf16),
            shaped((groups, relay_cap), jnp.int32),
        ],
        [ids_later.T, gate_weights.T, target.reshape(1, tok_rows), tokens_later, dec_embed],
        "prep",
        2 * tok_rows * dec_width * model_width,
        room=WIDE_ROOM,
    )
    spots = lax.all_to_all(spots, "expert", split_axis=0, concat_axis=0, tiled=True)
    folded = fold(down_later, dec_embed)
    arrived, high, low, base, relay, folded, spots = lax.optimization_barrier(
        (arrived, high, low, base, relay, folded, spots)
    )
    returned = swap_all(experts_apply(arrived, expert_gate, expert_up, folded, "experts"))
    packed = whole_call(
        functools.partial(combine_kernel, groups, relay_cap),
        [shaped((relay_cap, dec_width), bf16)] * groups,
        [high, low, base, relay] + returned,
        "combine",
        2 * tok_rows * dec_width * (2 * slots + relay_slots),
    )
    landed = swap_all(packed)
    owner = lax.axis_index("expert")
    band_row = lax.axis_index("dp")
    row_ids = band_row * tile_height + jnp.arange(tile_height, dtype=jnp.int32)
    col_ids = owner * tile_width + jnp.arange(tile_width, dtype=jnp.int32)
    row_table, col_table = positional(row_ids, col_ids, dec_width)
    edge = 16
    grid_shape = (tile_height, tile_width, dec_width)
    normed, decoder_in, keep, top, bottom, first, last = whole_call(
        functools.partial(place_kernel, groups),
        [
            shaped(grid_shape, bf16),
            shaped(grid_shape, jnp.float32),
            shaped((tile_height, tile_width, 1), jnp.float32),
            shaped((RAD, tile_width, dec_width), bf16),
            shaped((RAD, tile_width, dec_width), bf16),
            shaped((tile_height, edge, dec_width), bf16),
            shaped((tile_height, edge, dec_width), bf16),
        ],
        [spots, mask_token.reshape(1, dec_width), row_table, col_table, norm_gain.reshape(1, dec_width)] + landed,
        "place",
        2 * tile_size * relay_slots * dec_width,
    )
    bands = lax.axis_size("dp")
    upward = [(i + 1, i) for i in range(bands - 1)]
    downward = [(i, i + 1) for i in range(bands - 1)]
    above = lax.ppermute(bottom, "dp", downward)
    below = lax.ppermute(top, "dp", upward)
    before = lax.ppermute(last, "expert", [(i, i + 1) for i in range(groups - 1)])
    after = lax.ppermute(first, "expert", [(i + 1, i) for i in range(groups - 1)])
    sides = jnp.concatenate([before[:, edge // 2 :], after[:, : edge // 2]], 1)
    above_edge = lax.ppermute(sides[tile_height - RAD :], "dp", [(i, (i + 1) % bands) for i in range(bands)])
    below_edge = lax.ppermute(sides[:RAD], "dp", [((i + 1) % bands, i) for i in range(bands)])
    grid_height = tile_height * bands
    grid_width = tile_width * groups
    cols = -(-(tile_width - STRIP + SPAN) // 16) * 16
    queries, kv, attended = whole_call(
        functools.partial(inner_kernel, grid_height, grid_width),
        [
            shaped(grid_shape, bf16),
            shaped((tile_height, cols, 2 * dec_width), bf16),
            shaped(grid_shape, bf16),
        ],
        [normed, before, after, w_qkv],
        "inner",
        6 * tile_size * dec_width * dec_width,
        room=INNER_ROOM,
    )
    return whole_call(
        functools.partial(outer_kernel, grid_height, grid_width),
        [shaped(grid_shape, bf16), shaped(grid_shape, bf16), shaped((1, 1), jnp.float32)],
        [above, above_edge, below, below_edge, queries, kv, attended, decoder_in, keep, pixels, w_qkv, w_out, w_head],
        "outer",
        12 * tile_size * dec_width * dec_width,
        [
            pltpu.VMEM((tile_height + 2 * RAD, cols, 2 * dec_width), bf16),
            pltpu.VMEM(grid_shape, bf16),
        ],
        room=OUTER_ROOM,
    )

def solution(mesh):
    in_specs = (
        P(("dp", "expert"), None),
        P(("dp", "expert"), None),
        P(("dp", "expert"), None),
        P(("dp", "expert")),
        P("expert", None, None),
        P("expert", None, None),
        P("expert", None, None),
        P(),
        P(),
        P(),
        P(),
        P(),
        P(),
        P("dp", "expert", None),
    )
    out_specs = (P("dp", "expert", None), P("dp", "expert", None), P("dp", "expert"))
    return jax.shard_map(local, mesh=mesh, in_specs=in_specs, out_specs=out_specs, check_vma=False)
```

profile of v0, /device:TPU:4, one launch (start us, length us, event | category | flops | bytes accessed | tf_op | source)
XLA Modules:
  0.0 114.9 jit_solution(5576774979116144089)
XLA Ops:
  0.6 3.3 %pack.1 = (bf16[2,48,1280]{2,1,0:T(8,128)(2,1)}, bf16[2,48,1280]{2,1,0:T(8,128)(2,1)}, bf16[2,48,1280]{2,1,0:T(8,128)(2,1)}, bf16[2,48,1280]{2,1,0:T(8,128)(2,1)...) custom-call(s32[2,256]{1,0:T(2,128)} %bitcast.12, ...), custom_call_target="tpu_custom_call" | custom-call | flops 503316480 | bytes 2623488 | tf_op jit(solution)/shard_map/pack/pallas_call | solution.py:203
  4.0 1.5 %collective-permute-start.1 = (bf16[2,48,1280]{2,1,0:T(8,128)(2,1)}, bf16[2,48,1280]{2,1,0:T(8,128)(2,1)S(1)}, u32[]{:S(2)}, u32[]{:S(2)}) collective-permute-start(bf16[2,48,1280]{2,1,0:T(8,128)(2,1)} %get-tuple-element.77), channel_id=1, source_target_pairs={{0,2},{1,3},{2,0},{3,1},{4,6},{5,7},{6,4},{7,5},{8,10},{9,11},{10,... | collective-permute-start | bytes 737288 | tf_op jit(solution)/shard_map/ppermute | solution.py:404
  5.5 0.4 collective-permute-start.2
  5.8 0.3 collective-permute-start.3
  6.1 1.3 %collective-permute-start.4 = (bf16[2,48,1280]{2,1,0:T(8,128)(2,1)}, bf16[2,48,1280]{2,1,0:T(8,128)(2,1)S(1)}, u32[]{:S(2)}, u32[]{:S(2)}) collective-permute-start(bf16[2,48,1280]{2,1,0:T(8,128)(2,1)} %get-tuple-element.80), channel_id=1, source_target_pairs={{0,5},{1,4},{2,7},{3,6},{4,1},{5,0},{6,3},{7,2},{8,13},{9,12},{10,... | collective-permute-start | bytes 737288 | tf_op jit(solution)/shard_map/ppermute | solution.py:404
  7.5 3.8 %prep.1 = (bf16[256,768]{1,0:T(8,128)(2,1)}, bf16[256,768]{1,0:T(8,128)(2,1)}, f32[256,512]{1,0:T(8,128)}, bf16[1024,256]{1,0:T(8,128)(2,1)}, s32[8,128]{1,0:T(8,128)}) custom-call(s32[2,256]{1,0:T(2,128)} %bitcast.13, f32[2,256]{1,0:T(2,128)} %bitcast.14, s32[1,256]{1,0:T(1,128)} %bitcast.15, bf16[256,1280]{1,0:T(8,128)(2,1)} %tokens_ref.2, ...), custom_call_target="tpu_custom_call" | custom-call | flops 335544320 | bytes 3810304 | tf_op jit(solution)/shard_map/prep/pallas_call | solution.py:203
  11.3 4.3 %all-to-all-start = ((s32[8,1,128]{2,1,0:T(1,128)}), s32[8,1,128]{2,1,0:T(1,128)S(1)}, u32[]{:S(2)}, u32[]{:S(2)}) async-start(s32[8,1,128]{2,1,0:T(1,128)} %bitcast.11), calls=%async_computation | async-start | bytes 8192 | tf_op jit(solution)/shard_map/all_to_all | solution.py:438
  15.6 1.5 %collective-permute-start.5 = (bf16[2,48,1280]{2,1,0:T(8,128)(2,1)}, bf16[2,48,1280]{2,1,0:T(8,128)(2,1)S(1)}, u32[]{:S(2)}, u32[]{:S(2)}) collective-permute-start(bf16[2,48,1280]{2,1,0:T(8,128)(2,1)} %get-tuple-element.81), channel_id=1, source_target_pairs={{0,6},{1,7},{2,4},{3,5},{4,2},{5,3},{6,0},{7,1},{8,14},{9,15},{10,... | collective-permute-start | bytes 737288 | tf_op jit(solution)/shard_map/ppermute | solution.py:404
  17.2 0.9 collective-permute-start.6
  18.1 6.7 %fold.1.refs_10_ = bf16[2,1024,512]{2,1,0:T(8,128)(2,1)} custom-call(bf16[2,1024,1280]{2,1,0:T(8,128)(2,1)} %down_ref, bf16[1280,512]{1,0:T(8,128)(2,1)} %embed_ref.3), custom_call_target="tpu_custom_call" | custom-call | flops 2684354560 | bytes 5242880 | tf_op jit(solution)/shard_map/fold/pallas_call | solution.py:123
  24.9 0.7 collective-permute-done.5.refs_6_
  25.6 3.7 %collective-permute-done.6.refs_7_ = bf16[2,48,1280]{2,1,0:T(8,128)(2,1)S(1)} collective-permute-done((bf16[2,48,1280]{2,1,0:T(8,128)(2,1)}, bf16[2,48,1280]{2,1,0:T(8,128)(2,1)S(1)}, u32[]{:S(2)}, u32[]{:S(2)}) %collective-permute-start.6) | collective-permute-done | bytes 245792 | tf_op jit(solution)/shard_map/ppermute | solution.py:404
  29.3 0.7 copy-done.17
  30.0 9.3 %experts.1 = (bf16[2,48,512]{2,1,0:T(8,128)(2,1)}, bf16[2,48,512]{2,1,0:T(8,128)(2,1)}, bf16[2,48,512]{2,1,0:T(8,128)(2,1)}, bf16[2,48,512]{2,1,0:T(8,128)(2,1)}...) custom-call(bf16[2,48,1280]{2,1,0:T(8,128)(2,1)} %get-tuple-element., ...), custom_call_target="tpu_custom_call" | custom-call | flops 4831838208 | bytes 12582912 | tf_op jit(solution)/shard_map/experts/pallas_call | solution.py:225
  39.4 0.7 collective-permute-start.7
  40.1 1.5 %collective-permute-start.8 = (bf16[2,48,512]{2,1,0:T(8,128)(2,1)}, bf16[2,48,512]{2,1,0:T(8,128)(2,1)S(1)}, u32[]{:S(2)}, u32[]{:S(2)}) collective-permute-start(bf16[2,48,512]{2,1,0:T(8,128)(2,1)} %get-tuple-element.107), channel_id=1, source_target_pairs={{0,2},{1,3},{2,0},{3,1},{4,6},{5,7},{6,4},{7,5},{8,10},{9,11},{10,... | collective-permute-start | bytes 294920 | tf_op jit(solution)/shard_map/ppermute | solution.py:404
  41.5 0.3 multiply_sine_fusion
  41.8 0.1 collective-permute-start.9
  41.9 0.6 collective-permute-start.10
  42.5 1.4 %collective-permute-start.11 = (bf16[2,48,512]{2,1,0:T(8,128)(2,1)}, bf16[2,48,512]{2,1,0:T(8,128)(2,1)S(1)}, u32[]{:S(2)}, u32[]{:S(2)}) collective-permute-start(bf16[2,48,512]{2,1,0:T(8,128)(2,1)} %get-tuple-element.110), channel_id=1, source_target_pairs={{0,5},{1,4},{2,7},{3,6},{4,1},{5,0},{6,3},{7,2},{8,13},{9,12},{10,... | collective-permute-start | bytes 294920 | tf_op jit(solution)/shard_map/ppermute | solution.py:404
  43.9 1.5 %collective-permute-start.12 = (bf16[2,48,512]{2,1,0:T(8,128)(2,1)}, bf16[2,48,512]{2,1,0:T(8,128)(2,1)S(1)}, u32[]{:S(2)}, u32[]{:S(2)}) collective-permute-start(bf16[2,48,512]{2,1,0:T(8,128)(2,1)} %get-tuple-element.111), channel_id=1, source_target_pairs={{0,6},{1,7},{2,4},{3,5},{4,2},{5,3},{6,0},{7,1},{8,14},{9,15},{10,... | collective-permute-start | bytes 294920 | tf_op jit(solution)/shard_map/ppermute | solution.py:404
  45.4 1.0 collective-permute-start.13
  46.4 0.8 collective-permute-done.9.refs_3_
  47.2 0.6 collective-permute-done.10.refs_4_
  47.8 5.8 %collective-permute-done.11.refs_5_ = bf16[2,48,512]{2,1,0:T(8,128)(2,1)S(1)} collective-permute-done((bf16[2,48,512]{2,1,0:T(8,128)(2,1)}, bf16[2,48,512]{2,1,0:T(8,128)(2,1)S(1)}, u32[]{:S(2)}, u32[]{:S(2)}) %collective-permute-start.11) | collective-permute-done | bytes 98336 | tf_op jit(solution)/shard_map/ppermute | solution.py:404
  53.6 0.9 copy-done.8
  54.5 1.0 combine.1
  55.4 0.2 collective-permute-start.14
  55.6 1.5 %collective-permute-start.15 = (bf16[128,512]{1,0:T(8,128)(2,1)S(1)}, bf16[128,512]{1,0:T(8,128)(2,1)S(1)}, u32[]{:S(2)}, u32[]{:S(2)}) collective-permute-start(bf16[128,512]{1,0:T(8,128)(2,1)S(1)} %get-tuple-element.115), channel_id=1, source_target_pairs={{0,2},{1,3},{2,0},{3,1},{4,6},{5,7},{6,4},{7,5},{8,10},{9,11},{10,... | collective-permute-start | bytes 393224 | tf_op jit(solution)/shard_map/ppermute | solution.py:404
  57.1 0.1 multiply_sine_fusion.1
  57.2 0.3 collective-permute-start.16
  57.5 0.4 collective-permute-start.17
  58.0 1.4 %collective-permute-start.18 = (bf16[128,512]{1,0:T(8,128)(2,1)S(1)}, bf16[128,512]{1,0:T(8,128)(2,1)S(1)}, u32[]{:S(2)}, u32[]{:S(2)}) collective-permute-start(bf16[128,512]{1,0:T(8,128)(2,1)S(1)} %get-tuple-element.118), channel_id=1, source_target_pairs={{0,5},{1,4},{2,7},{3,6},{4,1},{5,0},{6,3},{7,2},{8,13},{9,12},{10,... | collective-permute-start | bytes 393224 | tf_op jit(solution)/shard_map/ppermute | solution.py:404
  59.3 1.5 %collective-permute-start.19 = (bf16[128,512]{1,0:T(8,128)(2,1)S(1)}, bf16[128,512]{1,0:T(8,128)(2,1)S(1)}, u32[]{:S(2)}, u32[]{:S(2)}) collective-permute-start(bf16[128,512]{1,0:T(8,128)(2,1)S(1)} %get-tuple-element.119), channel_id=1, source_target_pairs={{0,6},{1,7},{2,4},{3,5},{4,2},{5,3},{6,0},{7,1},{8,14},{9,15},{10,... | collective-permute-start | bytes 393224 | tf_op jit(solution)/shard_map/ppermute | solution.py:404
  60.8 1.2 %collective-permute-done.15.refs_2_ = bf16[128,512]{1,0:T(8,128)(2,1)S(1)} collective-permute-done((bf16[128,512]{1,0:T(8,128)(2,1)S(1)}, bf16[128,512]{1,0:T(8,128)(2,1)S(1)}, u32[]{:S(2)}, u32[]{:S(2)}) %collective-permute-start.15) | collective-permute-done | bytes 131104 | tf_op jit(solution)/shard_map/ppermute | solution.py:404
  62.0 0.1 collective-permute-start.20
  62.1 1.6 %collective-permute-done.16.refs_3_ = bf16[128,512]{1,0:T(8,128)(2,1)S(1)} collective-permute-done((bf16[128,512]{1,0:T(8,128)(2,1)S(1)}, bf16[128,512]{1,0:T(8,128)(2,1)S(1)}, u32[]{:S(2)}, u32[]{:S(2)}) %collective-permute-start.16) | collective-permute-done | bytes 131104 | tf_op jit(solution)/shard_map/ppermute | solution.py:404
  63.7 0.6 collective-permute-done.17.refs_4_
  64.3 7.0 %collective-permute-done.18.refs_5_ = bf16[128,512]{1,0:T(8,128)(2,1)S(1)} collective-permute-done((bf16[128,512]{1,0:T(8,128)(2,1)S(1)}, bf16[128,512]{1,0:T(8,128)(2,1)S(1)}, u32[]{:S(2)}, u32[]{:S(2)}) %collective-permute-start.18) | collective-permute-done | bytes 131104 | tf_op jit(solution)/shard_map/ppermute | solution.py:404
  71.4 1.8 %place.1 = (bf16[8,128,512]{2,1,0:T(8,128)(2,1)S(1)}, f32[8,128,512]{2,1,0:T(8,128)S(1)}, f32[8,128,1]{2,1,0:T(8,128)S(1)}, bf16[3,128,512]{2,1,0:T(8,128)(2,1)S...) custom-call(s32[8,128]{1,0:T(8,128)S(1)} %bitcast.9, ...), custom_call_target="tpu_custom_call" | custom-call | flops 1073741824 | bytes 5393408 | tf_op jit(solution)/shard_map/place/pallas_call | solution.py:203
  73.2 2.2 %collective-permute-start.22 = (bf16[8,16,512]{2,1,0:T(8,128)(2,1)S(1)}, bf16[8,16,512]{2,1,0:T(8,128)(2,1)S(1)}, u32[]{:S(2)}, u32[]{:S(2)}) collective-permute-start(bf16[8,16,512]{2,1,0:T(8,128)(2,1)S(1)} %get-tuple-element.122), channel_id=1, source_target_pairs={{0,1},{1,2},{2,3},{3,4},{4,5},{5,6},{6,7},{8,9},{9,10},{10,11},{11... | collective-permute-start | bytes 393224 | tf_op jit(solution)/shard_map/ppermute | solution.py:479
  75.4 4.2 %collective-permute-start.23 = (bf16[8,16,512]{2,1,0:T(8,128)(2,1)S(1)}, bf16[8,16,512]{2,1,0:T(8,128)(2,1)S(1)}, u32[]{:S(2)}, u32[]{:S(2)}) collective-permute-start(bf16[8,16,512]{2,1,0:T(8,128)(2,1)S(1)} %get-tuple-element.123), channel_id=1, source_target_pairs={{1,0},{2,1},{3,2},{4,3},{5,4},{6,5},{7,6},{9,8},{10,9},{11,10},{12... | collective-permute-start | bytes 393224 | tf_op jit(solution)/shard_map/ppermute | solution.py:480
  79.7 3.5 %collective-permute-start.21 = (bf16[3,128,512]{2,1,0:T(8,128)(2,1)S(1)}, bf16[3,128,512]{2,1,0:T(8,128)(2,1)S(1)}, u32[]{:S(2)}, u32[]{:S(2)}) collective-permute-start(bf16[3,128,512]{2,1,0:T(8,128)(2,1)S(1)} %get-tuple-element.121), channel_id=1, source_target_pairs={{0,8},{8,16},{16,24},{1,9},{9,17},{17,25},{2,10},{10,18},{18,26},{... | collective-permute-start | bytes 1179656 | tf_op jit(solution)/shard_map/ppermute | solution.py:477
  83.2 1.3 %collective-permute-start.25 = (bf16[3,128,512]{2,1,0:T(8,128)(2,1)S(1)}, bf16[3,128,512]{2,1,0:T(8,128)(2,1)S(1)}, u32[]{:S(2)}, u32[]{:S(2)}) collective-permute-start(bf16[3,128,512]{2,1,0:T(8,128)(2,1)S(1)} %get-tuple-element.124), channel_id=1, source_target_pairs={{8,0},{16,8},{24,16},{9,1},{17,9},{25,17},{10,2},{18,10},{26,18},{... | collective-permute-start | bytes 1179656 | tf_op jit(solution)/shard_map/ppermute | solution.py:478
  84.6 4.6 %collective-permute-start.26 = (bf16[3,16,512]{2,1,0:T(8,128)(2,1)S(1)}, bf16[3,16,512]{2,1,0:T(8,128)(2,1)S(1)}, u32[]{:S(2)}, u32[]{:S(2)}) collective-permute-start(bf16[3,16,512]{2,1,0:T(8,128)(2,1)S(1)} %get-tuple-element.131), channel_id=1, source_target_pairs={{8,0},{16,8},{24,16},{0,24},{9,1},{17,9},{25,17},{1,25},{10,2},{18... | collective-permute-start | bytes 147464 | tf_op jit(solution)/shard_map/ppermute | solution.py:483
  89.2 6.8 %inner.1 = (bf16[8,128,512]{2,1,0:T(8,128)(2,1)S(1)}, bf16[8,144,1024]{2,1,0:T(8,128)(2,1)S(1)}, bf16[8,128,512]{2,1,0:T(8,128)(2,1)S(1)}) custom-call(bf16[8,128,512]{2,1,0:T(8,128)(2,1)S(1)} %get-tuple-element.125.normed_ref, bf16[8,16,512]{2,1,0:T(8,128)(2,1)S(1)} %collective-permute-done.22.before_ref, ...), custom_call_target="tpu_custom_call" | custom-call | flops 1610612736 | bytes 7340032 | tf_op jit(solution)/shard_map/inner/pallas_call | solution.py:203
  96.1 2.9 %collective-permute-done.24.up_edge_ref = bf16[3,16,512]{2,1,0:T(8,128)(2,1)S(1)} collective-permute-done((bf16[3,16,512]{2,1,0:T(8,128)(2,1)S(1)}, bf16[3,16,512]{2,1,0:T(8,128)(2,1)S(1)}, u32[]{:S(2)}, u32[]{:S(2)}) %collective-permute-start.24) | collective-permute-done | bytes 49184 | tf_op jit(solution)/shard_map/ppermute | solution.py:482
  99.0 15.9 %outer.1 = (bf16[8,128,512]{2,1,0:T(8,128)(2,1)}, bf16[8,128,512]{2,1,0:T(8,128)(2,1)}, f32[1,1]{1,0:T(1,128)}) custom-call(bf16[3,128,512]{2,1,0:T(8,128)(2,1)S(1)} %collective-permute-done.21.up_ref, bf16[3,16,512]{2,1,0:T(8,128)(2,1)S(1)} %collective-permute-done.24.up_edge_ref, bf16[3,128,512]{2,1,0:T(8,128)(2,1)S(1)} %collective-permute-done.25.down_ref, ...), custom_call_target="tpu_custom_call" | custom-call | flops 3221225472 | bytes 13996036 | tf_op jit(solution)/shard_map/outer/pallas_call | solution.py:203
  (63 shorter events, 0.2 us)
Async XLA Ops:
  4.0 11.7 %collective-permute-start = (bf16[2,48,1280]{2,1,0:T(8,128)(2,1)}, bf16[2,48,1280]{2,1,0:T(8,128)(2,1)S(1)}, u32[]{:S(2)}, u32[]{:S(2)}) collective-permute-start(bf16[2,48,1280]{2,1,0:T(8,128)(2,1)} %get-tuple-element.76), channel_id=1, source_target_pairs={{0,1},{1,0},{2,3},{3,2},{4,5},{5,4},{6,7},{7,6},{8,9},{9,8},{10,11... | collective-permute-start | bytes 737288 | tf_op jit(solution)/shard_map/ppermute | solution.py:404
  4.0 13.2 %collective-permute-start.1 = (bf16[2,48,1280]{2,1,0:T(8,128)(2,1)}, bf16[2,48,1280]{2,1,0:T(8,128)(2,1)S(1)}, u32[]{:S(2)}, u32[]{:S(2)}) collective-permute-start(bf16[2,48,1280]{2,1,0:T(8,128)(2,1)} %get-tuple-element.77), channel_id=1, source_target_pairs={{0,2},{1,3},{2,0},{3,1},{4,6},{5,7},{6,4},{7,5},{8,10},{9,11},{10,... | collective-permute-start | bytes 737288 | tf_op jit(solution)/shard_map/ppermute | solution.py:404
  5.5 19.4 %collective-permute-start.2 = (bf16[2,48,1280]{2,1,0:T(8,128)(2,1)}, bf16[2,48,1280]{2,1,0:T(8,128)(2,1)S(1)}, u32[]{:S(2)}, u32[]{:S(2)}) collective-permute-start(bf16[2,48,1280]{2,1,0:T(8,128)(2,1)} %get-tuple-element.78), channel_id=1, source_target_pairs={{0,3},{1,2},{2,1},{3,0},{4,7},{5,6},{6,5},{7,4},{8,11},{9,10},{10,... | collective-permute-start | bytes 737288 | tf_op jit(solution)/shard_map/ppermute | solution.py:404
  5.8 19.0 %collective-permute-start.3 = (bf16[2,48,1280]{2,1,0:T(8,128)(2,1)}, bf16[2,48,1280]{2,1,0:T(8,128)(2,1)S(1)}, u32[]{:S(2)}, u32[]{:S(2)}) collective-permute-start(bf16[2,48,1280]{2,1,0:T(8,128)(2,1)} %get-tuple-element.79), channel_id=1, source_target_pairs={{0,4},{1,5},{2,6},{3,7},{4,0},{5,1},{6,2},{7,3},{8,12},{9,13},{10,... | collective-permute-start | bytes 737288 | tf_op jit(solution)/shard_map/ppermute | solution.py:404
  6.1 18.8 %collective-permute-start.4 = (bf16[2,48,1280]{2,1,0:T(8,128)(2,1)}, bf16[2,48,1280]{2,1,0:T(8,128)(2,1)S(1)}, u32[]{:S(2)}, u32[]{:S(2)}) collective-permute-start(bf16[2,48,1280]{2,1,0:T(8,128)(2,1)} %get-tuple-element.80), channel_id=1, source_target_pairs={{0,5},{1,4},{2,7},{3,6},{4,1},{5,0},{6,3},{7,2},{8,13},{9,12},{10,... | collective-permute-start | bytes 737288 | tf_op jit(solution)/shard_map/ppermute | solution.py:404
  11.3 13.5 %all-to-all-start = ((s32[8,1,128]{2,1,0:T(1,128)}), s32[8,1,128]{2,1,0:T(1,128)S(1)}, u32[]{:S(2)}, u32[]{:S(2)}) async-start(s32[8,1,128]{2,1,0:T(1,128)} %bitcast.11), calls=%async_computation | async-start | bytes 8192 | tf_op jit(solution)/shard_map/all_to_all | solution.py:438
  15.6 9.1 %copy-start.11 = (bf16[2,48,1280]{2,1,0:T(8,128)(2,1)}, bf16[2,48,1280]{2,1,0:T(8,128)(2,1)S(1)}, u32[]{:S(2)}) copy-start(bf16[2,48,1280]{2,1,0:T(8,128)(2,1)S(1)} %collective-permute-done.refs_1_) | copy-start | bytes 737284
  15.6 10.0 %collective-permute-start.5 = (bf16[2,48,1280]{2,1,0:T(8,128)(2,1)}, bf16[2,48,1280]{2,1,0:T(8,128)(2,1)S(1)}, u32[]{:S(2)}, u32[]{:S(2)}) collective-permute-start(bf16[2,48,1280]{2,1,0:T(8,128)(2,1)} %get-tuple-element.81), channel_id=1, source_target_pairs={{0,6},{1,7},{2,4},{3,5},{4,2},{5,3},{6,0},{7,1},{8,14},{9,15},{10,... | collective-permute-start | bytes 737288 | tf_op jit(solution)/shard_map/ppermute | solution.py:404
  17.2 7.6 %copy-start.12 = (bf16[2,48,1280]{2,1,0:T(8,128)(2,1)}, bf16[2,48,1280]{2,1,0:T(8,128)(2,1)S(1)}, u32[]{:S(2)}) copy-start(bf16[2,48,1280]{2,1,0:T(8,128)(2,1)S(1)} %collective-permute-done.1.refs_2_) | copy-start | bytes 737284
  17.2 12.1 %collective-permute-start.6 = (bf16[2,48,1280]{2,1,0:T(8,128)(2,1)}, bf16[2,48,1280]{2,1,0:T(8,128)(2,1)S(1)}, u32[]{:S(2)}, u32[]{:S(2)}) collective-permute-start(bf16[2,48,1280]{2,1,0:T(8,128)(2,1)} %get-tuple-element.82), channel_id=1, source_target_pairs={{0,7},{1,6},{2,5},{3,4},{4,3},{5,2},{6,1},{7,0},{8,15},{9,14},{10,... | collective-permute-start | bytes 737288 | tf_op jit(solution)/shard_map/ppermute | solution.py:404
  24.8 5.2 %copy-start.13 = (bf16[2,48,1280]{2,1,0:T(8,128)(2,1)}, bf16[2,48,1280]{2,1,0:T(8,128)(2,1)S(1)}, u32[]{:S(2)}) copy-start(bf16[2,48,1280]{2,1,0:T(8,128)(2,1)S(1)} %collective-permute-done.2.refs_3_) | copy-start | bytes 737284
  24.9 5.1 %copy-start.14 = (bf16[2,48,1280]{2,1,0:T(8,128)(2,1)}, bf16[2,48,1280]{2,1,0:T(8,128)(2,1)S(1)}, u32[]{:S(2)}) copy-start(bf16[2,48,1280]{2,1,0:T(8,128)(2,1)S(1)} %collective-permute-done.3.refs_4_) | copy-start | bytes 737284
  24.9 5.1 %copy-start.15 = (bf16[2,48,1280]{2,1,0:T(8,128)(2,1)}, bf16[2,48,1280]{2,1,0:T(8,128)(2,1)S(1)}, u32[]{:S(2)}) copy-start(bf16[2,48,1280]{2,1,0:T(8,128)(2,1)S(1)} %collective-permute-done.4.refs_5_) | copy-start | bytes 737284
  25.6 3.7 %copy-start.16 = (bf16[2,48,1280]{2,1,0:T(8,128)(2,1)}, bf16[2,48,1280]{2,1,0:T(8,128)(2,1)S(1)}, u32[]{:S(2)}) copy-start(bf16[2,48,1280]{2,1,0:T(8,128)(2,1)S(1)} %collective-permute-done.5.refs_6_) | copy-start | bytes 737284
  29.3 0.7 copy-start.17
  30.0 23.5 %copy-start.4 = (f32[256,512]{1,0:T(8,128)S(1)}, f32[256,512]{1,0:T(8,128)}, u32[]{:S(2)}) copy-start(f32[256,512]{1,0:T(8,128)} %get-tuple-element.94.base_ref) | copy-start | bytes 1572868
  30.0 23.5 %copy-start.5 = (bf16[1024,256]{1,0:T(8,128)(2,1)S(1)}, bf16[1024,256]{1,0:T(8,128)(2,1)}, u32[]{:S(2)}) copy-start(bf16[1024,256]{1,0:T(8,128)(2,1)} %get-tuple-element.95.relay_ref) | copy-start | bytes 1572868
  30.0 23.5 %copy-start.6 = (bf16[256,768]{1,0:T(8,128)(2,1)S(1)}, bf16[256,768]{1,0:T(8,128)(2,1)}, u32[]{:S(2)}) copy-start(bf16[256,768]{1,0:T(8,128)(2,1)} %get-tuple-element.92.high_ref) | copy-start | bytes 1179652
  30.0 23.5 %copy-start.7 = (bf16[256,768]{1,0:T(8,128)(2,1)S(1)}, bf16[256,768]{1,0:T(8,128)(2,1)}, u32[]{:S(2)}) copy-start(bf16[256,768]{1,0:T(8,128)(2,1)} %get-tuple-element.93.low_ref) | copy-start | bytes 1179652
  39.4 22.7 %copy-start.10 = (bf16[512]{0:T(512)(128)(2,1)S(1)}, bf16[512]{0:T(512)(128)(2,1)}, u32[]{:S(2)}) copy-start(bf16[512]{0:T(512)(128)(2,1)} %param.22) | copy-start | bytes 3076
  39.4 32.0 %copy-start.9 = (f32[512]{0:T(512)S(1)}, f32[512]{0:T(512)}, u32[]{:S(2)}) copy-start(f32[512]{0:T(512)} %param.23) | copy-start | bytes 6148
  39.4 4.6 %collective-permute-start.7 = (bf16[2,48,512]{2,1,0:T(8,128)(2,1)}, bf16[2,48,512]{2,1,0:T(8,128)(2,1)S(1)}, u32[]{:S(2)}, u32[]{:S(2)}) collective-permute-start(bf16[2,48,512]{2,1,0:T(8,128)(2,1)} %get-tuple-element.106), channel_id=1, source_target_pairs={{0,1},{1,0},{2,3},{3,2},{4,5},{5,4},{6,7},{7,6},{8,9},{9,8},{10,11... | collective-permute-start | bytes 294920 | tf_op jit(solution)/shard_map/ppermute | solution.py:404
  40.1 5.4 %collective-permute-start.8 = (bf16[2,48,512]{2,1,0:T(8,128)(2,1)}, bf16[2,48,512]{2,1,0:T(8,128)(2,1)S(1)}, u32[]{:S(2)}, u32[]{:S(2)}) collective-permute-start(bf16[2,48,512]{2,1,0:T(8,128)(2,1)} %get-tuple-element.107), channel_id=1, source_target_pairs={{0,2},{1,3},{2,0},{3,1},{4,6},{5,7},{6,4},{7,5},{8,10},{9,11},{10,... | collective-permute-start | bytes 294920 | tf_op jit(solution)/shard_map/ppermute | solution.py:404
  41.8 5.3 %collective-permute-start.9 = (bf16[2,48,512]{2,1,0:T(8,128)(2,1)}, bf16[2,48,512]{2,1,0:T(8,128)(2,1)S(1)}, u32[]{:S(2)}, u32[]{:S(2)}) collective-permute-start(bf16[2,48,512]{2,1,0:T(8,128)(2,1)} %get-tuple-element.108), channel_id=1, source_target_pairs={{0,3},{1,2},{2,1},{3,0},{4,7},{5,6},{6,5},{7,4},{8,11},{9,10},{10,... | collective-permute-start | bytes 294920 | tf_op jit(solution)/shard_map/ppermute | solution.py:404
  41.9 5.9 %collective-permute-start.10 = (bf16[2,48,512]{2,1,0:T(8,128)(2,1)}, bf16[2,48,512]{2,1,0:T(8,128)(2,1)S(1)}, u32[]{:S(2)}, u32[]{:S(2)}) collective-permute-start(bf16[2,48,512]{2,1,0:T(8,128)(2,1)} %get-tuple-element.109), channel_id=1, source_target_pairs={{0,4},{1,5},{2,6},{3,7},{4,0},{5,1},{6,2},{7,3},{8,12},{9,13},{10,... | collective-permute-start | bytes 294920 | tf_op jit(solution)/shard_map/ppermute | solution.py:404
  42.5 11.0 %collective-permute-start.11 = (bf16[2,48,512]{2,1,0:T(8,128)(2,1)}, bf16[2,48,512]{2,1,0:T(8,128)(2,1)S(1)}, u32[]{:S(2)}, u32[]{:S(2)}) collective-permute-start(bf16[2,48,512]{2,1,0:T(8,128)(2,1)} %get-tuple-element.110), channel_id=1, source_target_pairs={{0,5},{1,4},{2,7},{3,6},{4,1},{5,0},{6,3},{7,2},{8,13},{9,12},{10,... | collective-permute-start | bytes 294920 | tf_op jit(solution)/shard_map/ppermute | solution.py:404
  43.9 9.6 %collective-permute-start.12 = (bf16[2,48,512]{2,1,0:T(8,128)(2,1)}, bf16[2,48,512]{2,1,0:T(8,128)(2,1)S(1)}, u32[]{:S(2)}, u32[]{:S(2)}) collective-permute-start(bf16[2,48,512]{2,1,0:T(8,128)(2,1)} %get-tuple-element.111), channel_id=1, source_target_pairs={{0,6},{1,7},{2,4},{3,5},{4,2},{5,3},{6,0},{7,1},{8,14},{9,15},{10,... | collective-permute-start | bytes 294920 | tf_op jit(solution)/shard_map/ppermute | solution.py:404
  45.4 8.1 %collective-permute-start.13 = (bf16[2,48,512]{2,1,0:T(8,128)(2,1)}, bf16[2,48,512]{2,1,0:T(8,128)(2,1)S(1)}, u32[]{:S(2)}, u32[]{:S(2)}) collective-permute-start(bf16[2,48,512]{2,1,0:T(8,128)(2,1)} %get-tuple-element.112), channel_id=1, source_target_pairs={{0,7},{1,6},{2,5},{3,4},{4,3},{5,2},{6,1},{7,0},{8,15},{9,14},{10,... | collective-permute-start | bytes 294920 | tf_op jit(solution)/shard_map/ppermute | solution.py:404
  53.6 0.9 copy-start.8
  55.4 3.9 %collective-permute-start.14 = (bf16[128,512]{1,0:T(8,128)(2,1)S(1)}, bf16[128,512]{1,0:T(8,128)(2,1)S(1)}, u32[]{:S(2)}, u32[]{:S(2)}) collective-permute-start(bf16[128,512]{1,0:T(8,128)(2,1)S(1)} %get-tuple-element.114), channel_id=1, source_target_pairs={{0,1},{1,0},{2,3},{3,2},{4,5},{5,4},{6,7},{7,6},{8,9},{9,8},{10,11... | collective-permute-start | bytes 393224 | tf_op jit(solution)/shard_map/ppermute | solution.py:404
  55.6 6.3 %collective-permute-start.15 = (bf16[128,512]{1,0:T(8,128)(2,1)S(1)}, bf16[128,512]{1,0:T(8,128)(2,1)S(1)}, u32[]{:S(2)}, u32[]{:S(2)}) collective-permute-start(bf16[128,512]{1,0:T(8,128)(2,1)S(1)} %get-tuple-element.115), channel_id=1, source_target_pairs={{0,2},{1,3},{2,0},{3,1},{4,6},{5,7},{6,4},{7,5},{8,10},{9,11},{10,... | collective-permute-start | bytes 393224 | tf_op jit(solution)/shard_map/ppermute | solution.py:404
  57.2 6.5 %collective-permute-start.16 = (bf16[128,512]{1,0:T(8,128)(2,1)S(1)}, bf16[128,512]{1,0:T(8,128)(2,1)S(1)}, u32[]{:S(2)}, u32[]{:S(2)}) collective-permute-start(bf16[128,512]{1,0:T(8,128)(2,1)S(1)} %get-tuple-element.116), channel_id=1, source_target_pairs={{0,3},{1,2},{2,1},{3,0},{4,7},{5,6},{6,5},{7,4},{8,11},{9,10},{10,... | collective-permute-start | bytes 393224 | tf_op jit(solution)/shard_map/ppermute | solution.py:404
  57.5 6.8 %collective-permute-start.17 = (bf16[128,512]{1,0:T(8,128)(2,1)S(1)}, bf16[128,512]{1,0:T(8,128)(2,1)S(1)}, u32[]{:S(2)}, u32[]{:S(2)}) collective-permute-start(bf16[128,512]{1,0:T(8,128)(2,1)S(1)} %get-tuple-element.117), channel_id=1, source_target_pairs={{0,4},{1,5},{2,6},{3,7},{4,0},{5,1},{6,2},{7,3},{8,12},{9,13},{10,... | collective-permute-start | bytes 393224 | tf_op jit(solution)/shard_map/ppermute | solution.py:404
  58.0 13.4 %collective-permute-start.18 = (bf16[128,512]{1,0:T(8,128)(2,1)S(1)}, bf16[128,512]{1,0:T(8,128)(2,1)S(1)}, u32[]{:S(2)}, u32[]{:S(2)}) collective-permute-start(bf16[128,512]{1,0:T(8,128)(2,1)S(1)} %get-tuple-element.118), channel_id=1, source_target_pairs={{0,5},{1,4},{2,7},{3,6},{4,1},{5,0},{6,3},{7,2},{8,13},{9,12},{10,... | collective-permute-start | bytes 393224 | tf_op jit(solution)/shard_map/ppermute | solution.py:404
  59.3 12.0 %collective-permute-start.19 = (bf16[128,512]{1,0:T(8,128)(2,1)S(1)}, bf16[128,512]{1,0:T(8,128)(2,1)S(1)}, u32[]{:S(2)}, u32[]{:S(2)}) collective-permute-start(bf16[128,512]{1,0:T(8,128)(2,1)S(1)} %get-tuple-element.119), channel_id=1, source_target_pairs={{0,6},{1,7},{2,4},{3,5},{4,2},{5,3},{6,0},{7,1},{8,14},{9,15},{10,... | collective-permute-start | bytes 393224 | tf_op jit(solution)/shard_map/ppermute | solution.py:404
  62.0 9.4 %collective-permute-start.20 = (bf16[128,512]{1,0:T(8,128)(2,1)S(1)}, bf16[128,512]{1,0:T(8,128)(2,1)S(1)}, u32[]{:S(2)}, u32[]{:S(2)}) collective-permute-start(bf16[128,512]{1,0:T(8,128)(2,1)S(1)} %get-tuple-element.120), channel_id=1, source_target_pairs={{0,7},{1,6},{2,5},{3,4},{4,3},{5,2},{6,1},{7,0},{8,15},{9,14},{10,... | collective-permute-start | bytes 393224 | tf_op jit(solution)/shard_map/ppermute | solution.py:404
  71.4 17.8 %copy-start = (bf16[512,1536]{1,0:T(8,128)(2,1)S(1)}, bf16[512,1536]{1,0:T(8,128)(2,1)}, u32[]{:S(2)}) copy-start(bf16[512,1536]{1,0:T(8,128)(2,1)} %wqkv_ref.3) | copy-start | bytes 4718596
  73.2 11.3 %collective-permute-start.22 = (bf16[8,16,512]{2,1,0:T(8,128)(2,1)S(1)}, bf16[8,16,512]{2,1,0:T(8,128)(2,1)S(1)}, u32[]{:S(2)}, u32[]{:S(2)}) collective-permute-start(bf16[8,16,512]{2,1,0:T(8,128)(2,1)S(1)} %get-tuple-element.122), channel_id=1, source_target_pairs={{0,1},{1,2},{2,3},{3,4},{4,5},{5,6},{6,7},{8,9},{9,10},{10,11},{11... | collective-permute-start | bytes 393224 | tf_op jit(solution)/shard_map/ppermute | solution.py:479
  75.4 9.1 %collective-permute-start.23 = (bf16[8,16,512]{2,1,0:T(8,128)(2,1)S(1)}, bf16[8,16,512]{2,1,0:T(8,128)(2,1)S(1)}, u32[]{:S(2)}, u32[]{:S(2)}) collective-permute-start(bf16[8,16,512]{2,1,0:T(8,128)(2,1)S(1)} %get-tuple-element.123), channel_id=1, source_target_pairs={{1,0},{2,1},{3,2},{4,3},{5,4},{6,5},{7,6},{9,8},{10,9},{11,10},{12... | collective-permute-start | bytes 393224 | tf_op jit(solution)/shard_map/ppermute | solution.py:480
  79.7 19.2 %collective-permute-start.21 = (bf16[3,128,512]{2,1,0:T(8,128)(2,1)S(1)}, bf16[3,128,512]{2,1,0:T(8,128)(2,1)S(1)}, u32[]{:S(2)}, u32[]{:S(2)}) collective-permute-start(bf16[3,128,512]{2,1,0:T(8,128)(2,1)S(1)} %get-tuple-element.121), channel_id=1, source_target_pairs={{0,8},{8,16},{16,24},{1,9},{9,17},{17,25},{2,10},{10,18},{18,26},{... | collective-permute-start | bytes 1179656 | tf_op jit(solution)/shard_map/ppermute | solution.py:477
  83.2 15.7 %collective-permute-start.25 = (bf16[3,128,512]{2,1,0:T(8,128)(2,1)S(1)}, bf16[3,128,512]{2,1,0:T(8,128)(2,1)S(1)}, u32[]{:S(2)}, u32[]{:S(2)}) collective-permute-start(bf16[3,128,512]{2,1,0:T(8,128)(2,1)S(1)} %get-tuple-element.124), channel_id=1, source_target_pairs={{8,0},{16,8},{24,16},{9,1},{17,9},{25,17},{10,2},{18,10},{26,18},{... | collective-permute-start | bytes 1179656 | tf_op jit(solution)/shard_map/ppermute | solution.py:478
  84.6 11.5 %collective-permute-start.26 = (bf16[3,16,512]{2,1,0:T(8,128)(2,1)S(1)}, bf16[3,16,512]{2,1,0:T(8,128)(2,1)S(1)}, u32[]{:S(2)}, u32[]{:S(2)}) collective-permute-start(bf16[3,16,512]{2,1,0:T(8,128)(2,1)S(1)} %get-tuple-element.131), channel_id=1, source_target_pairs={{8,0},{16,8},{24,16},{0,24},{9,1},{17,9},{25,17},{1,25},{10,2},{18... | collective-permute-start | bytes 147464 | tf_op jit(solution)/shard_map/ppermute | solution.py:483
  89.1 9.8 %collective-permute-start.24 = (bf16[3,16,512]{2,1,0:T(8,128)(2,1)S(1)}, bf16[3,16,512]{2,1,0:T(8,128)(2,1)S(1)}, u32[]{:S(2)}, u32[]{:S(2)}) collective-permute-start(bf16[3,16,512]{2,1,0:T(8,128)(2,1)S(1)} %get-tuple-element.132), channel_id=1, source_target_pairs={{0,8},{8,16},{16,24},{24,0},{1,9},{9,17},{17,25},{25,1},{2,10},{10... | collective-permute-start | bytes 147464 | tf_op jit(solution)/shard_map/ppermute | solution.py:482
  89.2 9.8 %copy-start.1 = (bf16[8,128,768]{2,1,0:T(8,128)(2,1)S(1)}, bf16[8,128,768]{2,1,0:T(8,128)(2,1)}, u32[]{:S(2)}) copy-start(bf16[8,128,768]{2,1,0:T(8,128)(2,1)} %pixels_ref.1) | copy-start | bytes 4718596
  89.2 9.8 %copy-start.2 = (bf16[512,768]{1,0:T(8,128)(2,1)S(1)}, bf16[512,768]{1,0:T(8,128)(2,1)}, u32[]{:S(2)}) copy-start(bf16[512,768]{1,0:T(8,128)(2,1)} %whead_ref.1) | copy-start | bytes 2359300
  89.2 9.8 %copy-start.3 = (bf16[512,512]{1,0:T(8,128)(2,1)S(1)}, bf16[512,512]{1,0:T(8,128)(2,1)}, u32[]{:S(2)}) copy-start(bf16[512,512]{1,0:T(8,128)(2,1)} %wout_ref.1) | copy-start | bytes 1572868
where the time goes:
time: 115 us
  Pallas kernels  48.7 us (42%)
  starting transfers between devices  38.2 us (33%)
  waiting for transfers between devices  24.9 us (22%)
  local copies, waits for them, and re-layouts  1.67 us (1%)
    pallas_call x6, Pallas kernels, whole_call(): pl.pallas_call(kernel, out_shape=tuple(outs), in_specs=[VM] * len(ins), o...  32.7 us
    ppermute x21, waiting for transfers between devices, swap(): lax.ppermute(value, 'expert', [(i, i ^ k) for i in range(groups)])  22 us
    ppermute x21, starting transfers between devices, swap(): lax.ppermute(value, 'expert', [(i, i ^ k) for i in range(groups)])  18 us
    pallas_call x1, Pallas kernels, experts_apply(): pl.pallas_call(functools.partial(ffn_kernel, sources), grid=(local_expert...  9.31 us
    pallas_call x1, Pallas kernels, fold(): pl.pallas_call(fold_kernel, grid=(local_experts, hidden // chunk), out_sh...  6.67 us
    ppermute x1, starting transfers between devices, local(): lax.ppermute(sides[:RAD], 'dp', [((i + 1) % bands, i) for i in range(band...  4.56 us
    all_to_all x1, starting transfers between devices, local(): lax.all_to_all(spots, 'expert', split_axis=0, concat_axis=0, tiled=True)  4.34 us
    ppermute x1, starting transfers between devices, local(): lax.ppermute(first, 'expert', [(i + 1, i) for i in range(groups - 1)])  4.25 us
  transfers between devices with their start and end apart: 28, of which 10 were waited for; matrix products, arithmetic and copies ran while one was open for 0% of the time, Pallas kernels for 15%

commit v1 on v0

--- a/solution.py
+++ b/solution.py
@@ -198,12 +198,12 @@
 WIDE_ROOM = 56 * 2**20
 
 
-def whole_call(kernel, outs, ins, name, flops, scratch=(), room=ROOM):
+def whole_call(kernel, outs, ins, name, flops, scratch=(), room=ROOM, last=VM):
     size = sum(math.prod(a.shape) * a.dtype.itemsize for a in tuple(outs) + tuple(ins))
     return pl.pallas_call(
         kernel,
         out_shape=tuple(outs),
-        in_specs=[VM] * len(ins),
+        in_specs=[VM] * (len(ins) - 1) + [last],
         out_specs=tuple([VM] * len(outs)),
         scratch_shapes=list(scratch),
         compiler_params=pltpu.CompilerParams(vmem_limit_bytes=room),
@@ -266,17 +266,20 @@
     band_row = lax.axis_index("dp")
     owner = lax.axis_index("expert")
 
-    def column(j, carry):
-        c0 = pl.multiple_of(j * STRIP, STRIP)
+    near = {}
+    for count, q_row, k_row in starts:
+        qi, ki = iota((count * STRIP, keys), 0), iota((count * STRIP, keys), 1)
+        down = ki // SPAN + first_row + k_row - q_row - qi // STRIP
+        across = ki % SPAN - qi % STRIP
+        ok = (down >= -RAD) & (down <= RAD) & (across >= 0) & (across <= 2 * RAD)
+        near[count, k_row - q_row] = ok, ki // SPAN, ki % SPAN
+    for j in range(tile_w // STRIP):
+        c0 = j * STRIP
         for count, q_row, k_row in starts:
             items = count * STRIP
-            qi, ki = iota((items, keys), 0), iota((items, keys), 1)
-            key_row = first_row + k_row + ki // SPAN
-            down = key_row - q_row - qi // STRIP
-            across = ki % SPAN - qi % STRIP
-            grid_row = band_row * tile_h + key_row
-            grid_col = owner * tile_w + j * STRIP - RAD + ki % SPAN
-            ok = (down >= -RAD) & (down <= RAD) & (across >= 0) & (across <= 2 * RAD)
+            ok, key_row, key_col = near[count, k_row - q_row]
+            grid_row = band_row * tile_h + first_row + k_row + key_row
+            grid_col = owner * tile_w + j * STRIP - RAD + key_col
             ok = ok & (grid_row >= 0) & (grid_row < grid_h) & (grid_col >= 0) & (grid_col < grid_w)
             bias = jnp.where(ok, 0.0, -1e30)
             for g in range(width // lanes):
@@ -298,19 +301,42 @@
                 att_ref[q_row : q_row + count, pl.ds(c0, STRIP), part] = out.astype(jnp.bfloat16).reshape(
                     count, STRIP, lanes
                 )
-        return carry
-
-    lax.fori_loop(0, tile_w // STRIP, column, 0)
 
 
 def row_groups(rows):
     return [(min(2, rows.stop - r), r) for r in range(rows.start, rows.stop, 2)]
 
 
-def inner_kernel(grid_h, grid_w, normed_ref, before_ref, after_ref, wqkv_ref, q_ref, kv_ref, att_ref):
+def finish(rows, att_ref, dec_in_ref, keep_ref, pixels_ref, wout_ref, whead_ref, decoded_ref, dattn_ref, offset):
+    breadth, width = att_ref.shape[1:]
+    pd = pixels_ref.shape[2]
+    bf16 = jnp.bfloat16
+    lines = rows.stop - rows.start
+    count = lines * breadth
+    held = slice(rows.start - offset, rows.stop - offset)
+    att = att_ref[rows].reshape(count, width)
+    decoded = (dec_in_ref[rows].reshape(count, width) + dot(att, wout_ref[...])).astype(bf16)
+    decoded_ref[held] = decoded.reshape(lines, breadth, width)
+    pred = dot(decoded, whead_ref[...])
+    pix = pixels_ref[held].reshape(count, pd).astype(jnp.float32)
+    centred = pix - jnp.sum(pix, axis=1, keepdims=True) * (1.0 / pd)
+    spread = jnp.sum(centred * centred, axis=1, keepdims=True) * (1.0 / pd)
+    error = (pred - centred * lax.rsqrt(spread + EPSILON)) * (1.0 - keep_ref[rows].reshape(count, 1))
+    back = dot(error.astype(bf16), whead_ref[...], ((1,), (1,))).astype(bf16)
+    dattn_ref[held] = dot(back, wout_ref[...], ((1,), (1,))).astype(bf16).reshape(lines, breadth, width)
+    return jnp.sum(jnp.sum(error * error, axis=1, keepdims=True), axis=0, keepdims=True)
+
+
+def inner_kernel(
+    grid_h, grid_w, normed_ref, before_ref, after_ref, dec_in_ref, keep_ref, wqkv_ref, wout_ref, whead_ref, pixels_ref,
+    q_ref, kv_ref, decoded_ref, dattn_ref, loss_ref, att_ref, held_ref, sem,
+):
     height, breadth, width = normed_ref.shape
     cols = kv_ref.shape[1]
     edge = before_ref.shape[1]
+    inner = slice(RAD, height - RAD)
+    copy = pltpu.make_async_copy(pixels_ref.at[inner], held_ref, sem)
+    copy.start()
     shift = shift_matrix(
         cols, breadth + 2 * edge, ((RAD, breadth, 0), (0, RAD, breadth + edge - RAD), (RAD + breadth, RAD, breadth + edge))
     )
@@ -322,49 +348,42 @@
     kv_ref[...] = dot(wide, wqkv_ref[:, width:]).astype(jnp.bfloat16).reshape(kv_ref.shape)
     flat = normed_ref[...].reshape(height * breadth, width)
     q_ref[...] = dot(flat, wqkv_ref[:, :width]).astype(jnp.bfloat16).reshape(q_ref.shape)
-    starts = [(n, r, r - RAD) for n, r in row_groups(slice(RAD, height - RAD))]
+    starts = [(n, r, r - RAD) for n, r in row_groups(inner)]
     attention(q_ref, kv_ref, att_ref, starts, 0, grid_h, grid_w, height, breadth)
+    copy.wait()
+    loss_ref[...] = finish(
+        inner, att_ref, dec_in_ref, keep_ref, held_ref, wout_ref, whead_ref, decoded_ref, dattn_ref, RAD
+    )
 
 
 def outer_kernel(
-    grid_h, grid_w, up_ref, up_edge_ref, down_ref, down_edge_ref, q_ref, kv_in_ref, att_in_ref, dec_in_ref, keep_ref,
-    pixels_ref, wqkv_ref, wout_ref, whead_ref, decoded_ref, dattn_ref, loss_ref, kv_ref, att_ref,
+    grid_h, grid_w, up_ref, down_ref, q_ref, kv_in_ref, decoded_in_ref, dattn_in_ref, loss_in_ref,
+    dec_in_ref, keep_ref, pixels_ref, wqkv_ref, wout_ref, whead_ref, decoded_ref, dattn_ref, loss_ref, kv_ref, att_ref,
 ):
     height, breadth, pd = pixels_ref.shape
     width = q_ref.shape[2]
     cols = kv_ref.shape[1]
-    edge = up_edge_ref.shape[1]
+    edge = up_ref.shape[1] - breadth
     middle = edge // 2
     bf16 = jnp.bfloat16
     shift = shift_matrix(
         cols, breadth + edge, ((RAD, breadth, 0), (0, RAD, breadth + middle - RAD), (RAD + breadth, RAD, breadth + middle))
     )
     kv_ref[RAD : RAD + height] = kv_in_ref[...]
-    for main, side, start in ((up_ref, up_edge_ref, 0), (down_ref, down_edge_ref, RAD + height)):
-        wide = [dot(shift, jnp.concatenate([main[r], side[r]], 0)).astype(bf16) for r in range(RAD)]
+    for rim_ref, start in ((up_ref, 0), (down_ref, RAD + height)):
+        wide = [dot(shift, rim_ref[r]).astype(bf16) for r in range(RAD)]
         kv = dot(jnp.concatenate(wide, 0), wqkv_ref[:, width:]).astype(bf16)
         kv_ref[start : start + RAD] = kv.reshape(RAD, cols, 2 * width)
     inner = slice(RAD, height - RAD)
-    att_ref[inner] = att_in_ref[inner]
-    starts = [(n, r, r) for n, r in row_groups(slice(0, RAD))]
-    starts += [(n, r, min(r, height + 2 * RAD - 2 - 2 * RAD)) for n, r in row_groups(slice(height - RAD, height))]
+    decoded_ref[inner] = decoded_in_ref[...]
+    dattn_ref[inner] = dattn_in_ref[...]
+    starts = [(2, r, r) for r in range(0, height, 2)]
     attention(q_ref, kv_ref, att_ref, starts, -RAD, grid_h, grid_w, height, breadth)
-    loss = jnp.zeros((1, 1), jnp.float32)
-    step = height // 2
-    for r in range(0, height, step):
-        rows = slice(r, r + step)
-        count = step * breadth
-        att = att_ref[rows].reshape(count, width)
-        decoded = (dec_in_ref[rows].reshape(count, width) + dot(att, wout_ref[...])).astype(bf16)
-        decoded_ref[rows] = decoded.reshape(step, breadth, width)
-        pred = dot(decoded, whead_ref[...])
-        pix = pixels_ref[rows].reshape(count, pd).astype(jnp.float32)
-        centred = pix - jnp.sum(pix, axis=1, keepdims=True) * (1.0 / pd)
-        spread = jnp.sum(centred * centred, axis=1, keepdims=True) * (1.0 / pd)
-        error = (pred - centred * lax.rsqrt(spread + EPSILON)) * (1.0 - keep_ref[rows].reshape(count, 1))
-        loss = loss + jnp.sum(jnp.sum(error * error, axis=1, keepdims=True), axis=0, keepdims=True)
-        back = dot(error.astype(bf16), whead_ref[...], ((1,), (1,))).astype(bf16)
-        dattn_ref[rows] = dot(back, wout_ref[...], ((1,), (1,))).astype(bf16).reshape(step, breadth, width)
+    loss = loss_in_ref[...]
+    for rows in (slice(0, RAD), slice(height - RAD, height)):
+        loss = loss + finish(
+            rows, att_ref, dec_in_ref, keep_ref, pixels_ref, wout_ref, whead_ref, decoded_ref, dattn_ref, 0
+        )
     loss_ref[...] = loss * (0.5 / (height * breadth * pd))
 
 
@@ -474,32 +493,42 @@
     bands = lax.axis_size("dp")
     upward = [(i + 1, i) for i in range(bands - 1)]
     downward = [(i, i + 1) for i in range(bands - 1)]
-    above = lax.ppermute(bottom, "dp", downward)
-    below = lax.ppermute(top, "dp", upward)
     before = lax.ppermute(last, "expert", [(i, i + 1) for i in range(groups - 1)])
     after = lax.ppermute(first, "expert", [(i + 1, i) for i in range(groups - 1)])
     sides = jnp.concatenate([before[:, edge // 2 :], after[:, : edge // 2]], 1)
-    above_edge = lax.ppermute(sides[tile_height - RAD :], "dp", [(i, (i + 1) % bands) for i in range(bands)])
-    below_edge = lax.ppermute(sides[:RAD], "dp", [((i + 1) % bands, i) for i in range(bands)])
+    bottom = jnp.concatenate([bottom, sides[tile_height - RAD :]], 1)
+    top = jnp.concatenate([top, sides[:RAD]], 1)
+    above = lax.ppermute(bottom, "dp", downward)
+    below = lax.ppermute(top, "dp", upward)
     grid_height = tile_height * bands
     grid_width = tile_width * groups
     cols = -(-(tile_width - STRIP + SPAN) // 16) * 16
-    queries, kv, attended = whole_call(
+    inner_shape = (tile_height - 2 * RAD, tile_width, dec_width)
+    queries, kv, decoded_inner, d_attn_inner, loss_inner = whole_call(
         functools.partial(inner_kernel, grid_height, grid_width),
         [
             shaped(grid_shape, bf16),
             shaped((tile_height, cols, 2 * dec_width), bf16),
-            shaped(grid_shape, bf16),
+            shaped(inner_shape, bf16),
+            shaped(inner_shape, bf16),
+            shaped((1, 1), jnp.float32),
         ],
-        [normed, before, after, w_qkv],
+        [normed, before, after, decoder_in, keep, w_qkv, w_out, w_head, pixels],
         "inner",
-        6 * tile_size * dec_width * dec_width,
+        10 * tile_size * dec_width * dec_width,
+        [
+            pltpu.VMEM(grid_shape, bf16),
+            pltpu.VMEM((tile_height - 2 * RAD, tile_width, PD), bf16),
+            pltpu.SemaphoreType.DMA(()),
+        ],
         room=INNER_ROOM,
+        last=pl.BlockSpec(memory_space=pl.ANY),
     )
     return whole_call(
         functools.partial(outer_kernel, grid_height, grid_width),
         [shaped(grid_shape, bf16), shaped(grid_shape, bf16), shaped((1, 1), jnp.float32)],
-        [above, above_edge, below, below_edge, queries, kv, attended, decoder_in, keep, pixels, w_qkv, w_out, w_head],
+        [above, below, queries, kv, decoded_inner, d_attn_inner, loss_inner]
+        + [decoder_in, keep, pixels, w_qkv, w_out, w_head],
         "outer",
         12 * tile_size * dec_width * dec_width,
         [

time: 115 us -> 110 us (0.957)
  the two profiles are of different devices: /device:TPU:4 before, /device:TPU:13 now
where the time goes in v1:
time: 110 us
  Pallas kernels  41.7 us (38%)
  starting transfers between devices  36.5 us (33%)
  waiting for transfers between devices  28.3 us (26%)
  local copies, waits for them, and re-layouts  1.69 us (2%)
    pallas_call x6, Pallas kernels, whole_call(): pl.pallas_call(kernel, out_shape=tuple(outs), in_specs=[VM] * (len(ins) -...  25.7 us
    ppermute x21, starting transfers between devices, swap(): lax.ppermute(value, 'expert', [(i, i ^ k) for i in range(groups)])  22 us
    ppermute x21, waiting for transfers between devices, swap(): lax.ppermute(value, 'expert', [(i, i ^ k) for i in range(groups)])  18.7 us
    pallas_call x1, Pallas kernels, experts_apply(): pl.pallas_call(functools.partial(ffn_kernel, sources), grid=(local_expert...  9.32 us
    pallas_call x1, Pallas kernels, fold(): pl.pallas_call(fold_kernel, grid=(local_experts, hidden // chunk), out_sh...  6.67 us
    ppermute x1, waiting for transfers between devices, local(): lax.ppermute(first, 'expert', [(i + 1, i) for i in range(groups - 1)])  4.33 us
    all_to_all x1, starting transfers between devices, local(): lax.all_to_all(spots, 'expert', split_axis=0, concat_axis=0, tiled=True)  3.98 us
    ppermute x1, waiting for transfers between devices, local(): below = lax.ppermute(top, 'dp', upward)  3.42 us
  transfers between devices with their start and end apart: 26, of which 8 were waited for; matrix products, arithmetic and copies ran while one was open for 0% of the time, Pallas kernels for 14%

profile of v1, /device:TPU:13, one launch (start us, length us, event | category | flops | bytes accessed | tf_op | source)
XLA Modules:
  0.0 109.6 jit_solution(7866588619431920895)
XLA Ops:
  0.6 3.3 %pack.1 = (bf16[2,48,1280]{2,1,0:T(8,128)(2,1)}, bf16[2,48,1280]{2,1,0:T(8,128)(2,1)}, bf16[2,48,1280]{2,1,0:T(8,128)(2,1)}, bf16[2,48,1280]{2,1,0:T(8,128)(2,1)...) custom-call(s32[2,256]{1,0:T(2,128)} %bitcast.12, ...), custom_call_target="tpu_custom_call" | custom-call | flops 503316480 | bytes 2623488 | tf_op jit(solution)/shard_map/pack/pallas_call | solution.py:203
  4.0 0.7 collective-permute-start
  4.7 1.2 %collective-permute-start.1 = (bf16[2,48,1280]{2,1,0:T(8,128)(2,1)}, bf16[2,48,1280]{2,1,0:T(8,128)(2,1)S(1)}, u32[]{:S(2)}, u32[]{:S(2)}) collective-permute-start(bf16[2,48,1280]{2,1,0:T(8,128)(2,1)} %get-tuple-element.79), channel_id=1, source_target_pairs={{0,2},{1,3},{2,0},{3,1},{4,6},{5,7},{6,4},{7,5},{8,10},{9,11},{10,... | collective-permute-start | bytes 737288 | tf_op jit(solution)/shard_map/ppermute | solution.py:423
  5.9 0.4 collective-permute-start.2
  6.3 0.2 collective-permute-start.3
  6.5 1.6 %collective-permute-start.4 = (bf16[2,48,1280]{2,1,0:T(8,128)(2,1)}, bf16[2,48,1280]{2,1,0:T(8,128)(2,1)S(1)}, u32[]{:S(2)}, u32[]{:S(2)}) collective-permute-start(bf16[2,48,1280]{2,1,0:T(8,128)(2,1)} %get-tuple-element.82), channel_id=1, source_target_pairs={{0,5},{1,4},{2,7},{3,6},{4,1},{5,0},{6,3},{7,2},{8,13},{9,12},{10,... | collective-permute-start | bytes 737288 | tf_op jit(solution)/shard_map/ppermute | solution.py:423
  8.1 3.8 %prep.1 = (bf16[256,768]{1,0:T(8,128)(2,1)}, bf16[256,768]{1,0:T(8,128)(2,1)}, f32[256,512]{1,0:T(8,128)}, bf16[1024,256]{1,0:T(8,128)(2,1)}, s32[8,128]{1,0:T(8,128)}) custom-call(s32[2,256]{1,0:T(2,128)} %bitcast.13, f32[2,256]{1,0:T(2,128)} %bitcast.14, s32[1,256]{1,0:T(1,128)} %bitcast.15, bf16[256,1280]{1,0:T(8,128)(2,1)} %tokens_ref.2, ...), custom_call_target="tpu_custom_call" | custom-call | flops 335544320 | bytes 3810304 | tf_op jit(solution)/shard_map/prep/pallas_call | solution.py:203
  12.0 4.0 %all-to-all-start = ((s32[8,1,128]{2,1,0:T(1,128)}), s32[8,1,128]{2,1,0:T(1,128)S(1)}, u32[]{:S(2)}, u32[]{:S(2)}) async-start(s32[8,1,128]{2,1,0:T(1,128)} %bitcast.11), calls=%async_computation | async-start | bytes 8192 | tf_op jit(solution)/shard_map/all_to_all | solution.py:457
  16.0 1.2 %collective-permute-start.5 = (bf16[2,48,1280]{2,1,0:T(8,128)(2,1)}, bf16[2,48,1280]{2,1,0:T(8,128)(2,1)S(1)}, u32[]{:S(2)}, u32[]{:S(2)}) collective-permute-start(bf16[2,48,1280]{2,1,0:T(8,128)(2,1)} %get-tuple-element.83), channel_id=1, source_target_pairs={{0,6},{1,7},{2,4},{3,5},{4,2},{5,3},{6,0},{7,1},{8,14},{9,15},{10,... | collective-permute-start | bytes 737288 | tf_op jit(solution)/shard_map/ppermute | solution.py:423
  17.2 1.7 %collective-permute-start.6 = (bf16[2,48,1280]{2,1,0:T(8,128)(2,1)}, bf16[2,48,1280]{2,1,0:T(8,128)(2,1)S(1)}, u32[]{:S(2)}, u32[]{:S(2)}) collective-permute-start(bf16[2,48,1280]{2,1,0:T(8,128)(2,1)} %get-tuple-element.84), channel_id=1, source_target_pairs={{0,7},{1,6},{2,5},{3,4},{4,3},{5,2},{6,1},{7,0},{8,15},{9,14},{10,... | collective-permute-start | bytes 737288 | tf_op jit(solution)/shard_map/ppermute | solution.py:423
  18.9 6.7 %fold.1.refs_10_ = bf16[2,1024,512]{2,1,0:T(8,128)(2,1)} custom-call(bf16[2,1024,1280]{2,1,0:T(8,128)(2,1)} %down_ref, bf16[1280,512]{1,0:T(8,128)(2,1)} %embed_ref.3), custom_call_target="tpu_custom_call" | custom-call | flops 2684354560 | bytes 5242880 | tf_op jit(solution)/shard_map/fold/pallas_call | solution.py:123
  25.7 4.4 %collective-permute-done.6.refs_7_ = bf16[2,48,1280]{2,1,0:T(8,128)(2,1)S(1)} collective-permute-done((bf16[2,48,1280]{2,1,0:T(8,128)(2,1)}, bf16[2,48,1280]{2,1,0:T(8,128)(2,1)S(1)}, u32[]{:S(2)}, u32[]{:S(2)}) %collective-permute-start.6) | collective-permute-done | bytes 245792 | tf_op jit(solution)/shard_map/ppermute | solution.py:423
  30.1 0.7 copy-done.17
  30.9 9.3 %experts.1 = (bf16[2,48,512]{2,1,0:T(8,128)(2,1)}, bf16[2,48,512]{2,1,0:T(8,128)(2,1)}, bf16[2,48,512]{2,1,0:T(8,128)(2,1)}, bf16[2,48,512]{2,1,0:T(8,128)(2,1)}...) custom-call(bf16[2,48,1280]{2,1,0:T(8,128)(2,1)} %get-tuple-element., ...), custom_call_target="tpu_custom_call" | custom-call | flops 4831838208 | bytes 12582912 | tf_op jit(solution)/shard_map/experts/pallas_call | solution.py:225
  40.2 0.0 copy-start.10
  40.2 0.1 collective-permute-start.7
  40.3 1.2 %collective-permute-start.8 = (bf16[2,48,512]{2,1,0:T(8,128)(2,1)}, bf16[2,48,512]{2,1,0:T(8,128)(2,1)S(1)}, u32[]{:S(2)}, u32[]{:S(2)}) collective-permute-start(bf16[2,48,512]{2,1,0:T(8,128)(2,1)} %get-tuple-element.109), channel_id=1, source_target_pairs={{0,2},{1,3},{2,0},{3,1},{4,6},{5,7},{6,4},{7,5},{8,10},{9,11},{10,... | collective-permute-start | bytes 294920 | tf_op jit(solution)/shard_map/ppermute | solution.py:423
  41.5 0.3 multiply_sine_fusion
  41.8 0.9 collective-permute-start.9
  42.8 0.2 collective-permute-start.10
  42.9 1.4 %collective-permute-start.11 = (bf16[2,48,512]{2,1,0:T(8,128)(2,1)}, bf16[2,48,512]{2,1,0:T(8,128)(2,1)S(1)}, u32[]{:S(2)}, u32[]{:S(2)}) collective-permute-start(bf16[2,48,512]{2,1,0:T(8,128)(2,1)} %get-tuple-element.112), channel_id=1, source_target_pairs={{0,5},{1,4},{2,7},{3,6},{4,1},{5,0},{6,3},{7,2},{8,13},{9,12},{10,... | collective-permute-start | bytes 294920 | tf_op jit(solution)/shard_map/ppermute | solution.py:423
  44.3 1.1 collective-permute-start.12
  45.4 2.3 %collective-permute-start.13 = (bf16[2,48,512]{2,1,0:T(8,128)(2,1)}, bf16[2,48,512]{2,1,0:T(8,128)(2,1)S(1)}, u32[]{:S(2)}, u32[]{:S(2)}) collective-permute-start(bf16[2,48,512]{2,1,0:T(8,128)(2,1)} %get-tuple-element.114), channel_id=1, source_target_pairs={{0,7},{1,6},{2,5},{3,4},{4,3},{5,2},{6,1},{7,0},{8,15},{9,14},{10,... | collective-permute-start | bytes 294920 | tf_op jit(solution)/shard_map/ppermute | solution.py:423
  47.7 6.1 %collective-permute-done.11.refs_5_ = bf16[2,48,512]{2,1,0:T(8,128)(2,1)S(1)} collective-permute-done((bf16[2,48,512]{2,1,0:T(8,128)(2,1)}, bf16[2,48,512]{2,1,0:T(8,128)(2,1)S(1)}, u32[]{:S(2)}, u32[]{:S(2)}) %collective-permute-start.11) | collective-permute-done | bytes 98336 | tf_op jit(solution)/shard_map/ppermute | solution.py:423
  53.9 0.9 copy-done.4
  54.8 1.0 combine.1
  55.8 0.5 collective-permute-start.14
  56.2 1.2 %collective-permute-start.15 = (bf16[128,512]{1,0:T(8,128)(2,1)S(1)}, bf16[128,512]{1,0:T(8,128)(2,1)S(1)}, u32[]{:S(2)}, u32[]{:S(2)}) collective-permute-start(bf16[128,512]{1,0:T(8,128)(2,1)S(1)} %get-tuple-element.117), channel_id=1, source_target_pairs={{0,2},{1,3},{2,0},{3,1},{4,6},{5,7},{6,4},{7,5},{8,10},{9,11},{10,... | collective-permute-start | bytes 393224 | tf_op jit(solution)/shard_map/ppermute | solution.py:423
  57.4 0.1 multiply_sine_fusion.1
  57.5 0.6 collective-permute-start.16
  58.1 0.2 collective-permute-start.17
  58.3 1.6 %collective-permute-start.18 = (bf16[128,512]{1,0:T(8,128)(2,1)S(1)}, bf16[128,512]{1,0:T(8,128)(2,1)S(1)}, u32[]{:S(2)}, u32[]{:S(2)}) collective-permute-start(bf16[128,512]{1,0:T(8,128)(2,1)S(1)} %get-tuple-element.120), channel_id=1, source_target_pairs={{0,5},{1,4},{2,7},{3,6},{4,1},{5,0},{6,3},{7,2},{8,13},{9,12},{10,... | collective-permute-start | bytes 393224 | tf_op jit(solution)/shard_map/ppermute | solution.py:423
  59.9 1.2 %collective-permute-start.19 = (bf16[128,512]{1,0:T(8,128)(2,1)S(1)}, bf16[128,512]{1,0:T(8,128)(2,1)S(1)}, u32[]{:S(2)}, u32[]{:S(2)}) collective-permute-start(bf16[128,512]{1,0:T(8,128)(2,1)S(1)} %get-tuple-element.121), channel_id=1, source_target_pairs={{0,6},{1,7},{2,4},{3,5},{4,2},{5,3},{6,0},{7,1},{8,14},{9,15},{10,... | collective-permute-start | bytes 393224 | tf_op jit(solution)/shard_map/ppermute | solution.py:423
  61.2 0.1 collective-permute-done.15.refs_2_
  61.3 2.4 %collective-permute-start.20 = (bf16[128,512]{1,0:T(8,128)(2,1)S(1)}, bf16[128,512]{1,0:T(8,128)(2,1)S(1)}, u32[]{:S(2)}, u32[]{:S(2)}) collective-permute-start(bf16[128,512]{1,0:T(8,128)(2,1)S(1)} %get-tuple-element.122), channel_id=1, source_target_pairs={{0,7},{1,6},{2,5},{3,4},{4,3},{5,2},{6,1},{7,0},{8,15},{9,14},{10,... | collective-permute-start | bytes 393224 | tf_op jit(solution)/shard_map/ppermute | solution.py:423
  63.8 1.3 %collective-permute-done.16.refs_3_ = bf16[128,512]{1,0:T(8,128)(2,1)S(1)} collective-permute-done((bf16[128,512]{1,0:T(8,128)(2,1)S(1)}, bf16[128,512]{1,0:T(8,128)(2,1)S(1)}, u32[]{:S(2)}, u32[]{:S(2)}) %collective-permute-start.16) | collective-permute-done | bytes 131104 | tf_op jit(solution)/shard_map/ppermute | solution.py:423
  65.0 6.7 %collective-permute-done.18.refs_5_ = bf16[128,512]{1,0:T(8,128)(2,1)S(1)} collective-permute-done((bf16[128,512]{1,0:T(8,128)(2,1)S(1)}, bf16[128,512]{1,0:T(8,128)(2,1)S(1)}, u32[]{:S(2)}, u32[]{:S(2)}) %collective-permute-start.18) | collective-permute-done | bytes 131104 | tf_op jit(solution)/shard_map/ppermute | solution.py:423
  71.8 1.8 %place.1 = (bf16[8,128,512]{2,1,0:T(8,128)(2,1)S(1)}, f32[8,128,512]{2,1,0:T(8,128)S(1)}, f32[8,128,1]{2,1,0:T(8,128)S(1)}, bf16[3,128,512]{2,1,0:T(8,128)(2,1)S...) custom-call(s32[8,128]{1,0:T(8,128)S(1)} %bitcast.9, ...), custom_call_target="tpu_custom_call" | custom-call | flops 1073741824 | bytes 5393408 | tf_op jit(solution)/shard_map/place/pallas_call | solution.py:203
  73.6 3.3 %collective-permute-start.21 = (bf16[8,16,512]{2,1,0:T(8,128)(2,1)S(1)}, bf16[8,16,512]{2,1,0:T(8,128)(2,1)S(1)}, u32[]{:S(2)}, u32[]{:S(2)}) collective-permute-start(bf16[8,16,512]{2,1,0:T(8,128)(2,1)S(1)} %get-tuple-element.124), channel_id=1, source_target_pairs={{0,1},{1,2},{2,3},{3,4},{4,5},{5,6},{6,7},{8,9},{9,10},{10,11},{11... | collective-permute-start | bytes 393224 | tf_op jit(solution)/shard_map/ppermute | solution.py:496
  76.9 1.9 %collective-permute-start.22 = (bf16[8,16,512]{2,1,0:T(8,128)(2,1)S(1)}, bf16[8,16,512]{2,1,0:T(8,128)(2,1)S(1)}, u32[]{:S(2)}, u32[]{:S(2)}) collective-permute-start(bf16[8,16,512]{2,1,0:T(8,128)(2,1)S(1)} %get-tuple-element.125), channel_id=1, source_target_pairs={{1,0},{2,1},{3,2},{4,3},{5,4},{6,5},{7,6},{9,8},{10,9},{11,10},{12... | collective-permute-start | bytes 393224 | tf_op jit(solution)/shard_map/ppermute | solution.py:497
  78.9 4.3 %collective-permute-done.22.after_ref = bf16[8,16,512]{2,1,0:T(8,128)(2,1)S(1)} collective-permute-done((bf16[8,16,512]{2,1,0:T(8,128)(2,1)S(1)}, bf16[8,16,512]{2,1,0:T(8,128)(2,1)S(1)}, u32[]{:S(2)}, u32[]{:S(2)}) %collective-permute-start.22) | collective-permute-done | bytes 131104 | tf_op jit(solution)/shard_map/ppermute | solution.py:497
  83.2 0.1 fusion
  83.3 2.1 %collective-permute-start.24 = (bf16[3,144,512]{2,1,0:T(8,128)(2,1)S(1)}, bf16[3,144,512]{2,1,0:T(8,128)(2,1)S(1)}, u32[]{:S(2)}, u32[]{:S(2)}) collective-permute-start(bf16[3,144,512]{2,1,0:T(8,128)(2,1)S(1)} %get-tuple-element.135), channel_id=1, source_target_pairs={{8,0},{16,8},{24,16},{9,1},{17,9},{25,17},{10,2},{18,10},{26,18},{... | collective-permute-start | bytes 1327112 | tf_op jit(solution)/shard_map/ppermute | solution.py:502
  85.4 3.2 %collective-permute-start.23 = (bf16[3,144,512]{2,1,0:T(8,128)(2,1)S(1)}, bf16[3,144,512]{2,1,0:T(8,128)(2,1)S(1)}, u32[]{:S(2)}, u32[]{:S(2)}) collective-permute-start(bf16[3,144,512]{2,1,0:T(8,128)(2,1)S(1)} %get-tuple-element.136), channel_id=1, source_target_pairs={{0,8},{8,16},{16,24},{1,9},{9,17},{17,25},{2,10},{10,18},{18,26},{... | collective-permute-start | bytes 1327112 | tf_op jit(solution)/shard_map/ppermute | solution.py:501
  88.6 5.3 %inner.1 = (bf16[8,128,512]{2,1,0:T(8,128)(2,1)S(1)}, bf16[8,144,1024]{2,1,0:T(8,128)(2,1)S(1)}, bf16[2,128,512]{2,1,0:T(8,128)(2,1)S(1)}, bf16[2,128,512]{2,1,0:T(8,128)(2,1)S(1)}, f32[1,1]{1,0:T(1,128)}) custom-call(bf16[8,128,512]{2,1,0:T(8,128)(2,1)S(1)} %get-tuple-element.127.normed_ref, bf16[8,16,512]{2,1,0:T(8,128)(2,1)S(1)} %collective-permute-done.21.before_ref, ...), custom_call_target="tpu_custom_call" | custom-call | flops 2684354560 | bytes 11800580 | tf_op jit(solution)/shard_map/inner/pallas_call | solution.py:203
  93.9 3.4 %collective-permute-done.24.down_ref = bf16[3,144,512]{2,1,0:T(8,128)(2,1)S(1)} collective-permute-done((bf16[3,144,512]{2,1,0:T(8,128)(2,1)S(1)}, bf16[3,144,512]{2,1,0:T(8,128)(2,1)S(1)}, u32[]{:S(2)}, u32[]{:S(2)}) %collective-permute-start.24) | collective-permute-done | bytes 442400 | tf_op jit(solution)/shard_map/ppermute | solution.py:502
  97.3 1.8 %collective-permute-done.23.up_ref = bf16[3,144,512]{2,1,0:T(8,128)(2,1)S(1)} collective-permute-done((bf16[3,144,512]{2,1,0:T(8,128)(2,1)S(1)}, bf16[3,144,512]{2,1,0:T(8,128)(2,1)S(1)}, u32[]{:S(2)}, u32[]{:S(2)}) %collective-permute-start.23) | collective-permute-done | bytes 442400 | tf_op jit(solution)/shard_map/ppermute | solution.py:501
  99.2 10.5 %outer.1 = (bf16[8,128,512]{2,1,0:T(8,128)(2,1)}, bf16[8,128,512]{2,1,0:T(8,128)(2,1)}, f32[1,1]{1,0:T(1,128)}) custom-call(bf16[3,144,512]{2,1,0:T(8,128)(2,1)S(1)} %collective-permute-done.23.up_ref, bf16[3,144,512]{2,1,0:T(8,128)(2,1)S(1)} %collective-permute-done.24.down_ref, bf16[8,128,512]{2,1,0:T(8,128)(2,1)S(1)} %get-tuple-element.130.q_ref, ...), custom_call_target="tpu_custom_call" | custom-call | flops 3221225472 | bytes 13471752 | tf_op jit(solution)/shard_map/outer/pallas_call | solution.py:203
  (59 shorter events, 0.2 us)
Async XLA Ops:
  4.0 12.0 %collective-permute-start = (bf16[2,48,1280]{2,1,0:T(8,128)(2,1)}, bf16[2,48,1280]{2,1,0:T(8,128)(2,1)S(1)}, u32[]{:S(2)}, u32[]{:S(2)}) collective-permute-start(bf16[2,48,1280]{2,1,0:T(8,128)(2,1)} %get-tuple-element.78), channel_id=1, source_target_pairs={{0,1},{1,0},{2,3},{3,2},{4,5},{5,4},{6,7},{7,6},{8,9},{9,8},{10,11... | collective-permute-start | bytes 737288 | tf_op jit(solution)/shard_map/ppermute | solution.py:423
  4.7 12.6 %collective-permute-start.1 = (bf16[2,48,1280]{2,1,0:T(8,128)(2,1)}, bf16[2,48,1280]{2,1,0:T(8,128)(2,1)S(1)}, u32[]{:S(2)}, u32[]{:S(2)}) collective-permute-start(bf16[2,48,1280]{2,1,0:T(8,128)(2,1)} %get-tuple-element.79), channel_id=1, source_target_pairs={{0,2},{1,3},{2,0},{3,1},{4,6},{5,7},{6,4},{7,5},{8,10},{9,11},{10,... | collective-permute-start | bytes 737288 | tf_op jit(solution)/shard_map/ppermute | solution.py:423
  5.9 19.8 %collective-permute-start.2 = (bf16[2,48,1280]{2,1,0:T(8,128)(2,1)}, bf16[2,48,1280]{2,1,0:T(8,128)(2,1)S(1)}, u32[]{:S(2)}, u32[]{:S(2)}) collective-permute-start(bf16[2,48,1280]{2,1,0:T(8,128)(2,1)} %get-tuple-element.80), channel_id=1, source_target_pairs={{0,3},{1,2},{2,1},{3,0},{4,7},{5,6},{6,5},{7,4},{8,11},{9,10},{10,... | collective-permute-start | bytes 737288 | tf_op jit(solution)/shard_map/ppermute | solution.py:423
  6.3 19.4 %collective-permute-start.3 = (bf16[2,48,1280]{2,1,0:T(8,128)(2,1)}, bf16[2,48,1280]{2,1,0:T(8,128)(2,1)S(1)}, u32[]{:S(2)}, u32[]{:S(2)}) collective-permute-start(bf16[2,48,1280]{2,1,0:T(8,128)(2,1)} %get-tuple-element.81), channel_id=1, source_target_pairs={{0,4},{1,5},{2,6},{3,7},{4,0},{5,1},{6,2},{7,3},{8,12},{9,13},{10,... | collective-permute-start | bytes 737288 | tf_op jit(solution)/shard_map/ppermute | solution.py:423
  6.5 19.2 %collective-permute-start.4 = (bf16[2,48,1280]{2,1,0:T(8,128)(2,1)}, bf16[2,48,1280]{2,1,0:T(8,128)(2,1)S(1)}, u32[]{:S(2)}, u32[]{:S(2)}) collective-permute-start(bf16[2,48,1280]{2,1,0:T(8,128)(2,1)} %get-tuple-element.82), channel_id=1, source_target_pairs={{0,5},{1,4},{2,7},{3,6},{4,1},{5,0},{6,3},{7,2},{8,13},{9,12},{10,... | collective-permute-start | bytes 737288 | tf_op jit(solution)/shard_map/ppermute | solution.py:423
  12.0 13.7 %all-to-all-start = ((s32[8,1,128]{2,1,0:T(1,128)}), s32[8,1,128]{2,1,0:T(1,128)S(1)}, u32[]{:S(2)}, u32[]{:S(2)}) async-start(s32[8,1,128]{2,1,0:T(1,128)} %bitcast.11), calls=%async_computation | async-start | bytes 8192 | tf_op jit(solution)/shard_map/all_to_all | solution.py:457
  16.0 9.6 %copy-start.11 = (bf16[2,48,1280]{2,1,0:T(8,128)(2,1)}, bf16[2,48,1280]{2,1,0:T(8,128)(2,1)S(1)}, u32[]{:S(2)}) copy-start(bf16[2,48,1280]{2,1,0:T(8,128)(2,1)S(1)} %collective-permute-done.refs_1_) | copy-start | bytes 737284
  16.0 9.7 %collective-permute-start.5 = (bf16[2,48,1280]{2,1,0:T(8,128)(2,1)}, bf16[2,48,1280]{2,1,0:T(8,128)(2,1)S(1)}, u32[]{:S(2)}, u32[]{:S(2)}) collective-permute-start(bf16[2,48,1280]{2,1,0:T(8,128)(2,1)} %get-tuple-element.83), channel_id=1, source_target_pairs={{0,6},{1,7},{2,4},{3,5},{4,2},{5,3},{6,0},{7,1},{8,14},{9,15},{10,... | collective-permute-start | bytes 737288 | tf_op jit(solution)/shard_map/ppermute | solution.py:423
  17.2 8.4 %copy-start.12 = (bf16[2,48,1280]{2,1,0:T(8,128)(2,1)}, bf16[2,48,1280]{2,1,0:T(8,128)(2,1)S(1)}, u32[]{:S(2)}) copy-start(bf16[2,48,1280]{2,1,0:T(8,128)(2,1)S(1)} %collective-permute-done.1.refs_2_) | copy-start | bytes 737284
  17.2 12.9 %collective-permute-start.6 = (bf16[2,48,1280]{2,1,0:T(8,128)(2,1)}, bf16[2,48,1280]{2,1,0:T(8,128)(2,1)S(1)}, u32[]{:S(2)}, u32[]{:S(2)}) collective-permute-start(bf16[2,48,1280]{2,1,0:T(8,128)(2,1)} %get-tuple-element.84), channel_id=1, source_target_pairs={{0,7},{1,6},{2,5},{3,4},{4,3},{5,2},{6,1},{7,0},{8,15},{9,14},{10,... | collective-permute-start | bytes 737288 | tf_op jit(solution)/shard_map/ppermute | solution.py:423
  25.7 5.2 %copy-start.13 = (bf16[2,48,1280]{2,1,0:T(8,128)(2,1)}, bf16[2,48,1280]{2,1,0:T(8,128)(2,1)S(1)}, u32[]{:S(2)}) copy-start(bf16[2,48,1280]{2,1,0:T(8,128)(2,1)S(1)} %collective-permute-done.2.refs_3_) | copy-start | bytes 737284
  25.7 5.1 %copy-start.14 = (bf16[2,48,1280]{2,1,0:T(8,128)(2,1)}, bf16[2,48,1280]{2,1,0:T(8,128)(2,1)S(1)}, u32[]{:S(2)}) copy-start(bf16[2,48,1280]{2,1,0:T(8,128)(2,1)S(1)} %collective-permute-done.3.refs_4_) | copy-start | bytes 737284
  25.7 5.1 %copy-start.15 = (bf16[2,48,1280]{2,1,0:T(8,128)(2,1)}, bf16[2,48,1280]{2,1,0:T(8,128)(2,1)S(1)}, u32[]{:S(2)}) copy-start(bf16[2,48,1280]{2,1,0:T(8,128)(2,1)S(1)} %collective-permute-done.4.refs_5_) | copy-start | bytes 737284
  25.7 4.4 %copy-start.16 = (bf16[2,48,1280]{2,1,0:T(8,128)(2,1)}, bf16[2,48,1280]{2,1,0:T(8,128)(2,1)S(1)}, u32[]{:S(2)}) copy-start(bf16[2,48,1280]{2,1,0:T(8,128)(2,1)S(1)} %collective-permute-done.5.refs_6_) | copy-start | bytes 737284
  30.1 0.7 copy-start.17
  30.8 23.0 %copy-start = (f32[256,512]{1,0:T(8,128)S(1)}, f32[256,512]{1,0:T(8,128)}, u32[]{:S(2)}) copy-start(f32[256,512]{1,0:T(8,128)} %get-tuple-element.96.base_ref) | copy-start | bytes 1572868
  30.8 23.0 %copy-start.1 = (bf16[1024,256]{1,0:T(8,128)(2,1)S(1)}, bf16[1024,256]{1,0:T(8,128)(2,1)}, u32[]{:S(2)}) copy-start(bf16[1024,256]{1,0:T(8,128)(2,1)} %get-tuple-element.97.relay_ref) | copy-start | bytes 1572868
  30.8 23.0 %copy-start.2 = (bf16[256,768]{1,0:T(8,128)(2,1)S(1)}, bf16[256,768]{1,0:T(8,128)(2,1)}, u32[]{:S(2)}) copy-start(bf16[256,768]{1,0:T(8,128)(2,1)} %get-tuple-element.94.high_ref) | copy-start | bytes 1179652
  30.8 23.0 %copy-start.3 = (bf16[256,768]{1,0:T(8,128)(2,1)S(1)}, bf16[256,768]{1,0:T(8,128)(2,1)}, u32[]{:S(2)}) copy-start(bf16[256,768]{1,0:T(8,128)(2,1)} %get-tuple-element.95.low_ref) | copy-start | bytes 1179652
  40.2 23.6 %copy-start.10 = (bf16[512]{0:T(512)(128)(2,1)S(1)}, bf16[512]{0:T(512)(128)(2,1)}, u32[]{:S(2)}) copy-start(bf16[512]{0:T(512)(128)(2,1)} %param.22) | copy-start | bytes 3076
  40.2 31.6 %copy-start.9 = (f32[512]{0:T(512)S(1)}, f32[512]{0:T(512)}, u32[]{:S(2)}) copy-start(f32[512]{0:T(512)} %param.23) | copy-start | bytes 6148
  40.2 4.1 %collective-permute-start.7 = (bf16[2,48,512]{2,1,0:T(8,128)(2,1)}, bf16[2,48,512]{2,1,0:T(8,128)(2,1)S(1)}, u32[]{:S(2)}, u32[]{:S(2)}) collective-permute-start(bf16[2,48,512]{2,1,0:T(8,128)(2,1)} %get-tuple-element.108), channel_id=1, source_target_pairs={{0,1},{1,0},{2,3},{3,2},{4,5},{5,4},{6,7},{7,6},{8,9},{9,8},{10,11... | collective-permute-start | bytes 294920 | tf_op jit(solution)/shard_map/ppermute | solution.py:423
  40.3 5.1 %collective-permute-start.8 = (bf16[2,48,512]{2,1,0:T(8,128)(2,1)}, bf16[2,48,512]{2,1,0:T(8,128)(2,1)S(1)}, u32[]{:S(2)}, u32[]{:S(2)}) collective-permute-start(bf16[2,48,512]{2,1,0:T(8,128)(2,1)} %get-tuple-element.109), channel_id=1, source_target_pairs={{0,2},{1,3},{2,0},{3,1},{4,6},{5,7},{6,4},{7,5},{8,10},{9,11},{10,... | collective-permute-start | bytes 294920 | tf_op jit(solution)/shard_map/ppermute | solution.py:423
  41.8 5.9 %collective-permute-start.9 = (bf16[2,48,512]{2,1,0:T(8,128)(2,1)}, bf16[2,48,512]{2,1,0:T(8,128)(2,1)S(1)}, u32[]{:S(2)}, u32[]{:S(2)}) collective-permute-start(bf16[2,48,512]{2,1,0:T(8,128)(2,1)} %get-tuple-element.110), channel_id=1, source_target_pairs={{0,3},{1,2},{2,1},{3,0},{4,7},{5,6},{6,5},{7,4},{8,11},{9,10},{10,... | collective-permute-start | bytes 294920 | tf_op jit(solution)/shard_map/ppermute | solution.py:423
  42.8 4.9 %collective-permute-start.10 = (bf16[2,48,512]{2,1,0:T(8,128)(2,1)}, bf16[2,48,512]{2,1,0:T(8,128)(2,1)S(1)}, u32[]{:S(2)}, u32[]{:S(2)}) collective-permute-start(bf16[2,48,512]{2,1,0:T(8,128)(2,1)} %get-tuple-element.111), channel_id=1, source_target_pairs={{0,4},{1,5},{2,6},{3,7},{4,0},{5,1},{6,2},{7,3},{8,12},{9,13},{10,... | collective-permute-start | bytes 294920 | tf_op jit(solution)/shard_map/ppermute | solution.py:423
  42.9 10.9 %collective-permute-start.11 = (bf16[2,48,512]{2,1,0:T(8,128)(2,1)}, bf16[2,48,512]{2,1,0:T(8,128)(2,1)S(1)}, u32[]{:S(2)}, u32[]{:S(2)}) collective-permute-start(bf16[2,48,512]{2,1,0:T(8,128)(2,1)} %get-tuple-element.112), channel_id=1, source_target_pairs={{0,5},{1,4},{2,7},{3,6},{4,1},{5,0},{6,3},{7,2},{8,13},{9,12},{10,... | collective-permute-start | bytes 294920 | tf_op jit(solution)/shard_map/ppermute | solution.py:423
  44.3 9.5 %collective-permute-start.12 = (bf16[2,48,512]{2,1,0:T(8,128)(2,1)}, bf16[2,48,512]{2,1,0:T(8,128)(2,1)S(1)}, u32[]{:S(2)}, u32[]{:S(2)}) collective-permute-start(bf16[2,48,512]{2,1,0:T(8,128)(2,1)} %get-tuple-element.113), channel_id=1, source_target_pairs={{0,6},{1,7},{2,4},{3,5},{4,2},{5,3},{6,0},{7,1},{8,14},{9,15},{10,... | collective-permute-start | bytes 294920 | tf_op jit(solution)/shard_map/ppermute | solution.py:423
  45.4 8.4 %collective-permute-start.13 = (bf16[2,48,512]{2,1,0:T(8,128)(2,1)}, bf16[2,48,512]{2,1,0:T(8,128)(2,1)S(1)}, u32[]{:S(2)}, u32[]{:S(2)}) collective-permute-start(bf16[2,48,512]{2,1,0:T(8,128)(2,1)} %get-tuple-element.114), channel_id=1, source_target_pairs={{0,7},{1,6},{2,5},{3,4},{4,3},{5,2},{6,1},{7,0},{8,15},{9,14},{10,... | collective-permute-start | bytes 294920 | tf_op jit(solution)/shard_map/ppermute | solution.py:423
  53.9 0.9 copy-start.4
  55.8 4.2 %collective-permute-start.14 = (bf16[128,512]{1,0:T(8,128)(2,1)S(1)}, bf16[128,512]{1,0:T(8,128)(2,1)S(1)}, u32[]{:S(2)}, u32[]{:S(2)}) collective-permute-start(bf16[128,512]{1,0:T(8,128)(2,1)S(1)} %get-tuple-element.116), channel_id=1, source_target_pairs={{0,1},{1,0},{2,3},{3,2},{4,5},{5,4},{6,7},{7,6},{8,9},{9,8},{10,11... | collective-permute-start | bytes 393224 | tf_op jit(solution)/shard_map/ppermute | solution.py:423
  56.2 5.1 %collective-permute-start.15 = (bf16[128,512]{1,0:T(8,128)(2,1)S(1)}, bf16[128,512]{1,0:T(8,128)(2,1)S(1)}, u32[]{:S(2)}, u32[]{:S(2)}) collective-permute-start(bf16[128,512]{1,0:T(8,128)(2,1)S(1)} %get-tuple-element.117), channel_id=1, source_target_pairs={{0,2},{1,3},{2,0},{3,1},{4,6},{5,7},{6,4},{7,5},{8,10},{9,11},{10,... | collective-permute-start | bytes 393224 | tf_op jit(solution)/shard_map/ppermute | solution.py:423
  57.5 7.5 %collective-permute-start.16 = (bf16[128,512]{1,0:T(8,128)(2,1)S(1)}, bf16[128,512]{1,0:T(8,128)(2,1)S(1)}, u32[]{:S(2)}, u32[]{:S(2)}) collective-permute-start(bf16[128,512]{1,0:T(8,128)(2,1)S(1)} %get-tuple-element.118), channel_id=1, source_target_pairs={{0,3},{1,2},{2,1},{3,0},{4,7},{5,6},{6,5},{7,4},{8,11},{9,10},{10,... | collective-permute-start | bytes 393224 | tf_op jit(solution)/shard_map/ppermute | solution.py:423
  58.1 6.9 %collective-permute-start.17 = (bf16[128,512]{1,0:T(8,128)(2,1)S(1)}, bf16[128,512]{1,0:T(8,128)(2,1)S(1)}, u32[]{:S(2)}, u32[]{:S(2)}) collective-permute-start(bf16[128,512]{1,0:T(8,128)(2,1)S(1)} %get-tuple-element.119), channel_id=1, source_target_pairs={{0,4},{1,5},{2,6},{3,7},{4,0},{5,1},{6,2},{7,3},{8,12},{9,13},{10,... | collective-permute-start | bytes 393224 | tf_op jit(solution)/shard_map/ppermute | solution.py:423
  58.3 13.5 %collective-permute-start.18 = (bf16[128,512]{1,0:T(8,128)(2,1)S(1)}, bf16[128,512]{1,0:T(8,128)(2,1)S(1)}, u32[]{:S(2)}, u32[]{:S(2)}) collective-permute-start(bf16[128,512]{1,0:T(8,128)(2,1)S(1)} %get-tuple-element.120), channel_id=1, source_target_pairs={{0,5},{1,4},{2,7},{3,6},{4,1},{5,0},{6,3},{7,2},{8,13},{9,12},{10,... | collective-permute-start | bytes 393224 | tf_op jit(solution)/shard_map/ppermute | solution.py:423
  59.9 11.9 %collective-permute-start.19 = (bf16[128,512]{1,0:T(8,128)(2,1)S(1)}, bf16[128,512]{1,0:T(8,128)(2,1)S(1)}, u32[]{:S(2)}, u32[]{:S(2)}) collective-permute-start(bf16[128,512]{1,0:T(8,128)(2,1)S(1)} %get-tuple-element.121), channel_id=1, source_target_pairs={{0,6},{1,7},{2,4},{3,5},{4,2},{5,3},{6,0},{7,1},{8,14},{9,15},{10,... | collective-permute-start | bytes 393224 | tf_op jit(solution)/shard_map/ppermute | solution.py:423
  61.3 10.5 %collective-permute-start.20 = (bf16[128,512]{1,0:T(8,128)(2,1)S(1)}, bf16[128,512]{1,0:T(8,128)(2,1)S(1)}, u32[]{:S(2)}, u32[]{:S(2)}) collective-permute-start(bf16[128,512]{1,0:T(8,128)(2,1)S(1)} %get-tuple-element.122), channel_id=1, source_target_pairs={{0,7},{1,6},{2,5},{3,4},{4,3},{5,2},{6,1},{7,0},{8,15},{9,14},{10,... | collective-permute-start | bytes 393224 | tf_op jit(solution)/shard_map/ppermute | solution.py:423
  71.8 16.8 %copy-start.5 = (bf16[512,1536]{1,0:T(8,128)(2,1)S(1)}, bf16[512,1536]{1,0:T(8,128)(2,1)}, u32[]{:S(2)}) copy-start(bf16[512,1536]{1,0:T(8,128)(2,1)} %wqkv_ref.3) | copy-start | bytes 4718596
  71.8 16.8 %copy-start.6 = (bf16[8,128,768]{2,1,0:T(8,128)(2,1)S(1)}, bf16[8,128,768]{2,1,0:T(8,128)(2,1)}, u32[]{:S(2)}) copy-start(bf16[8,128,768]{2,1,0:T(8,128)(2,1)} %pixels_ref.3) | copy-start | bytes 4718596
  71.8 16.8 %copy-start.7 = (bf16[512,768]{1,0:T(8,128)(2,1)S(1)}, bf16[512,768]{1,0:T(8,128)(2,1)}, u32[]{:S(2)}) copy-start(bf16[512,768]{1,0:T(8,128)(2,1)} %whead_ref.3) | copy-start | bytes 2359300
  71.8 16.8 %copy-start.8 = (bf16[512,512]{1,0:T(8,128)(2,1)S(1)}, bf16[512,512]{1,0:T(8,128)(2,1)}, u32[]{:S(2)}) copy-start(bf16[512,512]{1,0:T(8,128)(2,1)} %wout_ref.3) | copy-start | bytes 1572868
  73.6 5.2 %collective-permute-start.21 = (bf16[8,16,512]{2,1,0:T(8,128)(2,1)S(1)}, bf16[8,16,512]{2,1,0:T(8,128)(2,1)S(1)}, u32[]{:S(2)}, u32[]{:S(2)}) collective-permute-start(bf16[8,16,512]{2,1,0:T(8,128)(2,1)S(1)} %get-tuple-element.124), channel_id=1, source_target_pairs={{0,1},{1,2},{2,3},{3,4},{4,5},{5,6},{6,7},{8,9},{9,10},{10,11},{11... | collective-permute-start | bytes 393224 | tf_op jit(solution)/shard_map/ppermute | solution.py:496
  76.9 6.3 %collective-permute-start.22 = (bf16[8,16,512]{2,1,0:T(8,128)(2,1)S(1)}, bf16[8,16,512]{2,1,0:T(8,128)(2,1)S(1)}, u32[]{:S(2)}, u32[]{:S(2)}) collective-permute-start(bf16[8,16,512]{2,1,0:T(8,128)(2,1)S(1)} %get-tuple-element.125), channel_id=1, source_target_pairs={{1,0},{2,1},{3,2},{4,3},{5,4},{6,5},{7,6},{9,8},{10,9},{11,10},{12... | collective-permute-start | bytes 393224 | tf_op jit(solution)/shard_map/ppermute | solution.py:497
  83.3 14.1 %collective-permute-start.24 = (bf16[3,144,512]{2,1,0:T(8,128)(2,1)S(1)}, bf16[3,144,512]{2,1,0:T(8,128)(2,1)S(1)}, u32[]{:S(2)}, u32[]{:S(2)}) collective-permute-start(bf16[3,144,512]{2,1,0:T(8,128)(2,1)S(1)} %get-tuple-element.135), channel_id=1, source_target_pairs={{8,0},{16,8},{24,16},{9,1},{17,9},{25,17},{10,2},{18,10},{26,18},{... | collective-permute-start | bytes 1327112 | tf_op jit(solution)/shard_map/ppermute | solution.py:502
  85.4 13.8 %collective-permute-start.23 = (bf16[3,144,512]{2,1,0:T(8,128)(2,1)S(1)}, bf16[3,144,512]{2,1,0:T(8,128)(2,1)S(1)}, u32[]{:S(2)}, u32[]{:S(2)}) collective-permute-start(bf16[3,144,512]{2,1,0:T(8,128)(2,1)S(1)} %get-tuple-element.136), channel_id=1, source_target_pairs={{0,8},{8,16},{16,24},{1,9},{9,17},{17,25},{2,10},{10,18},{18,26},{... | collective-permute-start | bytes 1327112 | tf_op jit(solution)/shard_map/ppermute | solution.py:501

commit v2 on v1

--- a/solution.py
+++ b/solution.py
@@ -253,58 +253,49 @@
     return ones_where(hit)
 
 
-def attention(q_ref, kv_ref, att_ref, starts, first_row, grid_h, grid_w, tile_h, tile_w):
+def attention(q_ref, kv_ref, key_rows, starts, grid_h, grid_w, tile_h, tile_w, sink):
     width = q_ref.shape[2]
     lanes = 256
     heads = lanes // HD
     lane_head = iota((1, lanes), 1) // HD
     masks = [lane_head == h for h in range(heads)]
     picks = [ones_where(m) for m in masks]
-    key_rows = 2 + 2 * RAD
     keys = key_rows * SPAN
     scale = math.log2(math.e) / math.sqrt(HD)
     band_row = lax.axis_index("dp")
     owner = lax.axis_index("expert")
-
-    near = {}
-    for count, q_row, k_row in starts:
+    near = []
+    for count, q_row, k_row, tile_row in starts:
         qi, ki = iota((count * STRIP, keys), 0), iota((count * STRIP, keys), 1)
-        down = ki // SPAN + first_row + k_row - q_row - qi // STRIP
+        down = ki // SPAN + tile_row - q_row - qi // STRIP
         across = ki % SPAN - qi % STRIP
         ok = (down >= -RAD) & (down <= RAD) & (across >= 0) & (across <= 2 * RAD)
-        near[count, k_row - q_row] = ok, ki // SPAN, ki % SPAN
+        grid_row = band_row * tile_h + tile_row + ki // SPAN
+        near.append((ok & (grid_row >= 0) & (grid_row < grid_h), ki % SPAN))
     for j in range(tile_w // STRIP):
         c0 = j * STRIP
-        for count, q_row, k_row in starts:
+        for (count, q_row, k_row, tile_row), (ok, key_col) in zip(starts, near):
             items = count * STRIP
-            ok, key_row, key_col = near[count, k_row - q_row]
-            grid_row = band_row * tile_h + first_row + k_row + key_row
             grid_col = owner * tile_w + j * STRIP - RAD + key_col
-            ok = ok & (grid_row >= 0) & (grid_row < grid_h) & (grid_col >= 0) & (grid_col < grid_w)
-            bias = jnp.where(ok, 0.0, -1e30)
+            bias = jnp.where(ok & (grid_col >= 0) & (grid_col < grid_w), 0.0, -1e30)
             for g in range(width // lanes):
                 part = slice(g * lanes, (g + 1) * lanes)
-                queries = q_ref[q_row : q_row + count, pl.ds(c0, STRIP), part].reshape(items, lanes)
-                key = kv_ref[k_row : k_row + key_rows, pl.ds(c0, SPAN), part].reshape(keys, lanes)
+                queries = q_ref[q_row : q_row + count, c0 : c0 + STRIP, part].reshape(items, lanes)
+                key = kv_ref[k_row : k_row + key_rows, c0 : c0 + SPAN, part].reshape(keys, lanes)
                 value = kv_ref[
-                    k_row : k_row + key_rows, pl.ds(c0, SPAN), width + g * lanes : width + (g + 1) * lanes
+                    k_row : k_row + key_rows, c0 : c0 + SPAN, width + g * lanes : width + (g + 1) * lanes
                 ].reshape(keys, lanes)
                 stacked = jnp.concatenate([queries * pick for pick in picks], 0)
                 score = dot(stacked, key, ((1,), (1,))).reshape(heads, items, keys)
                 weight = jnp.exp2(score * scale + bias[None]).reshape(heads * items, keys)
-                total = jnp.sum(weight, axis=1, keepdims=True)
-                mixed = dot(weight.astype(jnp.bfloat16), value) * (1.0 / total)
-                mixed = mixed.reshape(heads, items, lanes)
-                out = mixed[0]
+                total = jnp.sum(weight, axis=1, keepdims=True).reshape(heads, items, 1)
+                mixed = dot(weight.astype(jnp.bfloat16), value).reshape(heads, items, lanes)
+                over, under = mixed[0], total[0]
                 for h in range(1, heads):
-                    out = jnp.where(masks[h], mixed[h], out)
-                att_ref[q_row : q_row + count, pl.ds(c0, STRIP), part] = out.astype(jnp.bfloat16).reshape(
-                    count, STRIP, lanes
-                )
-
-
-def row_groups(rows):
-    return [(min(2, rows.stop - r), r) for r in range(rows.start, rows.stop, 2)]
+                    over = jnp.where(masks[h], mixed[h], over)
+                    under = jnp.where(masks[h], total[h], under)
+                shape = (count, STRIP, lanes)
+                sink((slice(q_row, q_row + count), slice(c0, c0 + STRIP), part), over.reshape(shape), under.reshape(shape))
 
 
 def finish(rows, att_ref, dec_in_ref, keep_ref, pixels_ref, wout_ref, whead_ref, decoded_ref, dattn_ref, offset):
@@ -329,7 +320,7 @@
 
 def inner_kernel(
     grid_h, grid_w, normed_ref, before_ref, after_ref, dec_in_ref, keep_ref, wqkv_ref, wout_ref, whead_ref, pixels_ref,
-    q_ref, kv_ref, decoded_ref, dattn_ref, loss_ref, att_ref, held_ref, sem,
+    q_ref, over_ref, under_ref, decoded_ref, dattn_ref, loss_ref, kv_ref, att_ref, held_ref, sem,
 ):
     height, breadth, width = normed_ref.shape
     cols = kv_ref.shape[1]
@@ -348,8 +339,13 @@
     kv_ref[...] = dot(wide, wqkv_ref[:, width:]).astype(jnp.bfloat16).reshape(kv_ref.shape)
     flat = normed_ref[...].reshape(height * breadth, width)
     q_ref[...] = dot(flat, wqkv_ref[:, :width]).astype(jnp.bfloat16).reshape(q_ref.shape)
-    starts = [(n, r, r - RAD) for n, r in row_groups(inner)]
-    attention(q_ref, kv_ref, att_ref, starts, 0, grid_h, grid_w, height, breadth)
+    def keep_sums(place, over, under):
+        over_ref[place] = over
+        under_ref[place] = under
+
+    starts = [(2, r, 0, 0) for r in range(0, height, 2)]
+    attention(q_ref, kv_ref, height, starts, grid_h, grid_w, height, breadth, keep_sums)
+    att_ref[inner] = (over_ref[inner] * (1.0 / under_ref[inner])).astype(jnp.bfloat16)
     copy.wait()
     loss_ref[...] = finish(
         inner, att_ref, dec_in_ref, keep_ref, held_ref, wout_ref, whead_ref, decoded_ref, dattn_ref, RAD
@@ -357,7 +353,7 @@
 
 
 def outer_kernel(
-    grid_h, grid_w, up_ref, down_ref, q_ref, kv_in_ref, decoded_in_ref, dattn_in_ref, loss_in_ref,
+    grid_h, grid_w, up_ref, down_ref, q_ref, over_ref, under_ref, decoded_in_ref, dattn_in_ref, loss_in_ref,
     dec_in_ref, keep_ref, pixels_ref, wqkv_ref, wout_ref, whead_ref, decoded_ref, dattn_ref, loss_ref, kv_ref, att_ref,
 ):
     height, breadth, pd = pixels_ref.shape
@@ -369,16 +365,23 @@
     shift = shift_matrix(
         cols, breadth + edge, ((RAD, breadth, 0), (0, RAD, breadth + middle - RAD), (RAD + breadth, RAD, breadth + middle))
     )
-    kv_ref[RAD : RAD + height] = kv_in_ref[...]
-    for rim_ref, start in ((up_ref, 0), (down_ref, RAD + height)):
+    reach = RAD + 1
+    blank = jnp.zeros((1,) + kv_ref.shape[1:], bf16)
+    kv_ref[0:1] = blank
+    kv_ref[2 * reach - 1 : 2 * reach] = blank
+    for rim_ref, start in ((up_ref, 1), (down_ref, reach)):
         wide = [dot(shift, rim_ref[r]).astype(bf16) for r in range(RAD)]
         kv = dot(jnp.concatenate(wide, 0), wqkv_ref[:, width:]).astype(bf16)
         kv_ref[start : start + RAD] = kv.reshape(RAD, cols, 2 * width)
     inner = slice(RAD, height - RAD)
     decoded_ref[inner] = decoded_in_ref[...]
     dattn_ref[inner] = dattn_in_ref[...]
-    starts = [(2, r, r) for r in range(0, height, 2)]
-    attention(q_ref, kv_ref, att_ref, starts, -RAD, grid_h, grid_w, height, breadth)
+
+    def join(place, over, under):
+        att_ref[place] = ((over_ref[place] + over) * (1.0 / (under_ref[place] + under))).astype(bf16)
+
+    starts = [(RAD, 0, 0, -reach), (RAD, height - RAD, reach, height)]
+    attention(q_ref, kv_ref, reach, starts, grid_h, grid_w, height, breadth, join)
     loss = loss_in_ref[...]
     for rows in (slice(0, RAD), slice(height - RAD, height)):
         loss = loss + finish(
@@ -504,11 +507,12 @@
     grid_width = tile_width * groups
     cols = -(-(tile_width - STRIP + SPAN) // 16) * 16
     inner_shape = (tile_height - 2 * RAD, tile_width, dec_width)
-    queries, kv, decoded_inner, d_attn_inner, loss_inner = whole_call(
+    queries, over, under, decoded_inner, d_attn_inner, loss_inner = whole_call(
         functools.partial(inner_kernel, grid_height, grid_width),
         [
             shaped(grid_shape, bf16),
-            shaped((tile_height, cols, 2 * dec_width), bf16),
+            shaped(grid_shape, jnp.float32),
+            shaped(grid_shape, jnp.float32),
             shaped(inner_shape, bf16),
             shaped(inner_shape, bf16),
             shaped((1, 1), jnp.float32),
@@ -517,6 +521,7 @@
         "inner",
         10 * tile_size * dec_width * dec_width,
         [
+            pltpu.VMEM((tile_height, cols, 2 * dec_width), bf16),
             pltpu.VMEM(grid_shape, bf16),
             pltpu.VMEM((tile_height - 2 * RAD, tile_width, PD), bf16),
             pltpu.SemaphoreType.DMA(()),
@@ -527,12 +532,12 @@
     return whole_call(
         functools.partial(outer_kernel, grid_height, grid_width),
         [shaped(grid_shape, bf16), shaped(grid_shape, bf16), shaped((1, 1), jnp.float32)],
-        [above, below, queries, kv, decoded_inner, d_attn_inner, loss_inner]
+        [above, below, queries, over, under, decoded_inner, d_attn_inner, loss_inner]
         + [decoder_in, keep, pixels, w_qkv, w_out, w_head],
         "outer",
         12 * tile_size * dec_width * dec_width,
         [
-            pltpu.VMEM((tile_height + 2 * RAD, cols, 2 * dec_width), bf16),
+            pltpu.VMEM((2 * RAD + 2, cols, 2 * dec_width), bf16),
             pltpu.VMEM(grid_shape, bf16),
         ],
         room=OUTER_ROOM,

time: 110 us -> 109 us (level)
  waiting for transfers between devices: 28.3 us -> 24.7 us
  Pallas kernels: 41.7 us -> 44.4 us
    ppermute x1, waiting for transfers between devices: 3.42 us -> 0.01 us  [local(): below = lax.ppermute(top, 'dp', upward)]
    pallas_call x6, Pallas kernels: 25.7 us -> 28.4 us  [whole_call(): pl.pallas_call(kernel, out_shape=tuple(outs), in_specs=[VM] * (len(ins) -...]
  transfers between devices with their start and end apart: 26 -> 26, of which waited for: 8 -> 7; matrix products, arithmetic and copies ran while one was open for 0% -> 0% of each run, Pallas kernels for 14% -> 18%
where the time goes in v2:
time: 109 us
  Pallas kernels  44.4 us (41%)
  starting transfers between devices  36.5 us (33%)
  waiting for transfers between devices  24.7 us (23%)
  local copies, waits for them, and re-layouts  1.69 us (2%)
    pallas_call x6, Pallas kernels, whole_call(): pl.pallas_call(kernel, out_shape=tuple(outs), in_specs=[VM] * (len(ins) -...  28.4 us
    ppermute x21, starting transfers between devices, swap(): lax.ppermute(value, 'expert', [(i, i ^ k) for i in range(groups)])  22 us
    ppermute x21, waiting for transfers between devices, swap(): lax.ppermute(value, 'expert', [(i, i ^ k) for i in range(groups)])  18.7 us
    pallas_call x1, Pallas kernels, experts_apply(): pl.pallas_call(functools.partial(ffn_kernel, sources), grid=(local_expert...  9.32 us
    pallas_call x1, Pallas kernels, fold(): pl.pallas_call(fold_kernel, grid=(local_experts, hidden // chunk), out_sh...  6.67 us
    ppermute x1, waiting for transfers between devices, local(): lax.ppermute(first, 'expert', [(i + 1, i) for i in range(groups - 1)])  4.33 us
    all_to_all x1, starting transfers between devices, local(): lax.all_to_all(spots, 'expert', split_axis=0, concat_axis=0, tiled=True)  3.98 us
    ppermute x1, starting transfers between devices, local(): lax.ppermute(last, 'expert', [(i, i + 1) for i in range(groups - 1)])  3.28 us
  transfers between devices with their start and end apart: 26, of which 7 were waited for; matrix products, arithmetic and copies ran while one was open for 0% of the time, Pallas kernels for 18%

profile of v2, /device:TPU:13, one launch (start us, length us, event | category | flops | bytes accessed | tf_op | source)
XLA Modules:
  0.0 108.8 jit_solution(10594660155760559593)
XLA Ops:
  0.6 3.3 %pack.1 = (bf16[2,48,1280]{2,1,0:T(8,128)(2,1)}, bf16[2,48,1280]{2,1,0:T(8,128)(2,1)}, bf16[2,48,1280]{2,1,0:T(8,128)(2,1)}, bf16[2,48,1280]{2,1,0:T(8,128)(2,1)...) custom-call(s32[2,256]{1,0:T(2,128)} %bitcast.12, ...), custom_call_target="tpu_custom_call" | custom-call | flops 503316480 | bytes 2623488 | tf_op jit(solution)/shard_map/pack/pallas_call | solution.py:203
  4.0 0.7 collective-permute-start
  4.7 1.2 %collective-permute-start.1 = (bf16[2,48,1280]{2,1,0:T(8,128)(2,1)}, bf16[2,48,1280]{2,1,0:T(8,128)(2,1)S(1)}, u32[]{:S(2)}, u32[]{:S(2)}) collective-permute-start(bf16[2,48,1280]{2,1,0:T(8,128)(2,1)} %get-tuple-element.80), channel_id=1, source_target_pairs={{0,2},{1,3},{2,0},{3,1},{4,6},{5,7},{6,4},{7,5},{8,10},{9,11},{10,... | collective-permute-start | bytes 737288 | tf_op jit(solution)/shard_map/ppermute | solution.py:426
  5.9 0.4 collective-permute-start.2
  6.3 0.2 collective-permute-start.3
  6.5 1.6 %collective-permute-start.4 = (bf16[2,48,1280]{2,1,0:T(8,128)(2,1)}, bf16[2,48,1280]{2,1,0:T(8,128)(2,1)S(1)}, u32[]{:S(2)}, u32[]{:S(2)}) collective-permute-start(bf16[2,48,1280]{2,1,0:T(8,128)(2,1)} %get-tuple-element.83), channel_id=1, source_target_pairs={{0,5},{1,4},{2,7},{3,6},{4,1},{5,0},{6,3},{7,2},{8,13},{9,12},{10,... | collective-permute-start | bytes 737288 | tf_op jit(solution)/shard_map/ppermute | solution.py:426
  8.1 3.8 %prep.1 = (bf16[256,768]{1,0:T(8,128)(2,1)}, bf16[256,768]{1,0:T(8,128)(2,1)}, f32[256,512]{1,0:T(8,128)}, bf16[1024,256]{1,0:T(8,128)(2,1)}, s32[8,128]{1,0:T(8,128)}) custom-call(s32[2,256]{1,0:T(2,128)} %bitcast.13, f32[2,256]{1,0:T(2,128)} %bitcast.14, s32[1,256]{1,0:T(1,128)} %bitcast.15, bf16[256,1280]{1,0:T(8,128)(2,1)} %tokens_ref.2, ...), custom_call_target="tpu_custom_call" | custom-call | flops 335544320 | bytes 3810304 | tf_op jit(solution)/shard_map/prep/pallas_call | solution.py:203
  12.0 4.0 %all-to-all-start = ((s32[8,1,128]{2,1,0:T(1,128)}), s32[8,1,128]{2,1,0:T(1,128)S(1)}, u32[]{:S(2)}, u32[]{:S(2)}) async-start(s32[8,1,128]{2,1,0:T(1,128)} %bitcast.11), calls=%async_computation | async-start | bytes 8192 | tf_op jit(solution)/shard_map/all_to_all | solution.py:460
  16.0 1.2 %collective-permute-start.5 = (bf16[2,48,1280]{2,1,0:T(8,128)(2,1)}, bf16[2,48,1280]{2,1,0:T(8,128)(2,1)S(1)}, u32[]{:S(2)}, u32[]{:S(2)}) collective-permute-start(bf16[2,48,1280]{2,1,0:T(8,128)(2,1)} %get-tuple-element.84), channel_id=1, source_target_pairs={{0,6},{1,7},{2,4},{3,5},{4,2},{5,3},{6,0},{7,1},{8,14},{9,15},{10,... | collective-permute-start | bytes 737288 | tf_op jit(solution)/shard_map/ppermute | solution.py:426
  17.2 1.7 %collective-permute-start.6 = (bf16[2,48,1280]{2,1,0:T(8,128)(2,1)}, bf16[2,48,1280]{2,1,0:T(8,128)(2,1)S(1)}, u32[]{:S(2)}, u32[]{:S(2)}) collective-permute-start(bf16[2,48,1280]{2,1,0:T(8,128)(2,1)} %get-tuple-element.85), channel_id=1, source_target_pairs={{0,7},{1,6},{2,5},{3,4},{4,3},{5,2},{6,1},{7,0},{8,15},{9,14},{10,... | collective-permute-start | bytes 737288 | tf_op jit(solution)/shard_map/ppermute | solution.py:426
  18.9 6.7 %fold.1.refs_10_ = bf16[2,1024,512]{2,1,0:T(8,128)(2,1)} custom-call(bf16[2,1024,1280]{2,1,0:T(8,128)(2,1)} %down_ref, bf16[1280,512]{1,0:T(8,128)(2,1)} %embed_ref.3), custom_call_target="tpu_custom_call" | custom-call | flops 2684354560 | bytes 5242880 | tf_op jit(solution)/shard_map/fold/pallas_call | solution.py:123
  25.7 4.4 %collective-permute-done.6.refs_7_ = bf16[2,48,1280]{2,1,0:T(8,128)(2,1)S(1)} collective-permute-done((bf16[2,48,1280]{2,1,0:T(8,128)(2,1)}, bf16[2,48,1280]{2,1,0:T(8,128)(2,1)S(1)}, u32[]{:S(2)}, u32[]{:S(2)}) %collective-permute-start.6) | collective-permute-done | bytes 245792 | tf_op jit(solution)/shard_map/ppermute | solution.py:426
  30.1 0.7 copy-done.17
  30.8 0.0 copy-start.4
  30.9 9.3 %experts.1 = (bf16[2,48,512]{2,1,0:T(8,128)(2,1)}, bf16[2,48,512]{2,1,0:T(8,128)(2,1)}, bf16[2,48,512]{2,1,0:T(8,128)(2,1)}, bf16[2,48,512]{2,1,0:T(8,128)(2,1)}...) custom-call(bf16[2,48,1280]{2,1,0:T(8,128)(2,1)} %get-tuple-element., ...), custom_call_target="tpu_custom_call" | custom-call | flops 4831838208 | bytes 12582912 | tf_op jit(solution)/shard_map/experts/pallas_call | solution.py:225
  40.2 0.0 copy-start.9
  40.2 0.1 collective-permute-start.7
  40.3 1.2 %collective-permute-start.8 = (bf16[2,48,512]{2,1,0:T(8,128)(2,1)}, bf16[2,48,512]{2,1,0:T(8,128)(2,1)S(1)}, u32[]{:S(2)}, u32[]{:S(2)}) collective-permute-start(bf16[2,48,512]{2,1,0:T(8,128)(2,1)} %get-tuple-element.110), channel_id=1, source_target_pairs={{0,2},{1,3},{2,0},{3,1},{4,6},{5,7},{6,4},{7,5},{8,10},{9,11},{10,... | collective-permute-start | bytes 294920 | tf_op jit(solution)/shard_map/ppermute | solution.py:426
  41.5 0.3 multiply_sine_fusion
  41.8 0.9 collective-permute-start.9
  42.8 0.2 collective-permute-start.10
  42.9 1.4 %collective-permute-start.11 = (bf16[2,48,512]{2,1,0:T(8,128)(2,1)}, bf16[2,48,512]{2,1,0:T(8,128)(2,1)S(1)}, u32[]{:S(2)}, u32[]{:S(2)}) collective-permute-start(bf16[2,48,512]{2,1,0:T(8,128)(2,1)} %get-tuple-element.113), channel_id=1, source_target_pairs={{0,5},{1,4},{2,7},{3,6},{4,1},{5,0},{6,3},{7,2},{8,13},{9,12},{10,... | collective-permute-start | bytes 294920 | tf_op jit(solution)/shard_map/ppermute | solution.py:426
  44.3 1.1 collective-permute-start.12
  45.4 2.3 %collective-permute-start.13 = (bf16[2,48,512]{2,1,0:T(8,128)(2,1)}, bf16[2,48,512]{2,1,0:T(8,128)(2,1)S(1)}, u32[]{:S(2)}, u32[]{:S(2)}) collective-permute-start(bf16[2,48,512]{2,1,0:T(8,128)(2,1)} %get-tuple-element.115), channel_id=1, source_target_pairs={{0,7},{1,6},{2,5},{3,4},{4,3},{5,2},{6,1},{7,0},{8,15},{9,14},{10,... | collective-permute-start | bytes 294920 | tf_op jit(solution)/shard_map/ppermute | solution.py:426
  47.7 6.1 %collective-permute-done.11.refs_5_ = bf16[2,48,512]{2,1,0:T(8,128)(2,1)S(1)} collective-permute-done((bf16[2,48,512]{2,1,0:T(8,128)(2,1)}, bf16[2,48,512]{2,1,0:T(8,128)(2,1)S(1)}, u32[]{:S(2)}, u32[]{:S(2)}) %collective-permute-start.11) | collective-permute-done | bytes 98336 | tf_op jit(solution)/shard_map/ppermute | solution.py:426
  53.9 0.9 copy-done.8
  54.8 1.0 combine.1
  55.8 0.5 collective-permute-start.14
  56.2 1.2 %collective-permute-start.15 = (bf16[128,512]{1,0:T(8,128)(2,1)S(1)}, bf16[128,512]{1,0:T(8,128)(2,1)S(1)}, u32[]{:S(2)}, u32[]{:S(2)}) collective-permute-start(bf16[128,512]{1,0:T(8,128)(2,1)S(1)} %get-tuple-element.118), channel_id=1, source_target_pairs={{0,2},{1,3},{2,0},{3,1},{4,6},{5,7},{6,4},{7,5},{8,10},{9,11},{10,... | collective-permute-start | bytes 393224 | tf_op jit(solution)/shard_map/ppermute | solution.py:426
  57.4 0.1 multiply_sine_fusion.1
  57.5 0.6 collective-permute-start.16
  58.1 0.2 collective-permute-start.17
  58.3 1.6 %collective-permute-start.18 = (bf16[128,512]{1,0:T(8,128)(2,1)S(1)}, bf16[128,512]{1,0:T(8,128)(2,1)S(1)}, u32[]{:S(2)}, u32[]{:S(2)}) collective-permute-start(bf16[128,512]{1,0:T(8,128)(2,1)S(1)} %get-tuple-element.121), channel_id=1, source_target_pairs={{0,5},{1,4},{2,7},{3,6},{4,1},{5,0},{6,3},{7,2},{8,13},{9,12},{10,... | collective-permute-start | bytes 393224 | tf_op jit(solution)/shard_map/ppermute | solution.py:426
  59.9 1.2 %collective-permute-start.19 = (bf16[128,512]{1,0:T(8,128)(2,1)S(1)}, bf16[128,512]{1,0:T(8,128)(2,1)S(1)}, u32[]{:S(2)}, u32[]{:S(2)}) collective-permute-start(bf16[128,512]{1,0:T(8,128)(2,1)S(1)} %get-tuple-element.122), channel_id=1, source_target_pairs={{0,6},{1,7},{2,4},{3,5},{4,2},{5,3},{6,0},{7,1},{8,14},{9,15},{10,... | collective-permute-start | bytes 393224 | tf_op jit(solution)/shard_map/ppermute | solution.py:426
  61.2 0.1 collective-permute-done.15.refs_2_
  61.3 2.4 %collective-permute-start.20 = (bf16[128,512]{1,0:T(8,128)(2,1)S(1)}, bf16[128,512]{1,0:T(8,128)(2,1)S(1)}, u32[]{:S(2)}, u32[]{:S(2)}) collective-permute-start(bf16[128,512]{1,0:T(8,128)(2,1)S(1)} %get-tuple-element.123), channel_id=1, source_target_pairs={{0,7},{1,6},{2,5},{3,4},{4,3},{5,2},{6,1},{7,0},{8,15},{9,14},{10,... | collective-permute-start | bytes 393224 | tf_op jit(solution)/shard_map/ppermute | solution.py:426
  63.8 1.3 %collective-permute-done.16.refs_3_ = bf16[128,512]{1,0:T(8,128)(2,1)S(1)} collective-permute-done((bf16[128,512]{1,0:T(8,128)(2,1)S(1)}, bf16[128,512]{1,0:T(8,128)(2,1)S(1)}, u32[]{:S(2)}, u32[]{:S(2)}) %collective-permute-start.16) | collective-permute-done | bytes 131104 | tf_op jit(solution)/shard_map/ppermute | solution.py:426
  65.0 6.7 %collective-permute-done.18.refs_5_ = bf16[128,512]{1,0:T(8,128)(2,1)S(1)} collective-permute-done((bf16[128,512]{1,0:T(8,128)(2,1)S(1)}, bf16[128,512]{1,0:T(8,128)(2,1)S(1)}, u32[]{:S(2)}, u32[]{:S(2)}) %collective-permute-start.18) | collective-permute-done | bytes 131104 | tf_op jit(solution)/shard_map/ppermute | solution.py:426
  71.8 1.8 %place.1 = (bf16[8,128,512]{2,1,0:T(8,128)(2,1)S(1)}, f32[8,128,512]{2,1,0:T(8,128)S(1)}, f32[8,128,1]{2,1,0:T(8,128)S(1)}, bf16[3,128,512]{2,1,0:T(8,128)(2,1)S...) custom-call(s32[8,128]{1,0:T(8,128)S(1)} %bitcast.9, ...), custom_call_target="tpu_custom_call" | custom-call | flops 1073741824 | bytes 5393408 | tf_op jit(solution)/shard_map/place/pallas_call | solution.py:203
  73.7 3.3 %collective-permute-start.21 = (bf16[8,16,512]{2,1,0:T(8,128)(2,1)S(1)}, bf16[8,16,512]{2,1,0:T(8,128)(2,1)S(1)}, u32[]{:S(2)}, u32[]{:S(2)}) collective-permute-start(bf16[8,16,512]{2,1,0:T(8,128)(2,1)S(1)} %get-tuple-element.125), channel_id=1, source_target_pairs={{0,1},{1,2},{2,3},{3,4},{4,5},{5,6},{6,7},{8,9},{9,10},{10,11},{11... | collective-permute-start | bytes 393224 | tf_op jit(solution)/shard_map/ppermute | solution.py:499
  77.0 1.9 %collective-permute-start.22 = (bf16[8,16,512]{2,1,0:T(8,128)(2,1)S(1)}, bf16[8,16,512]{2,1,0:T(8,128)(2,1)S(1)}, u32[]{:S(2)}, u32[]{:S(2)}) collective-permute-start(bf16[8,16,512]{2,1,0:T(8,128)(2,1)S(1)} %get-tuple-element.126), channel_id=1, source_target_pairs={{1,0},{2,1},{3,2},{4,3},{5,4},{6,5},{7,6},{9,8},{10,9},{11,10},{12... | collective-permute-start | bytes 393224 | tf_op jit(solution)/shard_map/ppermute | solution.py:500
  78.9 4.3 %collective-permute-done.22.after_ref = bf16[8,16,512]{2,1,0:T(8,128)(2,1)S(1)} collective-permute-done((bf16[8,16,512]{2,1,0:T(8,128)(2,1)S(1)}, bf16[8,16,512]{2,1,0:T(8,128)(2,1)S(1)}, u32[]{:S(2)}, u32[]{:S(2)}) %collective-permute-start.22) | collective-permute-done | bytes 131104 | tf_op jit(solution)/shard_map/ppermute | solution.py:500
  83.3 0.1 fusion
  83.3 2.1 %collective-permute-start.24 = (bf16[3,144,512]{2,1,0:T(8,128)(2,1)S(1)}, bf16[3,144,512]{2,1,0:T(8,128)(2,1)S(1)}, u32[]{:S(2)}, u32[]{:S(2)}) collective-permute-start(bf16[3,144,512]{2,1,0:T(8,128)(2,1)S(1)} %get-tuple-element.137), channel_id=1, source_target_pairs={{8,0},{16,8},{24,16},{9,1},{17,9},{25,17},{10,2},{18,10},{26,18},{... | collective-permute-start | bytes 1327112 | tf_op jit(solution)/shard_map/ppermute | solution.py:505
  85.4 3.2 %collective-permute-start.23 = (bf16[3,144,512]{2,1,0:T(8,128)(2,1)S(1)}, bf16[3,144,512]{2,1,0:T(8,128)(2,1)S(1)}, u32[]{:S(2)}, u32[]{:S(2)}) collective-permute-start(bf16[3,144,512]{2,1,0:T(8,128)(2,1)S(1)} %get-tuple-element.138), channel_id=1, source_target_pairs={{0,8},{8,16},{16,24},{1,9},{9,17},{17,25},{2,10},{10,18},{18,26},{... | collective-permute-start | bytes 1327112 | tf_op jit(solution)/shard_map/ppermute | solution.py:504
  88.7 8.9 %inner.1 = (bf16[8,128,512]{2,1,0:T(8,128)(2,1)S(1)}, f32[8,128,512]{2,1,0:T(8,128)S(1)}, f32[8,128,512]{2,1,0:T(8,128)S(1)}, bf16[2,128,512]{2,1,0:T(8,128)(2,1...) custom-call(bf16[8,128,512]{2,1,0:T(8,128)(2,1)S(1)} %get-tuple-element.128.normed_ref, ...), custom_call_target="tpu_custom_call" | custom-call | flops 2684354560 | bytes 13635588 | tf_op jit(solution)/shard_map/inner/pallas_call | solution.py:203
  97.6 1.6 %collective-permute-done.23.up_ref = bf16[3,144,512]{2,1,0:T(8,128)(2,1)S(1)} collective-permute-done((bf16[3,144,512]{2,1,0:T(8,128)(2,1)S(1)}, bf16[3,144,512]{2,1,0:T(8,128)(2,1)S(1)}, u32[]{:S(2)}, u32[]{:S(2)}) %collective-permute-start.23) | collective-permute-done | bytes 442400 | tf_op jit(solution)/shard_map/ppermute | solution.py:504
  99.3 9.5 %outer.1 = (bf16[8,128,512]{2,1,0:T(8,128)(2,1)}, bf16[8,128,512]{2,1,0:T(8,128)(2,1)}, f32[1,1]{1,0:T(1,128)}) custom-call(bf16[3,144,512]{2,1,0:T(8,128)(2,1)S(1)} %collective-permute-done.23.up_ref, bf16[3,144,512]{2,1,0:T(8,128)(2,1)S(1)} %collective-permute-done.24.down_ref, bf16[8,128,512]{2,1,0:T(8,128)(2,1)S(1)} %get-tuple-element.131.q_ref, ...), custom_call_target="tpu_custom_call" | custom-call | flops 3221225472 | bytes 15306760 | tf_op jit(solution)/shard_map/outer/pallas_call | solution.py:203
  (59 shorter events, 0.2 us)
Async XLA Ops:
  4.0 12.0 %collective-permute-start = (bf16[2,48,1280]{2,1,0:T(8,128)(2,1)}, bf16[2,48,1280]{2,1,0:T(8,128)(2,1)S(1)}, u32[]{:S(2)}, u32[]{:S(2)}) collective-permute-start(bf16[2,48,1280]{2,1,0:T(8,128)(2,1)} %get-tuple-element.79), channel_id=1, source_target_pairs={{0,1},{1,0},{2,3},{3,2},{4,5},{5,4},{6,7},{7,6},{8,9},{9,8},{10,11... | collective-permute-start | bytes 737288 | tf_op jit(solution)/shard_map/ppermute | solution.py:426
  4.7 12.6 %collective-permute-start.1 = (bf16[2,48,1280]{2,1,0:T(8,128)(2,1)}, bf16[2,48,1280]{2,1,0:T(8,128)(2,1)S(1)}, u32[]{:S(2)}, u32[]{:S(2)}) collective-permute-start(bf16[2,48,1280]{2,1,0:T(8,128)(2,1)} %get-tuple-element.80), channel_id=1, source_target_pairs={{0,2},{1,3},{2,0},{3,1},{4,6},{5,7},{6,4},{7,5},{8,10},{9,11},{10,... | collective-permute-start | bytes 737288 | tf_op jit(solution)/shard_map/ppermute | solution.py:426
  5.9 19.8 %collective-permute-start.2 = (bf16[2,48,1280]{2,1,0:T(8,128)(2,1)}, bf16[2,48,1280]{2,1,0:T(8,128)(2,1)S(1)}, u32[]{:S(2)}, u32[]{:S(2)}) collective-permute-start(bf16[2,48,1280]{2,1,0:T(8,128)(2,1)} %get-tuple-element.81), channel_id=1, source_target_pairs={{0,3},{1,2},{2,1},{3,0},{4,7},{5,6},{6,5},{7,4},{8,11},{9,10},{10,... | collective-permute-start | bytes 737288 | tf_op jit(solution)/shard_map/ppermute | solution.py:426
  6.3 19.4 %collective-permute-start.3 = (bf16[2,48,1280]{2,1,0:T(8,128)(2,1)}, bf16[2,48,1280]{2,1,0:T(8,128)(2,1)S(1)}, u32[]{:S(2)}, u32[]{:S(2)}) collective-permute-start(bf16[2,48,1280]{2,1,0:T(8,128)(2,1)} %get-tuple-element.82), channel_id=1, source_target_pairs={{0,4},{1,5},{2,6},{3,7},{4,0},{5,1},{6,2},{7,3},{8,12},{9,13},{10,... | collective-permute-start | bytes 737288 | tf_op jit(solution)/shard_map/ppermute | solution.py:426
  6.5 19.2 %collective-permute-start.4 = (bf16[2,48,1280]{2,1,0:T(8,128)(2,1)}, bf16[2,48,1280]{2,1,0:T(8,128)(2,1)S(1)}, u32[]{:S(2)}, u32[]{:S(2)}) collective-permute-start(bf16[2,48,1280]{2,1,0:T(8,128)(2,1)} %get-tuple-element.83), channel_id=1, source_target_pairs={{0,5},{1,4},{2,7},{3,6},{4,1},{5,0},{6,3},{7,2},{8,13},{9,12},{10,... | collective-permute-start | bytes 737288 | tf_op jit(solution)/shard_map/ppermute | solution.py:426
  12.0 13.7 %all-to-all-start = ((s32[8,1,128]{2,1,0:T(1,128)}), s32[8,1,128]{2,1,0:T(1,128)S(1)}, u32[]{:S(2)}, u32[]{:S(2)}) async-start(s32[8,1,128]{2,1,0:T(1,128)} %bitcast.11), calls=%async_computation | async-start | bytes 8192 | tf_op jit(solution)/shard_map/all_to_all | solution.py:460
  16.0 9.6 %copy-start.11 = (bf16[2,48,1280]{2,1,0:T(8,128)(2,1)}, bf16[2,48,1280]{2,1,0:T(8,128)(2,1)S(1)}, u32[]{:S(2)}) copy-start(bf16[2,48,1280]{2,1,0:T(8,128)(2,1)S(1)} %collective-permute-done.refs_1_) | copy-start | bytes 737284
  16.0 9.7 %collective-permute-start.5 = (bf16[2,48,1280]{2,1,0:T(8,128)(2,1)}, bf16[2,48,1280]{2,1,0:T(8,128)(2,1)S(1)}, u32[]{:S(2)}, u32[]{:S(2)}) collective-permute-start(bf16[2,48,1280]{2,1,0:T(8,128)(2,1)} %get-tuple-element.84), channel_id=1, source_target_pairs={{0,6},{1,7},{2,4},{3,5},{4,2},{5,3},{6,0},{7,1},{8,14},{9,15},{10,... | collective-permute-start | bytes 737288 | tf_op jit(solution)/shard_map/ppermute | solution.py:426
  17.2 8.4 %copy-start.12 = (bf16[2,48,1280]{2,1,0:T(8,128)(2,1)}, bf16[2,48,1280]{2,1,0:T(8,128)(2,1)S(1)}, u32[]{:S(2)}) copy-start(bf16[2,48,1280]{2,1,0:T(8,128)(2,1)S(1)} %collective-permute-done.1.refs_2_) | copy-start | bytes 737284
  17.2 12.9 %collective-permute-start.6 = (bf16[2,48,1280]{2,1,0:T(8,128)(2,1)}, bf16[2,48,1280]{2,1,0:T(8,128)(2,1)S(1)}, u32[]{:S(2)}, u32[]{:S(2)}) collective-permute-start(bf16[2,48,1280]{2,1,0:T(8,128)(2,1)} %get-tuple-element.85), channel_id=1, source_target_pairs={{0,7},{1,6},{2,5},{3,4},{4,3},{5,2},{6,1},{7,0},{8,15},{9,14},{10,... | collective-permute-start | bytes 737288 | tf_op jit(solution)/shard_map/ppermute | solution.py:426
  25.7 5.2 %copy-start.13 = (bf16[2,48,1280]{2,1,0:T(8,128)(2,1)}, bf16[2,48,1280]{2,1,0:T(8,128)(2,1)S(1)}, u32[]{:S(2)}) copy-start(bf16[2,48,1280]{2,1,0:T(8,128)(2,1)S(1)} %collective-permute-done.2.refs_3_) | copy-start | bytes 737284
  25.7 5.1 %copy-start.14 = (bf16[2,48,1280]{2,1,0:T(8,128)(2,1)}, bf16[2,48,1280]{2,1,0:T(8,128)(2,1)S(1)}, u32[]{:S(2)}) copy-start(bf16[2,48,1280]{2,1,0:T(8,128)(2,1)S(1)} %collective-permute-done.3.refs_4_) | copy-start | bytes 737284
  25.7 5.1 %copy-start.15 = (bf16[2,48,1280]{2,1,0:T(8,128)(2,1)}, bf16[2,48,1280]{2,1,0:T(8,128)(2,1)S(1)}, u32[]{:S(2)}) copy-start(bf16[2,48,1280]{2,1,0:T(8,128)(2,1)S(1)} %collective-permute-done.4.refs_5_) | copy-start | bytes 737284
  25.7 4.4 %copy-start.16 = (bf16[2,48,1280]{2,1,0:T(8,128)(2,1)}, bf16[2,48,1280]{2,1,0:T(8,128)(2,1)S(1)}, u32[]{:S(2)}) copy-start(bf16[2,48,1280]{2,1,0:T(8,128)(2,1)S(1)} %collective-permute-done.5.refs_6_) | copy-start | bytes 737284
  30.1 0.7 copy-start.17
  30.8 23.0 %copy-start.3 = (f32[256,512]{1,0:T(8,128)S(1)}, f32[256,512]{1,0:T(8,128)}, u32[]{:S(2)}) copy-start(f32[256,512]{1,0:T(8,128)} %get-tuple-element.97.base_ref) | copy-start | bytes 1572868
  30.8 23.0 %copy-start.4 = (bf16[1024,256]{1,0:T(8,128)(2,1)S(1)}, bf16[1024,256]{1,0:T(8,128)(2,1)}, u32[]{:S(2)}) copy-start(bf16[1024,256]{1,0:T(8,128)(2,1)} %get-tuple-element.98.relay_ref) | copy-start | bytes 1572868
  30.8 23.0 %copy-start.6 = (bf16[256,768]{1,0:T(8,128)(2,1)S(1)}, bf16[256,768]{1,0:T(8,128)(2,1)}, u32[]{:S(2)}) copy-start(bf16[256,768]{1,0:T(8,128)(2,1)} %get-tuple-element.95.high_ref) | copy-start | bytes 1179652
  30.8 23.0 %copy-start.7 = (bf16[256,768]{1,0:T(8,128)(2,1)S(1)}, bf16[256,768]{1,0:T(8,128)(2,1)}, u32[]{:S(2)}) copy-start(bf16[256,768]{1,0:T(8,128)(2,1)} %get-tuple-element.96.low_ref) | copy-start | bytes 1179652
  40.2 23.6 %copy-start.10 = (bf16[512]{0:T(512)(128)(2,1)S(1)}, bf16[512]{0:T(512)(128)(2,1)}, u32[]{:S(2)}) copy-start(bf16[512]{0:T(512)(128)(2,1)} %param.22) | copy-start | bytes 3076
  40.2 31.6 %copy-start.9 = (f32[512]{0:T(512)S(1)}, f32[512]{0:T(512)}, u32[]{:S(2)}) copy-start(f32[512]{0:T(512)} %param.23) | copy-start | bytes 6148
  40.2 4.1 %collective-permute-start.7 = (bf16[2,48,512]{2,1,0:T(8,128)(2,1)}, bf16[2,48,512]{2,1,0:T(8,128)(2,1)S(1)}, u32[]{:S(2)}, u32[]{:S(2)}) collective-permute-start(bf16[2,48,512]{2,1,0:T(8,128)(2,1)} %get-tuple-element.109), channel_id=1, source_target_pairs={{0,1},{1,0},{2,3},{3,2},{4,5},{5,4},{6,7},{7,6},{8,9},{9,8},{10,11... | collective-permute-start | bytes 294920 | tf_op jit(solution)/shard_map/ppermute | solution.py:426
  40.3 5.1 %collective-permute-start.8 = (bf16[2,48,512]{2,1,0:T(8,128)(2,1)}, bf16[2,48,512]{2,1,0:T(8,128)(2,1)S(1)}, u32[]{:S(2)}, u32[]{:S(2)}) collective-permute-start(bf16[2,48,512]{2,1,0:T(8,128)(2,1)} %get-tuple-element.110), channel_id=1, source_target_pairs={{0,2},{1,3},{2,0},{3,1},{4,6},{5,7},{6,4},{7,5},{8,10},{9,11},{10,... | collective-permute-start | bytes 294920 | tf_op jit(solution)/shard_map/ppermute | solution.py:426
  41.8 5.9 %collective-permute-start.9 = (bf16[2,48,512]{2,1,0:T(8,128)(2,1)}, bf16[2,48,512]{2,1,0:T(8,128)(2,1)S(1)}, u32[]{:S(2)}, u32[]{:S(2)}) collective-permute-start(bf16[2,48,512]{2,1,0:T(8,128)(2,1)} %get-tuple-element.111), channel_id=1, source_target_pairs={{0,3},{1,2},{2,1},{3,0},{4,7},{5,6},{6,5},{7,4},{8,11},{9,10},{10,... | collective-permute-start | bytes 294920 | tf_op jit(solution)/shard_map/ppermute | solution.py:426
  42.8 4.9 %collective-permute-start.10 = (bf16[2,48,512]{2,1,0:T(8,128)(2,1)}, bf16[2,48,512]{2,1,0:T(8,128)(2,1)S(1)}, u32[]{:S(2)}, u32[]{:S(2)}) collective-permute-start(bf16[2,48,512]{2,1,0:T(8,128)(2,1)} %get-tuple-element.112), channel_id=1, source_target_pairs={{0,4},{1,5},{2,6},{3,7},{4,0},{5,1},{6,2},{7,3},{8,12},{9,13},{10,... | collective-permute-start | bytes 294920 | tf_op jit(solution)/shard_map/ppermute | solution.py:426
  42.9 10.9 %collective-permute-start.11 = (bf16[2,48,512]{2,1,0:T(8,128)(2,1)}, bf16[2,48,512]{2,1,0:T(8,128)(2,1)S(1)}, u32[]{:S(2)}, u32[]{:S(2)}) collective-permute-start(bf16[2,48,512]{2,1,0:T(8,128)(2,1)} %get-tuple-element.113), channel_id=1, source_target_pairs={{0,5},{1,4},{2,7},{3,6},{4,1},{5,0},{6,3},{7,2},{8,13},{9,12},{10,... | collective-permute-start | bytes 294920 | tf_op jit(solution)/shard_map/ppermute | solution.py:426
  44.3 9.5 %collective-permute-start.12 = (bf16[2,48,512]{2,1,0:T(8,128)(2,1)}, bf16[2,48,512]{2,1,0:T(8,128)(2,1)S(1)}, u32[]{:S(2)}, u32[]{:S(2)}) collective-permute-start(bf16[2,48,512]{2,1,0:T(8,128)(2,1)} %get-tuple-element.114), channel_id=1, source_target_pairs={{0,6},{1,7},{2,4},{3,5},{4,2},{5,3},{6,0},{7,1},{8,14},{9,15},{10,... | collective-permute-start | bytes 294920 | tf_op jit(solution)/shard_map/ppermute | solution.py:426
  45.4 8.4 %collective-permute-start.13 = (bf16[2,48,512]{2,1,0:T(8,128)(2,1)}, bf16[2,48,512]{2,1,0:T(8,128)(2,1)S(1)}, u32[]{:S(2)}, u32[]{:S(2)}) collective-permute-start(bf16[2,48,512]{2,1,0:T(8,128)(2,1)} %get-tuple-element.115), channel_id=1, source_target_pairs={{0,7},{1,6},{2,5},{3,4},{4,3},{5,2},{6,1},{7,0},{8,15},{9,14},{10,... | collective-permute-start | bytes 294920 | tf_op jit(solution)/shard_map/ppermute | solution.py:426
  53.9 0.9 copy-start.8
  55.8 4.2 %collective-permute-start.14 = (bf16[128,512]{1,0:T(8,128)(2,1)S(1)}, bf16[128,512]{1,0:T(8,128)(2,1)S(1)}, u32[]{:S(2)}, u32[]{:S(2)}) collective-permute-start(bf16[128,512]{1,0:T(8,128)(2,1)S(1)} %get-tuple-element.117), channel_id=1, source_target_pairs={{0,1},{1,0},{2,3},{3,2},{4,5},{5,4},{6,7},{7,6},{8,9},{9,8},{10,11... | collective-permute-start | bytes 393224 | tf_op jit(solution)/shard_map/ppermute | solution.py:426
  56.2 5.1 %collective-permute-start.15 = (bf16[128,512]{1,0:T(8,128)(2,1)S(1)}, bf16[128,512]{1,0:T(8,128)(2,1)S(1)}, u32[]{:S(2)}, u32[]{:S(2)}) collective-permute-start(bf16[128,512]{1,0:T(8,128)(2,1)S(1)} %get-tuple-element.118), channel_id=1, source_target_pairs={{0,2},{1,3},{2,0},{3,1},{4,6},{5,7},{6,4},{7,5},{8,10},{9,11},{10,... | collective-permute-start | bytes 393224 | tf_op jit(solution)/shard_map/ppermute | solution.py:426
  57.5 7.5 %collective-permute-start.16 = (bf16[128,512]{1,0:T(8,128)(2,1)S(1)}, bf16[128,512]{1,0:T(8,128)(2,1)S(1)}, u32[]{:S(2)}, u32[]{:S(2)}) collective-permute-start(bf16[128,512]{1,0:T(8,128)(2,1)S(1)} %get-tuple-element.119), channel_id=1, source_target_pairs={{0,3},{1,2},{2,1},{3,0},{4,7},{5,6},{6,5},{7,4},{8,11},{9,10},{10,... | collective-permute-start | bytes 393224 | tf_op jit(solution)/shard_map/ppermute | solution.py:426
  58.1 6.9 %collective-permute-start.17 = (bf16[128,512]{1,0:T(8,128)(2,1)S(1)}, bf16[128,512]{1,0:T(8,128)(2,1)S(1)}, u32[]{:S(2)}, u32[]{:S(2)}) collective-permute-start(bf16[128,512]{1,0:T(8,128)(2,1)S(1)} %get-tuple-element.120), channel_id=1, source_target_pairs={{0,4},{1,5},{2,6},{3,7},{4,0},{5,1},{6,2},{7,3},{8,12},{9,13},{10,... | collective-permute-start | bytes 393224 | tf_op jit(solution)/shard_map/ppermute | solution.py:426
  58.3 13.5 %collective-permute-start.18 = (bf16[128,512]{1,0:T(8,128)(2,1)S(1)}, bf16[128,512]{1,0:T(8,128)(2,1)S(1)}, u32[]{:S(2)}, u32[]{:S(2)}) collective-permute-start(bf16[128,512]{1,0:T(8,128)(2,1)S(1)} %get-tuple-element.121), channel_id=1, source_target_pairs={{0,5},{1,4},{2,7},{3,6},{4,1},{5,0},{6,3},{7,2},{8,13},{9,12},{10,... | collective-permute-start | bytes 393224 | tf_op jit(solution)/shard_map/ppermute | solution.py:426
  59.9 11.9 %collective-permute-start.19 = (bf16[128,512]{1,0:T(8,128)(2,1)S(1)}, bf16[128,512]{1,0:T(8,128)(2,1)S(1)}, u32[]{:S(2)}, u32[]{:S(2)}) collective-permute-start(bf16[128,512]{1,0:T(8,128)(2,1)S(1)} %get-tuple-element.122), channel_id=1, source_target_pairs={{0,6},{1,7},{2,4},{3,5},{4,2},{5,3},{6,0},{7,1},{8,14},{9,15},{10,... | collective-permute-start | bytes 393224 | tf_op jit(solution)/shard_map/ppermute | solution.py:426
  61.3 10.5 %collective-permute-start.20 = (bf16[128,512]{1,0:T(8,128)(2,1)S(1)}, bf16[128,512]{1,0:T(8,128)(2,1)S(1)}, u32[]{:S(2)}, u32[]{:S(2)}) collective-permute-start(bf16[128,512]{1,0:T(8,128)(2,1)S(1)} %get-tuple-element.123), channel_id=1, source_target_pairs={{0,7},{1,6},{2,5},{3,4},{4,3},{5,2},{6,1},{7,0},{8,15},{9,14},{10,... | collective-permute-start | bytes 393224 | tf_op jit(solution)/shard_map/ppermute | solution.py:426
  71.8 16.8 %copy-start = (bf16[512,1536]{1,0:T(8,128)(2,1)S(1)}, bf16[512,1536]{1,0:T(8,128)(2,1)}, u32[]{:S(2)}) copy-start(bf16[512,1536]{1,0:T(8,128)(2,1)} %wqkv_ref.3) | copy-start | bytes 4718596
  71.8 16.8 %copy-start.1 = (bf16[8,128,768]{2,1,0:T(8,128)(2,1)S(1)}, bf16[8,128,768]{2,1,0:T(8,128)(2,1)}, u32[]{:S(2)}) copy-start(bf16[8,128,768]{2,1,0:T(8,128)(2,1)} %pixels_ref.3) | copy-start | bytes 4718596
  71.8 16.8 %copy-start.2 = (bf16[512,768]{1,0:T(8,128)(2,1)S(1)}, bf16[512,768]{1,0:T(8,128)(2,1)}, u32[]{:S(2)}) copy-start(bf16[512,768]{1,0:T(8,128)(2,1)} %whead_ref.3) | copy-start | bytes 2359300
  71.8 16.8 %copy-start.5 = (bf16[512,512]{1,0:T(8,128)(2,1)S(1)}, bf16[512,512]{1,0:T(8,128)(2,1)}, u32[]{:S(2)}) copy-start(bf16[512,512]{1,0:T(8,128)(2,1)} %wout_ref.3) | copy-start | bytes 1572868
  73.7 5.2 %collective-permute-start.21 = (bf16[8,16,512]{2,1,0:T(8,128)(2,1)S(1)}, bf16[8,16,512]{2,1,0:T(8,128)(2,1)S(1)}, u32[]{:S(2)}, u32[]{:S(2)}) collective-permute-start(bf16[8,16,512]{2,1,0:T(8,128)(2,1)S(1)} %get-tuple-element.125), channel_id=1, source_target_pairs={{0,1},{1,2},{2,3},{3,4},{4,5},{5,6},{6,7},{8,9},{9,10},{10,11},{11... | collective-permute-start | bytes 393224 | tf_op jit(solution)/shard_map/ppermute | solution.py:499
  77.0 6.3 %collective-permute-start.22 = (bf16[8,16,512]{2,1,0:T(8,128)(2,1)S(1)}, bf16[8,16,512]{2,1,0:T(8,128)(2,1)S(1)}, u32[]{:S(2)}, u32[]{:S(2)}) collective-permute-start(bf16[8,16,512]{2,1,0:T(8,128)(2,1)S(1)} %get-tuple-element.126), channel_id=1, source_target_pairs={{1,0},{2,1},{3,2},{4,3},{5,4},{6,5},{7,6},{9,8},{10,9},{11,10},{12... | collective-permute-start | bytes 393224 | tf_op jit(solution)/shard_map/ppermute | solution.py:500
  83.3 14.3 %collective-permute-start.24 = (bf16[3,144,512]{2,1,0:T(8,128)(2,1)S(1)}, bf16[3,144,512]{2,1,0:T(8,128)(2,1)S(1)}, u32[]{:S(2)}, u32[]{:S(2)}) collective-permute-start(bf16[3,144,512]{2,1,0:T(8,128)(2,1)S(1)} %get-tuple-element.137), channel_id=1, source_target_pairs={{8,0},{16,8},{24,16},{9,1},{17,9},{25,17},{10,2},{18,10},{26,18},{... | collective-permute-start | bytes 1327112 | tf_op jit(solution)/shard_map/ppermute | solution.py:505
  85.4 13.8 %collective-permute-start.23 = (bf16[3,144,512]{2,1,0:T(8,128)(2,1)S(1)}, bf16[3,144,512]{2,1,0:T(8,128)(2,1)S(1)}, u32[]{:S(2)}, u32[]{:S(2)}) collective-permute-start(bf16[3,144,512]{2,1,0:T(8,128)(2,1)S(1)} %get-tuple-element.138), channel_id=1, source_target_pairs={{0,8},{8,16},{16,24},{1,9},{9,17},{17,25},{2,10},{10,18},{18,26},{... | collective-permute-start | bytes 1327112 | tf_op jit(solution)/shard_map/ppermute | solution.py:504

commit v3 on v2

--- a/solution.py
+++ b/solution.py
@@ -343,7 +343,7 @@
         over_ref[place] = over
         under_ref[place] = under
 
-    starts = [(2, r, 0, 0) for r in range(0, height, 2)]
+    starts = [(height // 2, r, 0, 0) for r in range(0, height, height // 2)]
     attention(q_ref, kv_ref, height, starts, grid_h, grid_w, height, breadth, keep_sums)
     att_ref[inner] = (over_ref[inner] * (1.0 / under_ref[inner])).astype(jnp.bfloat16)
     copy.wait()

time: 109 us -> 109 us (level)
  no operation moved by 1% of the time
where the time goes in v3:
time: 109 us
  Pallas kernels  44.5 us (41%)
  starting transfers between devices  36.5 us (33%)
  waiting for transfers between devices  24.5 us (22%)
  local copies, waits for them, and re-layouts  1.69 us (2%)
    pallas_call x6, Pallas kernels, whole_call(): pl.pallas_call(kernel, out_shape=tuple(outs), in_specs=[VM] * (len(ins) -...  28.5 us
    ppermute x21, starting transfers between devices, swap(): lax.ppermute(value, 'expert', [(i, i ^ k) for i in range(groups)])  22 us
    ppermute x21, waiting for transfers between devices, swap(): lax.ppermute(value, 'expert', [(i, i ^ k) for i in range(groups)])  18.7 us
    pallas_call x1, Pallas kernels, experts_apply(): pl.pallas_call(functools.partial(ffn_kernel, sources), grid=(local_expert...  9.32 us
    pallas_call x1, Pallas kernels, fold(): pl.pallas_call(fold_kernel, grid=(local_experts, hidden // chunk), out_sh...  6.67 us
    ppermute x1, waiting for transfers between devices, local(): lax.ppermute(first, 'expert', [(i + 1, i) for i in range(groups - 1)])  4.33 us
    all_to_all x1, starting transfers between devices, local(): lax.all_to_all(spots, 'expert', split_axis=0, concat_axis=0, tiled=True)  3.98 us
    ppermute x1, starting transfers between devices, local(): lax.ppermute(last, 'expert', [(i, i + 1) for i in range(groups - 1)])  3.28 us
  transfers between devices with their start and end apart: 26, of which 7 were waited for; matrix products, arithmetic and copies ran while one was open for 0% of the time, Pallas kernels for 18%

profile of v3, /device:TPU:13, one launch (start us, length us, event | category | flops | bytes accessed | tf_op | source)
XLA Modules:
  0.0 108.8 jit_solution(12912952142923211133)
XLA Ops:
  0.6 3.3 %pack.1 = (bf16[2,48,1280]{2,1,0:T(8,128)(2,1)}, bf16[2,48,1280]{2,1,0:T(8,128)(2,1)}, bf16[2,48,1280]{2,1,0:T(8,128)(2,1)}, bf16[2,48,1280]{2,1,0:T(8,128)(2,1)...) custom-call(s32[2,256]{1,0:T(2,128)} %bitcast.12, ...), custom_call_target="tpu_custom_call" | custom-call | flops 503316480 | bytes 2623488 | tf_op jit(solution)/shard_map/pack/pallas_call | solution.py:203
  4.0 0.7 collective-permute-start
  4.7 1.2 %collective-permute-start.1 = (bf16[2,48,1280]{2,1,0:T(8,128)(2,1)}, bf16[2,48,1280]{2,1,0:T(8,128)(2,1)S(1)}, u32[]{:S(2)}, u32[]{:S(2)}) collective-permute-start(bf16[2,48,1280]{2,1,0:T(8,128)(2,1)} %get-tuple-element.80), channel_id=1, source_target_pairs={{0,2},{1,3},{2,0},{3,1},{4,6},{5,7},{6,4},{7,5},{8,10},{9,11},{10,... | collective-permute-start | bytes 737288 | tf_op jit(solution)/shard_map/ppermute | solution.py:426
  5.9 0.4 collective-permute-start.2
  6.3 0.2 collective-permute-start.3
  6.5 1.6 %collective-permute-start.4 = (bf16[2,48,1280]{2,1,0:T(8,128)(2,1)}, bf16[2,48,1280]{2,1,0:T(8,128)(2,1)S(1)}, u32[]{:S(2)}, u32[]{:S(2)}) collective-permute-start(bf16[2,48,1280]{2,1,0:T(8,128)(2,1)} %get-tuple-element.83), channel_id=1, source_target_pairs={{0,5},{1,4},{2,7},{3,6},{4,1},{5,0},{6,3},{7,2},{8,13},{9,12},{10,... | collective-permute-start | bytes 737288 | tf_op jit(solution)/shard_map/ppermute | solution.py:426
  8.1 3.8 %prep.1 = (bf16[256,768]{1,0:T(8,128)(2,1)}, bf16[256,768]{1,0:T(8,128)(2,1)}, f32[256,512]{1,0:T(8,128)}, bf16[1024,256]{1,0:T(8,128)(2,1)}, s32[8,128]{1,0:T(8,128)}) custom-call(s32[2,256]{1,0:T(2,128)} %bitcast.13, f32[2,256]{1,0:T(2,128)} %bitcast.14, s32[1,256]{1,0:T(1,128)} %bitcast.15, bf16[256,1280]{1,0:T(8,128)(2,1)} %tokens_ref.2, ...), custom_call_target="tpu_custom_call" | custom-call | flops 335544320 | bytes 3810304 | tf_op jit(solution)/shard_map/prep/pallas_call | solution.py:203
  12.0 4.0 %all-to-all-start = ((s32[8,1,128]{2,1,0:T(1,128)}), s32[8,1,128]{2,1,0:T(1,128)S(1)}, u32[]{:S(2)}, u32[]{:S(2)}) async-start(s32[8,1,128]{2,1,0:T(1,128)} %bitcast.11), calls=%async_computation | async-start | bytes 8192 | tf_op jit(solution)/shard_map/all_to_all | solution.py:460
  16.0 1.2 %collective-permute-start.5 = (bf16[2,48,1280]{2,1,0:T(8,128)(2,1)}, bf16[2,48,1280]{2,1,0:T(8,128)(2,1)S(1)}, u32[]{:S(2)}, u32[]{:S(2)}) collective-permute-start(bf16[2,48,1280]{2,1,0:T(8,128)(2,1)} %get-tuple-element.84), channel_id=1, source_target_pairs={{0,6},{1,7},{2,4},{3,5},{4,2},{5,3},{6,0},{7,1},{8,14},{9,15},{10,... | collective-permute-start | bytes 737288 | tf_op jit(solution)/shard_map/ppermute | solution.py:426
  17.2 1.7 %collective-permute-start.6 = (bf16[2,48,1280]{2,1,0:T(8,128)(2,1)}, bf16[2,48,1280]{2,1,0:T(8,128)(2,1)S(1)}, u32[]{:S(2)}, u32[]{:S(2)}) collective-permute-start(bf16[2,48,1280]{2,1,0:T(8,128)(2,1)} %get-tuple-element.85), channel_id=1, source_target_pairs={{0,7},{1,6},{2,5},{3,4},{4,3},{5,2},{6,1},{7,0},{8,15},{9,14},{10,... | collective-permute-start | bytes 737288 | tf_op jit(solution)/shard_map/ppermute | solution.py:426
  18.9 6.7 %fold.1.refs_10_ = bf16[2,1024,512]{2,1,0:T(8,128)(2,1)} custom-call(bf16[2,1024,1280]{2,1,0:T(8,128)(2,1)} %down_ref, bf16[1280,512]{1,0:T(8,128)(2,1)} %embed_ref.3), custom_call_target="tpu_custom_call" | custom-call | flops 2684354560 | bytes 5242880 | tf_op jit(solution)/shard_map/fold/pallas_call | solution.py:123
  25.7 4.4 %collective-permute-done.6.refs_7_ = bf16[2,48,1280]{2,1,0:T(8,128)(2,1)S(1)} collective-permute-done((bf16[2,48,1280]{2,1,0:T(8,128)(2,1)}, bf16[2,48,1280]{2,1,0:T(8,128)(2,1)S(1)}, u32[]{:S(2)}, u32[]{:S(2)}) %collective-permute-start.6) | collective-permute-done | bytes 245792 | tf_op jit(solution)/shard_map/ppermute | solution.py:426
  30.1 0.7 copy-done.17
  30.9 9.3 %experts.1 = (bf16[2,48,512]{2,1,0:T(8,128)(2,1)}, bf16[2,48,512]{2,1,0:T(8,128)(2,1)}, bf16[2,48,512]{2,1,0:T(8,128)(2,1)}, bf16[2,48,512]{2,1,0:T(8,128)(2,1)}...) custom-call(bf16[2,48,1280]{2,1,0:T(8,128)(2,1)} %get-tuple-element., ...), custom_call_target="tpu_custom_call" | custom-call | flops 4831838208 | bytes 12582912 | tf_op jit(solution)/shard_map/experts/pallas_call | solution.py:225
  40.2 0.0 copy-start.10
  40.2 0.1 collective-permute-start.7
  40.3 1.2 %collective-permute-start.8 = (bf16[2,48,512]{2,1,0:T(8,128)(2,1)}, bf16[2,48,512]{2,1,0:T(8,128)(2,1)S(1)}, u32[]{:S(2)}, u32[]{:S(2)}) collective-permute-start(bf16[2,48,512]{2,1,0:T(8,128)(2,1)} %get-tuple-element.110), channel_id=1, source_target_pairs={{0,2},{1,3},{2,0},{3,1},{4,6},{5,7},{6,4},{7,5},{8,10},{9,11},{10,... | collective-permute-start | bytes 294920 | tf_op jit(solution)/shard_map/ppermute | solution.py:426
  41.5 0.3 multiply_sine_fusion
  41.8 0.9 collective-permute-start.9
  42.8 0.2 collective-permute-start.10
  42.9 1.4 %collective-permute-start.11 = (bf16[2,48,512]{2,1,0:T(8,128)(2,1)}, bf16[2,48,512]{2,1,0:T(8,128)(2,1)S(1)}, u32[]{:S(2)}, u32[]{:S(2)}) collective-permute-start(bf16[2,48,512]{2,1,0:T(8,128)(2,1)} %get-tuple-element.113), channel_id=1, source_target_pairs={{0,5},{1,4},{2,7},{3,6},{4,1},{5,0},{6,3},{7,2},{8,13},{9,12},{10,... | collective-permute-start | bytes 294920 | tf_op jit(solution)/shard_map/ppermute | solution.py:426
  44.3 1.1 collective-permute-start.12
  45.4 2.3 %collective-permute-start.13 = (bf16[2,48,512]{2,1,0:T(8,128)(2,1)}, bf16[2,48,512]{2,1,0:T(8,128)(2,1)S(1)}, u32[]{:S(2)}, u32[]{:S(2)}) collective-permute-start(bf16[2,48,512]{2,1,0:T(8,128)(2,1)} %get-tuple-element.115), channel_id=1, source_target_pairs={{0,7},{1,6},{2,5},{3,4},{4,3},{5,2},{6,1},{7,0},{8,15},{9,14},{10,... | collective-permute-start | bytes 294920 | tf_op jit(solution)/shard_map/ppermute | solution.py:426
  47.7 6.1 %collective-permute-done.11.refs_5_ = bf16[2,48,512]{2,1,0:T(8,128)(2,1)S(1)} collective-permute-done((bf16[2,48,512]{2,1,0:T(8,128)(2,1)}, bf16[2,48,512]{2,1,0:T(8,128)(2,1)S(1)}, u32[]{:S(2)}, u32[]{:S(2)}) %collective-permute-start.11) | collective-permute-done | bytes 98336 | tf_op jit(solution)/shard_map/ppermute | solution.py:426
  53.9 0.9 copy-done.8
  54.8 1.0 combine.1
  55.8 0.5 collective-permute-start.14
  56.2 1.2 %collective-permute-start.15 = (bf16[128,512]{1,0:T(8,128)(2,1)S(1)}, bf16[128,512]{1,0:T(8,128)(2,1)S(1)}, u32[]{:S(2)}, u32[]{:S(2)}) collective-permute-start(bf16[128,512]{1,0:T(8,128)(2,1)S(1)} %get-tuple-element.118), channel_id=1, source_target_pairs={{0,2},{1,3},{2,0},{3,1},{4,6},{5,7},{6,4},{7,5},{8,10},{9,11},{10,... | collective-permute-start | bytes 393224 | tf_op jit(solution)/shard_map/ppermute | solution.py:426
  57.4 0.1 multiply_sine_fusion.1
  57.5 0.6 collective-permute-start.16
  58.1 0.2 collective-permute-start.17
  58.3 1.6 %collective-permute-start.18 = (bf16[128,512]{1,0:T(8,128)(2,1)S(1)}, bf16[128,512]{1,0:T(8,128)(2,1)S(1)}, u32[]{:S(2)}, u32[]{:S(2)}) collective-permute-start(bf16[128,512]{1,0:T(8,128)(2,1)S(1)} %get-tuple-element.121), channel_id=1, source_target_pairs={{0,5},{1,4},{2,7},{3,6},{4,1},{5,0},{6,3},{7,2},{8,13},{9,12},{10,... | collective-permute-start | bytes 393224 | tf_op jit(solution)/shard_map/ppermute | solution.py:426
  59.9 1.2 %collective-permute-start.19 = (bf16[128,512]{1,0:T(8,128)(2,1)S(1)}, bf16[128,512]{1,0:T(8,128)(2,1)S(1)}, u32[]{:S(2)}, u32[]{:S(2)}) collective-permute-start(bf16[128,512]{1,0:T(8,128)(2,1)S(1)} %get-tuple-element.122), channel_id=1, source_target_pairs={{0,6},{1,7},{2,4},{3,5},{4,2},{5,3},{6,0},{7,1},{8,14},{9,15},{10,... | collective-permute-start | bytes 393224 | tf_op jit(solution)/shard_map/ppermute | solution.py:426
  61.2 0.1 collective-permute-done.15.refs_2_
  61.3 2.4 %collective-permute-start.20 = (bf16[128,512]{1,0:T(8,128)(2,1)S(1)}, bf16[128,512]{1,0:T(8,128)(2,1)S(1)}, u32[]{:S(2)}, u32[]{:S(2)}) collective-permute-start(bf16[128,512]{1,0:T(8,128)(2,1)S(1)} %get-tuple-element.123), channel_id=1, source_target_pairs={{0,7},{1,6},{2,5},{3,4},{4,3},{5,2},{6,1},{7,0},{8,15},{9,14},{10,... | collective-permute-start | bytes 393224 | tf_op jit(solution)/shard_map/ppermute | solution.py:426
  63.8 1.3 %collective-permute-done.16.refs_3_ = bf16[128,512]{1,0:T(8,128)(2,1)S(1)} collective-permute-done((bf16[128,512]{1,0:T(8,128)(2,1)S(1)}, bf16[128,512]{1,0:T(8,128)(2,1)S(1)}, u32[]{:S(2)}, u32[]{:S(2)}) %collective-permute-start.16) | collective-permute-done | bytes 131104 | tf_op jit(solution)/shard_map/ppermute | solution.py:426
  65.0 6.7 %collective-permute-done.18.refs_5_ = bf16[128,512]{1,0:T(8,128)(2,1)S(1)} collective-permute-done((bf16[128,512]{1,0:T(8,128)(2,1)S(1)}, bf16[128,512]{1,0:T(8,128)(2,1)S(1)}, u32[]{:S(2)}, u32[]{:S(2)}) %collective-permute-start.18) | collective-permute-done | bytes 131104 | tf_op jit(solution)/shard_map/ppermute | solution.py:426
  71.8 0.0 copy-start.1
  71.8 1.8 %place.1 = (bf16[8,128,512]{2,1,0:T(8,128)(2,1)S(1)}, f32[8,128,512]{2,1,0:T(8,128)S(1)}, f32[8,128,1]{2,1,0:T(8,128)S(1)}, bf16[3,128,512]{2,1,0:T(8,128)(2,1)S...) custom-call(s32[8,128]{1,0:T(8,128)S(1)} %bitcast.9, ...), custom_call_target="tpu_custom_call" | custom-call | flops 1073741824 | bytes 5393408 | tf_op jit(solution)/shard_map/place/pallas_call | solution.py:203
  73.7 3.3 %collective-permute-start.21 = (bf16[8,16,512]{2,1,0:T(8,128)(2,1)S(1)}, bf16[8,16,512]{2,1,0:T(8,128)(2,1)S(1)}, u32[]{:S(2)}, u32[]{:S(2)}) collective-permute-start(bf16[8,16,512]{2,1,0:T(8,128)(2,1)S(1)} %get-tuple-element.125), channel_id=1, source_target_pairs={{0,1},{1,2},{2,3},{3,4},{4,5},{5,6},{6,7},{8,9},{9,10},{10,11},{11... | collective-permute-start | bytes 393224 | tf_op jit(solution)/shard_map/ppermute | solution.py:499
  77.0 1.9 %collective-permute-start.22 = (bf16[8,16,512]{2,1,0:T(8,128)(2,1)S(1)}, bf16[8,16,512]{2,1,0:T(8,128)(2,1)S(1)}, u32[]{:S(2)}, u32[]{:S(2)}) collective-permute-start(bf16[8,16,512]{2,1,0:T(8,128)(2,1)S(1)} %get-tuple-element.126), channel_id=1, source_target_pairs={{1,0},{2,1},{3,2},{4,3},{5,4},{6,5},{7,6},{9,8},{10,9},{11,10},{12... | collective-permute-start | bytes 393224 | tf_op jit(solution)/shard_map/ppermute | solution.py:500
  78.9 4.3 %collective-permute-done.22.after_ref = bf16[8,16,512]{2,1,0:T(8,128)(2,1)S(1)} collective-permute-done((bf16[8,16,512]{2,1,0:T(8,128)(2,1)S(1)}, bf16[8,16,512]{2,1,0:T(8,128)(2,1)S(1)}, u32[]{:S(2)}, u32[]{:S(2)}) %collective-permute-start.22) | collective-permute-done | bytes 131104 | tf_op jit(solution)/shard_map/ppermute | solution.py:500
  83.3 0.1 fusion
  83.3 2.1 %collective-permute-start.24 = (bf16[3,144,512]{2,1,0:T(8,128)(2,1)S(1)}, bf16[3,144,512]{2,1,0:T(8,128)(2,1)S(1)}, u32[]{:S(2)}, u32[]{:S(2)}) collective-permute-start(bf16[3,144,512]{2,1,0:T(8,128)(2,1)S(1)} %get-tuple-element.137), channel_id=1, source_target_pairs={{8,0},{16,8},{24,16},{9,1},{17,9},{25,17},{10,2},{18,10},{26,18},{... | collective-permute-start | bytes 1327112 | tf_op jit(solution)/shard_map/ppermute | solution.py:505
  85.4 3.2 %collective-permute-start.23 = (bf16[3,144,512]{2,1,0:T(8,128)(2,1)S(1)}, bf16[3,144,512]{2,1,0:T(8,128)(2,1)S(1)}, u32[]{:S(2)}, u32[]{:S(2)}) collective-permute-start(bf16[3,144,512]{2,1,0:T(8,128)(2,1)S(1)} %get-tuple-element.138), channel_id=1, source_target_pairs={{0,8},{8,16},{16,24},{1,9},{9,17},{17,25},{2,10},{10,18},{18,26},{... | collective-permute-start | bytes 1327112 | tf_op jit(solution)/shard_map/ppermute | solution.py:504
  88.7 9.0 %inner.1 = (bf16[8,128,512]{2,1,0:T(8,128)(2,1)S(1)}, f32[8,128,512]{2,1,0:T(8,128)S(1)}, f32[8,128,512]{2,1,0:T(8,128)S(1)}, bf16[2,128,512]{2,1,0:T(8,128)(2,1...) custom-call(bf16[8,128,512]{2,1,0:T(8,128)(2,1)S(1)} %get-tuple-element.128.normed_ref, ...), custom_call_target="tpu_custom_call" | custom-call | flops 2684354560 | bytes 13635588 | tf_op jit(solution)/shard_map/inner/pallas_call | solution.py:203
  97.7 1.5 %collective-permute-done.23.up_ref = bf16[3,144,512]{2,1,0:T(8,128)(2,1)S(1)} collective-permute-done((bf16[3,144,512]{2,1,0:T(8,128)(2,1)S(1)}, bf16[3,144,512]{2,1,0:T(8,128)(2,1)S(1)}, u32[]{:S(2)}, u32[]{:S(2)}) %collective-permute-start.23) | collective-permute-done | bytes 442400 | tf_op jit(solution)/shard_map/ppermute | solution.py:504
  99.3 9.5 %outer.1 = (bf16[8,128,512]{2,1,0:T(8,128)(2,1)}, bf16[8,128,512]{2,1,0:T(8,128)(2,1)}, f32[1,1]{1,0:T(1,128)}) custom-call(bf16[3,144,512]{2,1,0:T(8,128)(2,1)S(1)} %collective-permute-done.23.up_ref, bf16[3,144,512]{2,1,0:T(8,128)(2,1)S(1)} %collective-permute-done.24.down_ref, bf16[8,128,512]{2,1,0:T(8,128)(2,1)S(1)} %get-tuple-element.131.q_ref, ...), custom_call_target="tpu_custom_call" | custom-call | flops 3221225472 | bytes 15306760 | tf_op jit(solution)/shard_map/outer/pallas_call | solution.py:203
  (59 shorter events, 0.2 us)
Async XLA Ops:
  4.0 12.0 %collective-permute-start = (bf16[2,48,1280]{2,1,0:T(8,128)(2,1)}, bf16[2,48,1280]{2,1,0:T(8,128)(2,1)S(1)}, u32[]{:S(2)}, u32[]{:S(2)}) collective-permute-start(bf16[2,48,1280]{2,1,0:T(8,128)(2,1)} %get-tuple-element.79), channel_id=1, source_target_pairs={{0,1},{1,0},{2,3},{3,2},{4,5},{5,4},{6,7},{7,6},{8,9},{9,8},{10,11... | collective-permute-start | bytes 737288 | tf_op jit(solution)/shard_map/ppermute | solution.py:426
  4.7 12.6 %collective-permute-start.1 = (bf16[2,48,1280]{2,1,0:T(8,128)(2,1)}, bf16[2,48,1280]{2,1,0:T(8,128)(2,1)S(1)}, u32[]{:S(2)}, u32[]{:S(2)}) collective-permute-start(bf16[2,48,1280]{2,1,0:T(8,128)(2,1)} %get-tuple-element.80), channel_id=1, source_target_pairs={{0,2},{1,3},{2,0},{3,1},{4,6},{5,7},{6,4},{7,5},{8,10},{9,11},{10,... | collective-permute-start | bytes 737288 | tf_op jit(solution)/shard_map/ppermute | solution.py:426
  5.9 19.8 %collective-permute-start.2 = (bf16[2,48,1280]{2,1,0:T(8,128)(2,1)}, bf16[2,48,1280]{2,1,0:T(8,128)(2,1)S(1)}, u32[]{:S(2)}, u32[]{:S(2)}) collective-permute-start(bf16[2,48,1280]{2,1,0:T(8,128)(2,1)} %get-tuple-element.81), channel_id=1, source_target_pairs={{0,3},{1,2},{2,1},{3,0},{4,7},{5,6},{6,5},{7,4},{8,11},{9,10},{10,... | collective-permute-start | bytes 737288 | tf_op jit(solution)/shard_map/ppermute | solution.py:426
  6.3 19.4 %collective-permute-start.3 = (bf16[2,48,1280]{2,1,0:T(8,128)(2,1)}, bf16[2,48,1280]{2,1,0:T(8,128)(2,1)S(1)}, u32[]{:S(2)}, u32[]{:S(2)}) collective-permute-start(bf16[2,48,1280]{2,1,0:T(8,128)(2,1)} %get-tuple-element.82), channel_id=1, source_target_pairs={{0,4},{1,5},{2,6},{3,7},{4,0},{5,1},{6,2},{7,3},{8,12},{9,13},{10,... | collective-permute-start | bytes 737288 | tf_op jit(solution)/shard_map/ppermute | solution.py:426
  6.5 19.2 %collective-permute-start.4 = (bf16[2,48,1280]{2,1,0:T(8,128)(2,1)}, bf16[2,48,1280]{2,1,0:T(8,128)(2,1)S(1)}, u32[]{:S(2)}, u32[]{:S(2)}) collective-permute-start(bf16[2,48,1280]{2,1,0:T(8,128)(2,1)} %get-tuple-element.83), channel_id=1, source_target_pairs={{0,5},{1,4},{2,7},{3,6},{4,1},{5,0},{6,3},{7,2},{8,13},{9,12},{10,... | collective-permute-start | bytes 737288 | tf_op jit(solution)/shard_map/ppermute | solution.py:426
  12.0 13.7 %all-to-all-start = ((s32[8,1,128]{2,1,0:T(1,128)}), s32[8,1,128]{2,1,0:T(1,128)S(1)}, u32[]{:S(2)}, u32[]{:S(2)}) async-start(s32[8,1,128]{2,1,0:T(1,128)} %bitcast.11), calls=%async_computation | async-start | bytes 8192 | tf_op jit(solution)/shard_map/all_to_all | solution.py:460
  16.0 9.6 %copy-start.11 = (bf16[2,48,1280]{2,1,0:T(8,128)(2,1)}, bf16[2,48,1280]{2,1,0:T(8,128)(2,1)S(1)}, u32[]{:S(2)}) copy-start(bf16[2,48,1280]{2,1,0:T(8,128)(2,1)S(1)} %collective-permute-done.refs_1_) | copy-start | bytes 737284
  16.0 9.7 %collective-permute-start.5 = (bf16[2,48,1280]{2,1,0:T(8,128)(2,1)}, bf16[2,48,1280]{2,1,0:T(8,128)(2,1)S(1)}, u32[]{:S(2)}, u32[]{:S(2)}) collective-permute-start(bf16[2,48,1280]{2,1,0:T(8,128)(2,1)} %get-tuple-element.84), channel_id=1, source_target_pairs={{0,6},{1,7},{2,4},{3,5},{4,2},{5,3},{6,0},{7,1},{8,14},{9,15},{10,... | collective-permute-start | bytes 737288 | tf_op jit(solution)/shard_map/ppermute | solution.py:426
  17.2 8.4 %copy-start.12 = (bf16[2,48,1280]{2,1,0:T(8,128)(2,1)}, bf16[2,48,1280]{2,1,0:T(8,128)(2,1)S(1)}, u32[]{:S(2)}) copy-start(bf16[2,48,1280]{2,1,0:T(8,128)(2,1)S(1)} %collective-permute-done.1.refs_2_) | copy-start | bytes 737284
  17.2 12.9 %collective-permute-start.6 = (bf16[2,48,1280]{2,1,0:T(8,128)(2,1)}, bf16[2,48,1280]{2,1,0:T(8,128)(2,1)S(1)}, u32[]{:S(2)}, u32[]{:S(2)}) collective-permute-start(bf16[2,48,1280]{2,1,0:T(8,128)(2,1)} %get-tuple-element.85), channel_id=1, source_target_pairs={{0,7},{1,6},{2,5},{3,4},{4,3},{5,2},{6,1},{7,0},{8,15},{9,14},{10,... | collective-permute-start | bytes 737288 | tf_op jit(solution)/shard_map/ppermute | solution.py:426
  25.7 5.2 %copy-start.13 = (bf16[2,48,1280]{2,1,0:T(8,128)(2,1)}, bf16[2,48,1280]{2,1,0:T(8,128)(2,1)S(1)}, u32[]{:S(2)}) copy-start(bf16[2,48,1280]{2,1,0:T(8,128)(2,1)S(1)} %collective-permute-done.2.refs_3_) | copy-start | bytes 737284
  25.7 5.1 %copy-start.14 = (bf16[2,48,1280]{2,1,0:T(8,128)(2,1)}, bf16[2,48,1280]{2,1,0:T(8,128)(2,1)S(1)}, u32[]{:S(2)}) copy-start(bf16[2,48,1280]{2,1,0:T(8,128)(2,1)S(1)} %collective-permute-done.3.refs_4_) | copy-start | bytes 737284
  25.7 5.1 %copy-start.15 = (bf16[2,48,1280]{2,1,0:T(8,128)(2,1)}, bf16[2,48,1280]{2,1,0:T(8,128)(2,1)S(1)}, u32[]{:S(2)}) copy-start(bf16[2,48,1280]{2,1,0:T(8,128)(2,1)S(1)} %collective-permute-done.4.refs_5_) | copy-start | bytes 737284
  25.7 4.4 %copy-start.16 = (bf16[2,48,1280]{2,1,0:T(8,128)(2,1)}, bf16[2,48,1280]{2,1,0:T(8,128)(2,1)S(1)}, u32[]{:S(2)}) copy-start(bf16[2,48,1280]{2,1,0:T(8,128)(2,1)S(1)} %collective-permute-done.5.refs_6_) | copy-start | bytes 737284
  30.1 0.7 copy-start.17
  30.8 23.0 %copy-start.3 = (f32[256,512]{1,0:T(8,128)S(1)}, f32[256,512]{1,0:T(8,128)}, u32[]{:S(2)}) copy-start(f32[256,512]{1,0:T(8,128)} %get-tuple-element.97.base_ref) | copy-start | bytes 1572868
  30.8 23.0 %copy-start.4 = (bf16[1024,256]{1,0:T(8,128)(2,1)S(1)}, bf16[1024,256]{1,0:T(8,128)(2,1)}, u32[]{:S(2)}) copy-start(bf16[1024,256]{1,0:T(8,128)(2,1)} %get-tuple-element.98.relay_ref) | copy-start | bytes 1572868
  30.8 23.0 %copy-start.6 = (bf16[256,768]{1,0:T(8,128)(2,1)S(1)}, bf16[256,768]{1,0:T(8,128)(2,1)}, u32[]{:S(2)}) copy-start(bf16[256,768]{1,0:T(8,128)(2,1)} %get-tuple-element.95.high_ref) | copy-start | bytes 1179652
  30.8 23.0 %copy-start.7 = (bf16[256,768]{1,0:T(8,128)(2,1)S(1)}, bf16[256,768]{1,0:T(8,128)(2,1)}, u32[]{:S(2)}) copy-start(bf16[256,768]{1,0:T(8,128)(2,1)} %get-tuple-element.96.low_ref) | copy-start | bytes 1179652
  40.2 23.6 %copy-start.10 = (bf16[512]{0:T(512)(128)(2,1)S(1)}, bf16[512]{0:T(512)(128)(2,1)}, u32[]{:S(2)}) copy-start(bf16[512]{0:T(512)(128)(2,1)} %param.22) | copy-start | bytes 3076
  40.2 31.6 %copy-start.9 = (f32[512]{0:T(512)S(1)}, f32[512]{0:T(512)}, u32[]{:S(2)}) copy-start(f32[512]{0:T(512)} %param.23) | copy-start | bytes 6148
  40.2 4.1 %collective-permute-start.7 = (bf16[2,48,512]{2,1,0:T(8,128)(2,1)}, bf16[2,48,512]{2,1,0:T(8,128)(2,1)S(1)}, u32[]{:S(2)}, u32[]{:S(2)}) collective-permute-start(bf16[2,48,512]{2,1,0:T(8,128)(2,1)} %get-tuple-element.109), channel_id=1, source_target_pairs={{0,1},{1,0},{2,3},{3,2},{4,5},{5,4},{6,7},{7,6},{8,9},{9,8},{10,11... | collective-permute-start | bytes 294920 | tf_op jit(solution)/shard_map/ppermute | solution.py:426
  40.3 5.1 %collective-permute-start.8 = (bf16[2,48,512]{2,1,0:T(8,128)(2,1)}, bf16[2,48,512]{2,1,0:T(8,128)(2,1)S(1)}, u32[]{:S(2)}, u32[]{:S(2)}) collective-permute-start(bf16[2,48,512]{2,1,0:T(8,128)(2,1)} %get-tuple-element.110), channel_id=1, source_target_pairs={{0,2},{1,3},{2,0},{3,1},{4,6},{5,7},{6,4},{7,5},{8,10},{9,11},{10,... | collective-permute-start | bytes 294920 | tf_op jit(solution)/shard_map/ppermute | solution.py:426
  41.8 5.9 %collective-permute-start.9 = (bf16[2,48,512]{2,1,0:T(8,128)(2,1)}, bf16[2,48,512]{2,1,0:T(8,128)(2,1)S(1)}, u32[]{:S(2)}, u32[]{:S(2)}) collective-permute-start(bf16[2,48,512]{2,1,0:T(8,128)(2,1)} %get-tuple-element.111), channel_id=1, source_target_pairs={{0,3},{1,2},{2,1},{3,0},{4,7},{5,6},{6,5},{7,4},{8,11},{9,10},{10,... | collective-permute-start | bytes 294920 | tf_op jit(solution)/shard_map/ppermute | solution.py:426
  42.8 4.9 %collective-permute-start.10 = (bf16[2,48,512]{2,1,0:T(8,128)(2,1)}, bf16[2,48,512]{2,1,0:T(8,128)(2,1)S(1)}, u32[]{:S(2)}, u32[]{:S(2)}) collective-permute-start(bf16[2,48,512]{2,1,0:T(8,128)(2,1)} %get-tuple-element.112), channel_id=1, source_target_pairs={{0,4},{1,5},{2,6},{3,7},{4,0},{5,1},{6,2},{7,3},{8,12},{9,13},{10,... | collective-permute-start | bytes 294920 | tf_op jit(solution)/shard_map/ppermute | solution.py:426
  42.9 10.9 %collective-permute-start.11 = (bf16[2,48,512]{2,1,0:T(8,128)(2,1)}, bf16[2,48,512]{2,1,0:T(8,128)(2,1)S(1)}, u32[]{:S(2)}, u32[]{:S(2)}) collective-permute-start(bf16[2,48,512]{2,1,0:T(8,128)(2,1)} %get-tuple-element.113), channel_id=1, source_target_pairs={{0,5},{1,4},{2,7},{3,6},{4,1},{5,0},{6,3},{7,2},{8,13},{9,12},{10,... | collective-permute-start | bytes 294920 | tf_op jit(solution)/shard_map/ppermute | solution.py:426
  44.3 9.5 %collective-permute-start.12 = (bf16[2,48,512]{2,1,0:T(8,128)(2,1)}, bf16[2,48,512]{2,1,0:T(8,128)(2,1)S(1)}, u32[]{:S(2)}, u32[]{:S(2)}) collective-permute-start(bf16[2,48,512]{2,1,0:T(8,128)(2,1)} %get-tuple-element.114), channel_id=1, source_target_pairs={{0,6},{1,7},{2,4},{3,5},{4,2},{5,3},{6,0},{7,1},{8,14},{9,15},{10,... | collective-permute-start | bytes 294920 | tf_op jit(solution)/shard_map/ppermute | solution.py:426
  45.4 8.4 %collective-permute-start.13 = (bf16[2,48,512]{2,1,0:T(8,128)(2,1)}, bf16[2,48,512]{2,1,0:T(8,128)(2,1)S(1)}, u32[]{:S(2)}, u32[]{:S(2)}) collective-permute-start(bf16[2,48,512]{2,1,0:T(8,128)(2,1)} %get-tuple-element.115), channel_id=1, source_target_pairs={{0,7},{1,6},{2,5},{3,4},{4,3},{5,2},{6,1},{7,0},{8,15},{9,14},{10,... | collective-permute-start | bytes 294920 | tf_op jit(solution)/shard_map/ppermute | solution.py:426
  53.9 0.9 copy-start.8
  55.8 4.2 %collective-permute-start.14 = (bf16[128,512]{1,0:T(8,128)(2,1)S(1)}, bf16[128,512]{1,0:T(8,128)(2,1)S(1)}, u32[]{:S(2)}, u32[]{:S(2)}) collective-permute-start(bf16[128,512]{1,0:T(8,128)(2,1)S(1)} %get-tuple-element.117), channel_id=1, source_target_pairs={{0,1},{1,0},{2,3},{3,2},{4,5},{5,4},{6,7},{7,6},{8,9},{9,8},{10,11... | collective-permute-start | bytes 393224 | tf_op jit(solution)/shard_map/ppermute | solution.py:426
  56.2 5.1 %collective-permute-start.15 = (bf16[128,512]{1,0:T(8,128)(2,1)S(1)}, bf16[128,512]{1,0:T(8,128)(2,1)S(1)}, u32[]{:S(2)}, u32[]{:S(2)}) collective-permute-start(bf16[128,512]{1,0:T(8,128)(2,1)S(1)} %get-tuple-element.118), channel_id=1, source_target_pairs={{0,2},{1,3},{2,0},{3,1},{4,6},{5,7},{6,4},{7,5},{8,10},{9,11},{10,... | collective-permute-start | bytes 393224 | tf_op jit(solution)/shard_map/ppermute | solution.py:426
  57.5 7.5 %collective-permute-start.16 = (bf16[128,512]{1,0:T(8,128)(2,1)S(1)}, bf16[128,512]{1,0:T(8,128)(2,1)S(1)}, u32[]{:S(2)}, u32[]{:S(2)}) collective-permute-start(bf16[128,512]{1,0:T(8,128)(2,1)S(1)} %get-tuple-element.119), channel_id=1, source_target_pairs={{0,3},{1,2},{2,1},{3,0},{4,7},{5,6},{6,5},{7,4},{8,11},{9,10},{10,... | collective-permute-start | bytes 393224 | tf_op jit(solution)/shard_map/ppermute | solution.py:426
  58.1 6.9 %collective-permute-start.17 = (bf16[128,512]{1,0:T(8,128)(2,1)S(1)}, bf16[128,512]{1,0:T(8,128)(2,1)S(1)}, u32[]{:S(2)}, u32[]{:S(2)}) collective-permute-start(bf16[128,512]{1,0:T(8,128)(2,1)S(1)} %get-tuple-element.120), channel_id=1, source_target_pairs={{0,4},{1,5},{2,6},{3,7},{4,0},{5,1},{6,2},{7,3},{8,12},{9,13},{10,... | collective-permute-start | bytes 393224 | tf_op jit(solution)/shard_map/ppermute | solution.py:426
  58.3 13.5 %collective-permute-start.18 = (bf16[128,512]{1,0:T(8,128)(2,1)S(1)}, bf16[128,512]{1,0:T(8,128)(2,1)S(1)}, u32[]{:S(2)}, u32[]{:S(2)}) collective-permute-start(bf16[128,512]{1,0:T(8,128)(2,1)S(1)} %get-tuple-element.121), channel_id=1, source_target_pairs={{0,5},{1,4},{2,7},{3,6},{4,1},{5,0},{6,3},{7,2},{8,13},{9,12},{10,... | collective-permute-start | bytes 393224 | tf_op jit(solution)/shard_map/ppermute | solution.py:426
  59.9 11.9 %collective-permute-start.19 = (bf16[128,512]{1,0:T(8,128)(2,1)S(1)}, bf16[128,512]{1,0:T(8,128)(2,1)S(1)}, u32[]{:S(2)}, u32[]{:S(2)}) collective-permute-start(bf16[128,512]{1,0:T(8,128)(2,1)S(1)} %get-tuple-element.122), channel_id=1, source_target_pairs={{0,6},{1,7},{2,4},{3,5},{4,2},{5,3},{6,0},{7,1},{8,14},{9,15},{10,... | collective-permute-start | bytes 393224 | tf_op jit(solution)/shard_map/ppermute | solution.py:426
  61.3 10.5 %collective-permute-start.20 = (bf16[128,512]{1,0:T(8,128)(2,1)S(1)}, bf16[128,512]{1,0:T(8,128)(2,1)S(1)}, u32[]{:S(2)}, u32[]{:S(2)}) collective-permute-start(bf16[128,512]{1,0:T(8,128)(2,1)S(1)} %get-tuple-element.123), channel_id=1, source_target_pairs={{0,7},{1,6},{2,5},{3,4},{4,3},{5,2},{6,1},{7,0},{8,15},{9,14},{10,... | collective-permute-start | bytes 393224 | tf_op jit(solution)/shard_map/ppermute | solution.py:426
  71.8 16.8 %copy-start = (bf16[512,1536]{1,0:T(8,128)(2,1)S(1)}, bf16[512,1536]{1,0:T(8,128)(2,1)}, u32[]{:S(2)}) copy-start(bf16[512,1536]{1,0:T(8,128)(2,1)} %wqkv_ref.3) | copy-start | bytes 4718596
  71.8 16.8 %copy-start.1 = (bf16[8,128,768]{2,1,0:T(8,128)(2,1)S(1)}, bf16[8,128,768]{2,1,0:T(8,128)(2,1)}, u32[]{:S(2)}) copy-start(bf16[8,128,768]{2,1,0:T(8,128)(2,1)} %pixels_ref.3) | copy-start | bytes 4718596
  71.8 16.8 %copy-start.2 = (bf16[512,768]{1,0:T(8,128)(2,1)S(1)}, bf16[512,768]{1,0:T(8,128)(2,1)}, u32[]{:S(2)}) copy-start(bf16[512,768]{1,0:T(8,128)(2,1)} %whead_ref.3) | copy-start | bytes 2359300
  71.8 16.8 %copy-start.5 = (bf16[512,512]{1,0:T(8,128)(2,1)S(1)}, bf16[512,512]{1,0:T(8,128)(2,1)}, u32[]{:S(2)}) copy-start(bf16[512,512]{1,0:T(8,128)(2,1)} %wout_ref.3) | copy-start | bytes 1572868
  73.7 5.2 %collective-permute-start.21 = (bf16[8,16,512]{2,1,0:T(8,128)(2,1)S(1)}, bf16[8,16,512]{2,1,0:T(8,128)(2,1)S(1)}, u32[]{:S(2)}, u32[]{:S(2)}) collective-permute-start(bf16[8,16,512]{2,1,0:T(8,128)(2,1)S(1)} %get-tuple-element.125), channel_id=1, source_target_pairs={{0,1},{1,2},{2,3},{3,4},{4,5},{5,6},{6,7},{8,9},{9,10},{10,11},{11... | collective-permute-start | bytes 393224 | tf_op jit(solution)/shard_map/ppermute | solution.py:499
  77.0 6.3 %collective-permute-start.22 = (bf16[8,16,512]{2,1,0:T(8,128)(2,1)S(1)}, bf16[8,16,512]{2,1,0:T(8,128)(2,1)S(1)}, u32[]{:S(2)}, u32[]{:S(2)}) collective-permute-start(bf16[8,16,512]{2,1,0:T(8,128)(2,1)S(1)} %get-tuple-element.126), channel_id=1, source_target_pairs={{1,0},{2,1},{3,2},{4,3},{5,4},{6,5},{7,6},{9,8},{10,9},{11,10},{12... | collective-permute-start | bytes 393224 | tf_op jit(solution)/shard_map/ppermute | solution.py:500
  83.3 14.4 %collective-permute-start.24 = (bf16[3,144,512]{2,1,0:T(8,128)(2,1)S(1)}, bf16[3,144,512]{2,1,0:T(8,128)(2,1)S(1)}, u32[]{:S(2)}, u32[]{:S(2)}) collective-permute-start(bf16[3,144,512]{2,1,0:T(8,128)(2,1)S(1)} %get-tuple-element.137), channel_id=1, source_target_pairs={{8,0},{16,8},{24,16},{9,1},{17,9},{25,17},{10,2},{18,10},{26,18},{... | collective-permute-start | bytes 1327112 | tf_op jit(solution)/shard_map/ppermute | solution.py:505
  85.4 13.8 %collective-permute-start.23 = (bf16[3,144,512]{2,1,0:T(8,128)(2,1)S(1)}, bf16[3,144,512]{2,1,0:T(8,128)(2,1)S(1)}, u32[]{:S(2)}, u32[]{:S(2)}) collective-permute-start(bf16[3,144,512]{2,1,0:T(8,128)(2,1)S(1)} %get-tuple-element.138), channel_id=1, source_target_pairs={{0,8},{8,16},{16,24},{1,9},{9,17},{17,25},{2,10},{10,18},{18,26},{... | collective-permute-start | bytes 1327112 | tf_op jit(solution)/shard_map/ppermute | solution.py:504
